TPU v7x, 512 devices: a whole 4x8x8 slice. The times are simulated.
512 devices in a mesh: ctx: 64 (over y, x, core), grp: 8 (over z).
Axes of the slice: x: 4, y: 8, z: 8, core: 2. Of those that a mesh axis runs over, the one named last changes fastest.
Arguments:
- x_in: bfloat16 [8192, 16384], P('ctx', 'grp'), may hold values from -0.29882812 to 0.29882812
- b_in: bfloat16 [8192, 128], P('ctx'), may hold values from -6 to 6
- c_in: bfloat16 [8192, 128], P('ctx'), may hold values from -0.52734375 to 0.52734375
- decay_log: float32 [128, 8192], P('grp', 'ctx'), may hold values from -1 to 0
- q_in: bfloat16 [8192, 4096], P('ctx', 'grp'), may hold values from -64 to 64
- k_in: bfloat16 [8192, 1024], P('ctx', 'grp'), may hold values from -4 to 4
- v_in: bfloat16 [8192, 1024], P('ctx', 'grp'), may hold values from -6 to 6
- expert_ids: int32 [8192, 2], P(('ctx', 'grp')), may hold values from 0 to 15, all different within a row; in each aligned block of 16 rows (0 to 15, 16 to 31, ...) at most 4 rows name the same one
- gates: float32 [8192, 2], P(('ctx', 'grp')), may hold values from 0.2 to 1
- expert_out: bfloat16 [64, 16, 8, 4, 8192], P('ctx', 'grp'), may hold values from -6 to 6
Outputs:
- mamba_out: bfloat16 [8192, 16384], P('ctx', 'grp')
- attn_out: bfloat16 [8192, 4096], P('ctx', 'grp')
- moe_out: bfloat16 [8192, 8192], P(('ctx', 'grp'))
Inputs may be any that keep to these rules, and one draw needn't show every extreme that they name: `expert_ids`: within the 16 rows of one device no expert is named more than 4 times; each row names 2 different experts.
All inputs are finite; a program needn't handle non-finite values.
Results may differ from a plain program's by a relative error of at most 0.0047.
Values may be sent and summed in bfloat16 or wider, within the bound.
No kernel may reach another device: no remote copies, remote signals or barrier semaphores. Data moves between devices by JAX's collectives and lax.ppermute only.
A program may use at most 192 MiB of HBM per device.

v0:
```python
import math

import jax
import jax.numpy as jnp
from jax import lax
from jax.sharding import PartitionSpec as P

HD = 128


very_negative = -1e30


def carried_in(value, axis, join, neutral):
    count, mine = (lax.axis_size(axis), lax.axis_index(axis))
    pieces = jax.tree.map(lambda part: lax.all_gather(part, axis), value)
    subtotal = jax.tree.map(
        lambda part, zero: jnp.full_like(part, 0) + jnp.asarray(zero, part.dtype), value, neutral
    )

    def lap(position, subtotal):
        longer = join(subtotal, jax.tree.map(lambda part: part[position], pieces))
        return jax.tree.map(lambda new, old: jnp.where(position < mine, new, old), longer, subtotal)

    return lax.fori_loop(0, count - 1, lap, subtotal)


def chain_join(earlier, later):
    return (earlier[0] * later[0], later[0][:, None, None] * earlier[1] + later[1])


def mamba_part(x_in, b_in, c_in, decay_log):
    length = x_in.shape[0]
    head_count = decay_log.shape[0]
    head_width = x_in.shape[1] // head_count
    x_heads = x_in.reshape(length, head_count, head_width)
    cumulative = jnp.cumsum(decay_log, axis=1)
    cross_block = jnp.dot(c_in, b_in.T, preferred_element_type=jnp.float32)
    token_offsets = jnp.arange(length, dtype=jnp.int32)
    causal_mask = token_offsets[:, None] >= token_offsets[None, :]
    log_gap = jnp.where(
        causal_mask[None], cumulative[:, :, None] - cumulative[:, None, :], -jnp.inf
    )
    blended_weights = (jnp.exp(log_gap) * cross_block[None]).astype(jnp.bfloat16)
    local_part = jnp.einsum(
        "hts,shp->thp", blended_weights, x_heads, preferred_element_type=jnp.float32
    )
    tail_decay = jnp.exp(cumulative[:, -1:] - cumulative)
    weighted_b = (tail_decay[:, :, None] * b_in.astype(jnp.float32)[None]).astype(jnp.bfloat16)
    block_state = jnp.einsum(
        "shp,hsn->hpn", x_heads, weighted_b, preferred_element_type=jnp.float32
    )
    block_decay = jnp.exp(cumulative[:, -1])
    identity = (jnp.ones_like(block_decay), jnp.zeros_like(block_state))
    carried = carried_in((block_decay, block_state), "ctx", chain_join, identity)
    entering = carried[1]
    readout = jnp.einsum(
        "tn,hpn->thp", c_in.astype(jnp.float32), entering, precision=lax.Precision.HIGHEST
    )
    carried_part = jnp.exp(cumulative).T[:, :, None] * readout
    return (local_part + carried_part).reshape(length, head_count * head_width).astype(jnp.bfloat16)


def attention_part(q_in, k_in, v_in):
    length = q_in.shape[0]
    kv_count = k_in.shape[1] // HD
    q_count = q_in.shape[1] // HD
    group_size = q_count // kv_count
    scale = 1.0 / math.sqrt(HD)
    shard = lax.axis_index("ctx")
    query_sets = [q_in]
    position_sets = [shard * length + jnp.arange(length, dtype=jnp.int32)]
    query_heads = [rows.reshape(rows.shape[0], kv_count, group_size, HD) for rows in query_sets]
    start_state = tuple(
        (
            (
                jnp.full((kv_count, group_size, rows.shape[0]), very_negative, jnp.float32),
                jnp.zeros((kv_count, group_size, rows.shape[0]), jnp.float32),
                jnp.zeros((kv_count, group_size, rows.shape[0], HD), jnp.float32),
            )
            for rows in query_sets
        )
    )
    carry = start_state
    keys = lax.all_gather(k_in, "ctx", axis=0, tiled=True)
    values = lax.all_gather(v_in, "ctx", axis=0, tiled=True)
    count = keys.shape[0]
    step_rows = math.gcd(count, 512)
    key_blocks = keys.reshape(count // step_rows, step_rows, kv_count, HD)
    value_blocks = values.reshape(count // step_rows, step_rows, kv_count, HD)

    def one_block(state_tensors, item):
        index, key_blk, value_blk = item
        key_pos = index * step_rows + jnp.arange(step_rows, dtype=jnp.int32)
        updated = []
        for queries, query_pos, running_state in zip(query_heads, position_sets, state_tensors):

            def compute(running, queries=queries, query_pos=query_pos):
                run_max, run_total, run_acc = running
                scores = (
                    jnp.einsum(
                        "lkgd,skd->kgls", queries, key_blk, preferred_element_type=jnp.float32
                    )
                    * scale
                )
                allowed = key_pos[None, :] <= query_pos[:, None]
                scores = jnp.where(allowed, scores, -jnp.inf)
                new_max = jnp.maximum(run_max, jnp.max(scores, axis=3))
                factor = jnp.exp(run_max - new_max)
                probs = jnp.exp(scores - new_max[..., None])
                new_total = run_total * factor + jnp.sum(probs, axis=3)
                added = jnp.einsum(
                    "kgls,skd->kgld",
                    probs.astype(jnp.bfloat16),
                    value_blk,
                    preferred_element_type=jnp.float32,
                )
                return (new_max, new_total, run_acc * factor[..., None] + added)

            running_state = compute(running_state)
            updated.append(running_state)
        return (tuple(updated), None)

    indices = jnp.arange(count // step_rows, dtype=jnp.int32)
    carry, unused = lax.scan(one_block, carry, (indices, key_blocks, value_blocks))
    outputs = []
    for final_max, final_total, final_acc in carry:
        result = final_acc / final_total[..., None]
        outputs.append(
            result.transpose(2, 0, 1, 3).reshape(result.shape[2], q_count * HD).astype(jnp.bfloat16)
        )
    return outputs[0]


def expert_part(expert_ids, gates, expert_out):
    held_rows = expert_out[0]
    returned = lax.all_to_all(held_rows, "grp", split_axis=1, concat_axis=0, tiled=True)
    expert_count, single, capacity, model_width = returned.shape
    row_table = returned.reshape(expert_count * capacity, model_width)
    tok_rows, top_count = expert_ids.shape
    flattened_identifiers = expert_ids.reshape(tok_rows * top_count)
    onehot = (
        flattened_identifiers[:, None] == jnp.arange(expert_count, dtype=jnp.int32)[None, :]
    ).astype(jnp.int32)
    before = jnp.cumsum(onehot, axis=0, dtype=jnp.int32) - onehot
    slot_index = jnp.sum(before * onehot, axis=1, dtype=jnp.int32)
    row_number = (flattened_identifiers * capacity + slot_index).reshape(tok_rows, top_count)
    combined = jnp.zeros((tok_rows, model_width), jnp.float32)
    for which_one in range(top_count):
        combined = combined + gates[:, which_one : which_one + 1] * row_table[
            row_number[:, which_one]
        ].astype(jnp.float32)
    return combined.astype(jnp.bfloat16)


def shards(x_in, b_in, c_in, decay_log, q_in, k_in, v_in, expert_ids, gates, expert_out):
    mamba_out = mamba_part(x_in, b_in, c_in, decay_log)
    attn_out = attention_part(q_in, k_in, v_in)
    moe_out = expert_part(expert_ids, gates, expert_out)
    return (mamba_out, attn_out, moe_out)


def solution(mesh):
    return jax.shard_map(
        shards,
        mesh=mesh,
        in_specs=(
            P("ctx", "grp"),
            P("ctx", None),
            P("ctx", None),
            P("grp", "ctx"),
            P("ctx", "grp"),
            P("ctx", "grp"),
            P("ctx", "grp"),
            P(("ctx", "grp"), None),
            P(("ctx", "grp"), None),
            P("ctx", "grp", None, None, None),
        ),
        out_specs=(P("ctx", "grp"), P("ctx", "grp"), P(("ctx", "grp"), None)),
        check_vma=False,
    )
```

profile of v0, /device:TPU:1, one launch (start us, length us, event | category | flops | bytes accessed | tf_op | source)
XLA Modules:
  0.0 571.3 jit_solution(3690729015166879934)
XLA Ops:
  14.0 10.9 %all-to-all-start = ((bf16[2,8,4,8192]{3,2,0,1:T(4,128)(2,1)}), bf16[2,8,4,8192]{3,2,0,1:T(4,128)(2,1)S(1)}, u32[]{:S(2)}, u32[]{:S(2)}) async-start(bf16[2,8,4,8192]{3,2,0,1:T(4,128)(2,1)} %bitcast.106), calls=%async_computation | async-start | bytes 2097152 | tf_op jit(solution)/shard_map/all_to_all | solution.py:137
  27.1 125.6 %all-reduce = f32[1024]{0:T(1024)S(1)} all-reduce(f32[1024]{0:T(1024)S(1)} %dynamic-update-slice), channel_id=2, replica_groups=mesh['ctx'=64,'grp'=8] {'ctx'}, use_global_device_ids=true, to_apply=%add | all-reduce | flops 1024 | bytes 8192
  155.7 1.7 convolution_bitcast_fusion.3
  161.3 1.5 add_convert_fusion
  162.8 20.8 %all-gather.6.cloned.1.call-done = bf16[8192,128]{1,0:T(8,128)(2,1)} async-done(((bf16[128,128]{1,0:T(8,128)(2,1)}), bf16[8192,128]{1,0:T(8,128)(2,1)}) %all-gather.6.cloned.1.call-update) | async-done | bytes 2097168 | tf_op jit(solution)/shard_map/all_gather | solution.py:85
  183.6 66.2 %while.30 = (s32[]{:T(128)}, f32[1,4,128]{2,1,0:T(4,128)S(1)}, f32[1,4,128]{2,1,0:T(4,128)S(1)}, f32[1,4,128,128]{3,2,1,0:T(8,128)S(1)}, s32[16]{0:T(128)S(1)}, ...) while((s32[]{:T(128)}, f32[1,4,128]{2,1,0:T(4,128)S(1)}, ...), condition=%wide.region_6.7_spmd.clone, body=%wide.region_3.6_spmd.clone.sunk | while | flops 136318592 | bytes 4233377 | solution.py:125
  250.7 175.7 %all-gather.10.cloned.1.call-done = f32[1024,128,128]{2,1,0:T(8,128)} async-done(((f32[16,128,128]{2,1,0:T(8,128)}), f32[1024,128,128]{2,1,0:T(8,128)}) %all-gather.10.cloned.1.call-update) | async-done | bytes 67108880 | tf_op jit(solution)/shard_map/all_gather | solution.py:16
  426.5 136.6 %while.29 = (s32[]{:T(128)}, f32[16,128,128]{2,1,0:T(8,128)S(1)}, s32[]{:T(128)}, f32[64,16]{1,0:T(8,128)}, f32[64,16,128,128]{3,2,1,0:T(8,128)}, /*index=5*/s32[]{:T(128)}, s32[]{:T(128)}) while((s32[]{:T(128)}, f32[16,128,128]{2,1,0:T(8,128)S(1)}, s32[]{:T(128)}, f32[64,16]{1,0:T(8,128)}, f32[64,16,128,128]{3,2,1,0:T(8,128)}, ...), condition=%wide.region_2.3_spmd.clone, body=%wide.region_1.2_spmd.clone.sunk | while | flops 1048580 | bytes 3146025 | solution.py:25
  427.2 1.5 fusion.53
  429.4 1.5 fusion.53
  431.6 1.5 fusion.53
  433.7 1.5 fusion.53
  435.9 1.5 fusion.53
  438.1 1.5 fusion.53
  440.2 1.5 fusion.53
  442.4 1.5 fusion.53
  444.6 1.5 fusion.53
  446.8 1.5 fusion.53
  448.9 1.5 fusion.53
  451.1 1.5 fusion.53
  453.3 1.5 fusion.53
  455.4 1.5 fusion.53
  457.6 1.5 fusion.53
  459.8 1.5 fusion.53
  461.9 1.5 fusion.53
  464.1 1.5 fusion.53
  466.3 1.5 fusion.53
  468.4 1.5 fusion.53
  470.6 1.5 fusion.53
  472.8 1.5 fusion.53
  474.9 1.5 fusion.53
  477.1 1.5 fusion.53
  479.3 1.5 fusion.53
  481.4 1.5 fusion.53
  483.6 1.5 fusion.53
  485.8 1.5 fusion.53
  487.9 1.5 fusion.53
  490.1 1.5 fusion.53
  492.3 1.5 fusion.53
  494.4 1.5 fusion.53
  496.6 1.5 fusion.53
  498.8 1.5 fusion.53
  507.5 1.5 fusion.53
  516.1 1.5 fusion.53
  524.8 1.5 fusion.53
  540.0 1.5 fusion.53
  548.6 1.5 fusion.53
  557.3 1.5 fusion.53
  (313 shorter events, 149.6 us)
Async XLA Ops:
  7.2 3.6 copy-start
  7.2 155.7 %all-gather.8.cloned.1.call-start = ((), (), s32[]{:S(2)}) async-start(), calls=%async_computation.2 | async-start | bytes 2129920 | tf_op jit(solution)/shard_map/all_gather | solution.py:86
  7.9 175.7 %all-gather.6.cloned.1.call-start = ((), (), s32[]{:S(2)}) async-start(), calls=%async_computation.1 | async-start | bytes 2129920 | tf_op jit(solution)/shard_map/all_gather | solution.py:85
  8.7 417.8 %all-gather.10.cloned.1.call-start = ((), (), s32[]{:S(2)}) async-start(), calls=%async_computation.3 | async-start | bytes 68157440 | tf_op jit(solution)/shard_map/all_gather | solution.py:16
  10.8 1.7 copy-start.2
  12.5 140.9 %copy-start.8 = (s32[16,2]{0,1:T(2,128)S(1)}, s32[16,2]{0,1:T(2,128)}, u32[]{:S(2)}) copy-start(s32[16,2]{0,1:T(2,128)} %param.21) | copy-start | bytes 388
  12.6 141.5 %copy-start.4 = (bf16[128,512]{1,0:T(8,128)(2,1)S(1)}, bf16[128,512]{1,0:T(8,128)(2,1)}, u32[]{:S(2)}) copy-start(bf16[128,512]{1,0:T(8,128)(2,1)} %param.18) | copy-start | bytes 393220
  12.6 142.4 %copy-start.9 = (f32[16,2]{0,1:T(2,128)S(1)}, f32[16,2]{0,1:T(2,128)}, u32[]{:S(2)}) copy-start(f32[16,2]{0,1:T(2,128)} %param.22) | copy-start | bytes 388
  12.6 143.0 %copy-start.5 = (bf16[128,128]{1,0:T(8,128)(2,1)S(1)}, bf16[128,128]{1,0:T(8,128)(2,1)}, u32[]{:S(2)}) copy-start(bf16[128,128]{1,0:T(8,128)(2,1)} %param.15) | copy-start | bytes 98308
  12.6 143.0 %copy-start.6 = (bf16[128,128]{1,0:T(8,128)(2,1)S(1)}, bf16[128,128]{1,0:T(8,128)(2,1)}, u32[]{:S(2)}) copy-start(bf16[128,128]{1,0:T(8,128)(2,1)} %param.16) | copy-start | bytes 98308
  14.0 143.4 %all-to-all-start = ((bf16[2,8,4,8192]{3,2,0,1:T(4,128)(2,1)}), bf16[2,8,4,8192]{3,2,0,1:T(4,128)(2,1)S(1)}, u32[]{:S(2)}, u32[]{:S(2)}) async-start(bf16[2,8,4,8192]{3,2,0,1:T(4,128)(2,1)} %bitcast.106), calls=%async_computation | async-start | bytes 2097152 | tf_op jit(solution)/shard_map/all_to_all | solution.py:137
  157.4 1.0 copy-start.1
  426.5 136.7 %copy-start.3 = (f32[128,16,128]{0,2,1:T(8,128)S(1)}, f32[128,16,128]{0,2,1:T(8,128)}, u32[]{:S(2)}) copy-start(f32[128,16,128]{0,2,1:T(8,128)} %convolution_bitcast_fusion.3) | copy-start | bytes 3145732
  426.5 136.7 %copy-start.7 = (bf16[128,128]{1,0:T(8,128)(2,1)S(1)}, bf16[128,128]{1,0:T(8,128)(2,1)}, u32[]{:S(2)}) copy-start(bf16[128,128]{1,0:T(8,128)(2,1)} %param.16) | copy-start | bytes 98308
Sparse Core Ops, SparseCore 0:
  11.4 88.3 all-gather.7
  103.1 80.5 all-gather.5
  187.0 239.4 all-gather.9
where the time goes:
time: 577 us; the launch traced here: 571 us
  waiting for transfers between devices  198 us (34%)
  blocking collectives  126 us (22%)
  other arithmetic  101 us (18%)
  local copies, waits for them, and re-layouts  66.3 us (11%)
  matrix products  42.6 us (7%)
  between operations  14.6 us (3%)
  loops' own time  12.7 us (2%)
  starting transfers between devices  11 us (2%)
    all_gather x1, waiting for transfers between devices, carried_in(): pieces = jax.tree.map(lambda part: lax.all_gather(part, axis), value)  176 us
    unnamed x1, blocking collectives  126 us
    select_n x63, other arithmetic, lap(): jnp.where(position < mine, new, old)  91.6 us
    mul x63, local copies, waits for them, and re-layouts, chain_join(): later[0][:, None, None] * earlier[1] + later[1]  43.9 us
    all_gather x1, waiting for transfers between devices, attention_part(): keys = lax.all_gather(k_in, 'ctx', axis=0, tiled=True)  20.8 us
    dot_general x16, matrix products, compute(): jnp.einsum('kgls,skd->kgld', probs.astype(jnp.bfloat16), value_blk, prefe...  20.3 us
    dot_general x16, matrix products, compute(): jnp.einsum('lkgd,skd->kgls', queries, key_blk, preferred_element_type=jnp...  19.5 us
  transfers between devices with their start and end apart: 4, of which 2 were waited for; matrix products, arithmetic and copies ran while one was open for 12% of the time, Pallas kernels for 0%

commit v1 on v0

v1 whole, which is shorter than its diff:
```python
import math

import jax
import jax.numpy as jnp
from jax import lax
from jax.experimental import pallas as pl
from jax.experimental.pallas import tpu as pltpu
from jax.sharding import PartitionSpec as P

HD = 128
L = 128
MH = 16
NCTX = 64
QH = 4
CAP = 4
LOG2E = 1.4426950408889634
F32 = jnp.float32
BF16 = jnp.bfloat16
VM = pl.BlockSpec(memory_space=pltpu.VMEM)
SM = pl.BlockSpec(memory_space=pltpu.SMEM)


def params(mib=40):
    return pltpu.CompilerParams(vmem_limit_bytes=mib * 2**20)


def cost(flops, nbytes):
    return pl.CostEstimate(flops=flops, bytes_accessed=nbytes, transcendentals=0)


def tri(lower):
    r = lax.broadcasted_iota(jnp.int32, (L, L), 0)
    c = lax.broadcasted_iota(jnp.int32, (L, L), 1)
    return (c <= r) if lower else (r <= c)


def row_cumulative(decay):
    return jnp.dot(
        decay, tri(False).astype(F32), precision=lax.Precision.HIGHEST, preferred_element_type=F32
    )


def col_cumulative(decay):
    return lax.dot_general(
        tri(True).astype(F32),
        decay,
        (((1,), (1,)), ((), ())),
        precision=lax.Precision.HIGHEST,
        preferred_element_type=F32,
    )


def pack_kernel(k_ref, v_ref, o_ref):
    o_ref[0:HD, :] = k_ref[...].astype(F32).T.astype(BF16)
    o_ref[HD:, :] = v_ref[...]


def pack_kv(k_in, v_in):
    return pl.pallas_call(
        pack_kernel,
        out_shape=jax.ShapeDtypeStruct((2 * HD, L), BF16),
        in_specs=[VM, VM],
        out_specs=VM,
        compiler_params=params(),
        cost_estimate=cost(1 << 20, 1 << 17),
    )(k_in, v_in)


def state_kernel(x_ref, b_ref, d_ref, o_ref):
    cum = row_cumulative(d_ref[...])
    tail = jnp.exp(cum[:, L - 1 :] - cum)
    block_decay = jnp.exp(cum[:, L - 1 :])
    bt = b_ref[...].astype(F32).T
    row = lax.broadcasted_iota(jnp.int32, (8, L), 0)
    for h in range(MH):
        wb = (tail[h : h + 1, :] * bt).astype(BF16)
        s = jnp.dot(wb, x_ref[:, h * HD : (h + 1) * HD], preferred_element_type=F32)
        d = jnp.broadcast_to(block_decay[h : h + 1, :], (8, L))
        hi = d.astype(BF16).astype(F32)
        mid = (d - hi).astype(BF16).astype(F32)
        lo = d - hi - mid
        terms = jnp.where(row == 0, hi, jnp.where(row == 1, mid, jnp.where(row == 2, lo, 0.0)))
        for q in range(4):
            o_ref[h * 4 + q] = jnp.concatenate([s[q * 32 : (q + 1) * 32], terms], axis=0).astype(BF16)


def block_states(x_in, b_in, decay_log):
    return pl.pallas_call(
        state_kernel,
        out_shape=jax.ShapeDtypeStruct((NCTX, 40, HD), BF16),
        in_specs=[VM] * 3,
        out_specs=VM,
        compiler_params=params(),
        cost_estimate=cost(1 << 26, 1 << 20),
    )(x_in, b_in, decay_log)


def scan_kernel(s_ref, o_ref):
    def step(k, e):
        o_ref[k] = e.astype(BF16)
        block = s_ref[k].astype(F32)
        d = block[32:33] + block[33:34] + block[34:35]
        return d * e + block[:32]

    lax.fori_loop(0, NCTX, step, jnp.zeros((32, HD), F32), unroll=8)


def scan_states(pieces):
    return pl.pallas_call(
        scan_kernel,
        out_shape=jax.ShapeDtypeStruct((NCTX, 32, HD), BF16),
        in_specs=[VM],
        out_specs=VM,
        compiler_params=params(),
        cost_estimate=cost(1 << 20, 1 << 20),
    )(pieces)


def local_kernel(x_ref, b_ref, c_ref, d_ref, o_ref):
    cum = row_cumulative(d_ref[...])
    cum_col = col_cumulative(d_ref[...])
    cross = lax.dot_general(
        c_ref[...], b_ref[...], (((1,), (1,)), ((), ())), preferred_element_type=F32
    )
    mask = tri(True)
    for h in range(MH):
        gap = jnp.where(mask, cum_col[:, h : h + 1] - cum[h : h + 1, :], -1e30)
        w = (jnp.exp(gap) * cross).astype(BF16)
        o_ref[:, h * HD : (h + 1) * HD] = jnp.dot(
            w, x_ref[:, h * HD : (h + 1) * HD], preferred_element_type=F32
        )


def local_part(x_in, b_in, c_in, decay_log):
    return pl.pallas_call(
        local_kernel,
        out_shape=jax.ShapeDtypeStruct((L, MH * HD), F32),
        in_specs=[VM] * 4,
        out_specs=VM,
        compiler_params=params(),
        cost_estimate=cost(1 << 28, 1 << 21),
    )(x_in, b_in, c_in, decay_log)


def join_kernel(l_ref, e_ref, c_ref, d_ref, o_ref):
    grow = jnp.exp(col_cumulative(d_ref[...]))
    c = c_ref[...]
    for h in range(MH):
        cols = slice(h * HD, (h + 1) * HD)
        readout = jnp.dot(c, e_ref[cols, :], preferred_element_type=F32)
        o_ref[:, cols] = (l_ref[:, cols] + grow[:, h : h + 1] * readout).astype(BF16)


def join_mamba(local, entering, c_in, decay_log):
    return pl.pallas_call(
        join_kernel,
        out_shape=jax.ShapeDtypeStruct((L, MH * HD), BF16),
        in_specs=[VM] * 4,
        out_specs=VM,
        compiler_params=params(),
        cost_estimate=cost(1 << 26, 1 << 21),
    )(local, entering, c_in, decay_log)


def mamba_part(x_in, b_in, c_in, decay_log):
    pieces = block_states(x_in, b_in, decay_log)
    pieces = lax.all_to_all(pieces, "ctx", split_axis=0, concat_axis=0, tiled=True)
    entering = scan_states(pieces)
    entering = lax.all_to_all(entering, "ctx", split_axis=0, concat_axis=0, tiled=True)
    local = local_part(x_in, b_in, c_in, decay_log)
    return join_mamba(local, entering.reshape(MH * L, HD), c_in, decay_log)


PER = 8


def attention_kernel(me_ref, q_ref, kv_ref, o_ref, m_ref, l_ref, acc_ref):
    step = pl.program_id(0)
    me = me_ref[0]
    c = LOG2E / math.sqrt(HD)
    rows = QH * L

    @pl.when(step == 0)
    def _():
        m_ref[...] = jnp.full((rows, 1), -1e30, F32)
        l_ref[...] = jnp.zeros((rows, L), F32)
        acc_ref[...] = jnp.zeros((rows, HD), F32)

    def work(masked):
        q = jnp.concatenate([q_ref[:, g * HD : (g + 1) * HD] for g in range(QH)], axis=0)
        kt = jnp.concatenate([kv_ref[j, :HD, :] for j in range(PER)], axis=1)
        s = jnp.dot(q, kt, preferred_element_type=F32)
        if masked:
            t = lax.broadcasted_iota(jnp.int32, s.shape, 0) % L
            k = lax.broadcasted_iota(jnp.int32, s.shape, 1)
            s = jnp.where(k <= t + (me - step * PER) * L, s, -1e30)
        m_old = m_ref[...]
        m_new = jnp.maximum(m_old, jnp.max(s, axis=1, keepdims=True))
        factor = jnp.exp2((m_old - m_new) * c)
        p = jnp.exp2((s - m_new) * c)
        total = p[:, :L]
        for j in range(1, PER):
            total = total + p[:, j * L : (j + 1) * L]
        v = jnp.concatenate([kv_ref[j, HD:, :] for j in range(PER)], axis=0)
        added = jnp.dot(p.astype(BF16), v, preferred_element_type=F32)
        m_ref[...] = m_new
        l_ref[...] = l_ref[...] * factor + total
        acc_ref[...] = acc_ref[...] * factor + added

    @pl.when((step + 1) * PER <= me)
    def _():
        work(False)

    @pl.when(jnp.logical_and((step + 1) * PER > me, step * PER <= me))
    def _():
        work(True)

    @pl.when(step == NCTX // PER - 1)
    def _():
        out = acc_ref[...] / jnp.sum(l_ref[...], axis=1, keepdims=True)
        for g in range(QH):
            o_ref[:, g * HD : (g + 1) * HD] = out[g * L : (g + 1) * L].astype(BF16)


def attention_part(q_in, k_in, v_in):
    packed = pack_kv(k_in, v_in)
    gathered = lax.all_gather(packed, "ctx", axis=0, tiled=False)
    me = lax.axis_index("ctx").astype(jnp.int32).reshape(1)
    rows = QH * L
    return pl.pallas_call(
        attention_kernel,
        grid=(NCTX // PER,),
        out_shape=jax.ShapeDtypeStruct((L, QH * HD), BF16),
        in_specs=[
            SM,
            pl.BlockSpec((L, QH * HD), lambda i: (0, 0)),
            pl.BlockSpec((PER, 2 * HD, L), lambda i: (i, 0, 0)),
        ],
        out_specs=pl.BlockSpec((L, QH * HD), lambda i: (0, 0)),
        scratch_shapes=[
            pltpu.VMEM((rows, 1), F32),
            pltpu.VMEM((rows, L), F32),
            pltpu.VMEM((rows, HD), F32),
        ],
        compiler_params=params(),
        cost_estimate=cost(1 << 31, 1 << 22),
    )(me, q_in, gathered)


def combine_kernel(ids_ref, idst_ref, gates_ref, rows_ref, o_ref):
    count = ids_ref.shape[0]
    ids, idst, gates = ids_ref[...], idst_ref[...], gates_ref[...]
    t = lax.broadcasted_iota(jnp.int32, (count, count), 0)
    u = lax.broadcasted_iota(jnp.int32, (count, count), 1)
    place = lax.broadcasted_iota(jnp.int32, (count, rows_ref.shape[0]), 1)
    out = None
    for k in range(2):
        mine = ids[:, k : k + 1]
        slot = jnp.zeros((count, 1), jnp.int32)
        for j in range(2):
            before = (u < t) if j >= k else (u <= t)
            same = jnp.logical_and(before, idst[j : j + 1, :] == mine)
            slot = slot + jnp.sum(same.astype(jnp.int32), axis=1, keepdims=True)
        pick = (place == mine * CAP + slot).astype(F32).astype(BF16)
        row = jnp.dot(pick, rows_ref[...], preferred_element_type=F32)
        term = gates[:, k : k + 1] * row
        out = term if out is None else out + term
    o_ref[...] = out.astype(BF16)


def expert_part(expert_ids, gates, expert_out):
    owned, peers, cap, width = expert_out.shape[1:]
    held = expert_out[0].transpose(1, 0, 2, 3).reshape(peers, owned * cap, width)
    rows = lax.all_to_all(held, "grp", split_axis=0, concat_axis=0, tiled=True)
    rows = rows.reshape(peers * owned * cap, width)
    count = expert_ids.shape[0]
    block = 2048
    return pl.pallas_call(
        combine_kernel,
        grid=(width // block,),
        out_shape=jax.ShapeDtypeStruct((count, width), BF16),
        in_specs=[
            pl.BlockSpec((count, 2), lambda i: (0, 0)),
            pl.BlockSpec((2, count), lambda i: (0, 0)),
            pl.BlockSpec((count, 2), lambda i: (0, 0)),
            pl.BlockSpec((peers * owned * cap, block), lambda i: (0, i)),
        ],
        out_specs=pl.BlockSpec((count, block), lambda i: (0, i)),
        compiler_params=params(),
        cost_estimate=cost(1 << 24, 1 << 20),
    )(expert_ids, expert_ids.T, gates, rows)


def shards(x_in, b_in, c_in, decay_log, q_in, k_in, v_in, expert_ids, gates, expert_out):
    attn_out = attention_part(q_in, k_in, v_in)
    mamba_out = mamba_part(x_in, b_in, c_in, decay_log)
    moe_out = expert_part(expert_ids, gates, expert_out)
    return (mamba_out, attn_out, moe_out)


def solution(mesh):
    return jax.shard_map(
        shards,
        mesh=mesh,
        in_specs=(
            P("ctx", "grp"),
            P("ctx", None),
            P("ctx", None),
            P("grp", "ctx"),
            P("ctx", "grp"),
            P("ctx", "grp"),
            P("ctx", "grp"),
            P(("ctx", "grp"), None),
            P(("ctx", "grp"), None),
            P("ctx", "grp", None, None, None),
        ),
        out_specs=(P("ctx", "grp"), P("ctx", "grp"), P(("ctx", "grp"), None)),
        check_vma=False,
    )
```

time: 577 us -> 130 us (0.23)
  the two profiles are of different devices: /device:TPU:1 before, /device:TPU:57 now
where the time goes in v1:
time: 130 us; the launch traced here: 129 us
  waiting for transfers between devices  58.2 us (45%)
  starting transfers between devices  27.8 us (21%)
  Pallas kernels  19.5 us (15%)
  between operations  14.1 us (11%)
  local copies, waits for them, and re-layouts  9.81 us (8%)
    all_to_all x1, waiting for transfers between devices, expert_part(): rows = lax.all_to_all(held, 'grp', split_axis=0, concat_axis=0, tiled=True)  28.4 us
    all_to_all x1, waiting for transfers between devices, mamba_part(): lax.all_to_all(pieces, 'ctx', split_axis=0, concat_axis=0, tiled=True)  16.3 us
    all_to_all x1, waiting for transfers between devices, mamba_part(): lax.all_to_all(entering, 'ctx', split_axis=0, concat_axis=0, tiled=True)  13.5 us
    pallas_call x1, Pallas kernels, attention_part(): pl.pallas_call(attention_kernel, grid=(NCTX // PER,), out_shape=jax.Shape...  11.4 us
    all_to_all x1, starting transfers between devices, expert_part(): rows = lax.all_to_all(held, 'grp', split_axis=0, concat_axis=0, tiled=True)  11.4 us
    all_to_all x1, starting transfers between devices, mamba_part(): lax.all_to_all(pieces, 'ctx', split_axis=0, concat_axis=0, tiled=True)  10.5 us
    unnamed x29, local copies, waits for them, and re-layouts  8.25 us
    all_to_all x1, starting transfers between devices, mamba_part(): lax.all_to_all(entering, 'ctx', split_axis=0, concat_axis=0, tiled=True)  5.89 us
  transfers between devices with their start and end apart: 4, of which 3 were waited for; matrix products, arithmetic and copies ran while one was open for 3% of the time, Pallas kernels for 6%

profile of v1, /device:TPU:57, one launch (start us, length us, event | category | flops | bytes accessed | tf_op | source)
XLA Modules:
  0.0 129.5 jit_solution(2952229827572546570)
XLA Ops:
  7.2 0.0 all-gather.3.cloned.1.call-start
  7.2 0.0 copy-start.7
  7.2 0.7 copy-done.7
  8.0 0.0 copy-start.8
  8.0 0.8 copy-done.8
  8.7 0.7 shard_map.125
  9.5 0.0 all-gather.3.cloned.1.call-update
  9.5 0.0 copy-start
  9.5 1.0 copy-done
  10.5 0.0 copy-start.3
  10.5 0.8 copy-done.3
  11.3 0.0 copy-start.5
  11.3 0.7 copy-done.5
  12.0 1.5 %shard_map.122 = bf16[64,40,128]{2,1,0:T(8,128)(2,1)} custom-call(bf16[128,2048]{1,0:T(8,128)(2,1)S(1)} %copy-done, bf16[128,128]{1,0:T(8,128)(2,1)S(1)} %copy-done.3, f32[16,128]{1,0:T(8,128)S(1)} %copy-done.5), custom_call_target="tpu_custom_call" | custom-call | flops 67108864 | bytes 1048576 | tf_op jit(solution)/shard_map/pallas_call | solution.py:88
  13.5 10.5 %all-to-all-start = ((bf16[64,40,128]{2,1,0:T(8,128)(2,1)}), bf16[64,40,128]{2,1,0:T(8,128)(2,1)S(1)}, u32[]{:S(2)}, u32[]{:S(2)}) async-start(bf16[64,40,128]{2,1,0:T(8,128)(2,1)} %shard_map.122), calls=%async_computation | async-start | bytes 1310720 | tf_op jit(solution)/shard_map/all_to_all | solution.py:167
  24.0 0.0 copy-start.12
  24.0 0.0 copy-start.9
  24.0 0.0 copy-start.1
  24.0 0.0 copy-start.2
  24.0 0.0 copy-start.4
  24.0 0.0 copy-start.6
  24.0 1.9 %copy.19 = bf16[1,2,8,4,8192]{4,2,3,1,0:T(8,128)(2,1)S(1)} copy(bf16[1,2,8,4,8192]{4,3,2,1,0:T(4,128)(2,1)} %param.19) | data formatting | bytes 2097152 | tf_op args[9]
  25.9 1.6 %copy.20 = bf16[8,8,8192]{2,1,0:T(8,128)(2,1)} copy(bf16[8,8,8192]{2,0,1:T(8,128)(2,1)S(1)} %bitcast.14) | data formatting | bytes 2097152 | tf_op jit(solution)/shard_map/reshape | solution.py:273
  27.5 16.3 %all-to-all-done.s_ref = bf16[64,40,128]{2,1,0:T(8,128)(2,1)S(1)} async-done(((bf16[64,40,128]{2,1,0:T(8,128)(2,1)}), bf16[64,40,128]{2,1,0:T(8,128)(2,1)S(1)}, u32[]{:S(2)}, u32[]{:S(2)}) %all-to-all-start) | async-done | bytes 655392 | tf_op jit(solution)/shard_map/all_to_all | solution.py:167
  43.8 11.4 %all-to-all-start.2 = ((bf16[8,8,8192]{2,1,0:T(8,128)(2,1)}), bf16[8,8,8192]{2,1,0:T(8,128)(2,1)S(1)}, u32[]{:S(2)}, u32[]{:S(2)}) async-start(bf16[8,8,8192]{2,1,0:T(8,128)(2,1)} %copy.20), calls=%async_computation.2 | async-start | bytes 2097152 | tf_op jit(solution)/shard_map/all_to_all | solution.py:274
  55.2 0.0 copy-start.11
  55.2 1.0 shard_map.123
  56.2 28.4 %all-to-all-done.2 = bf16[8,8,8192]{2,1,0:T(8,128)(2,1)S(1)} async-done(((bf16[8,8,8192]{2,1,0:T(8,128)(2,1)}), bf16[8,8,8192]{2,1,0:T(8,128)(2,1)S(1)}, u32[]{:S(2)}, u32[]{:S(2)}) %all-to-all-start.2) | async-done | bytes 1048608 | tf_op jit(solution)/shard_map/all_to_all | solution.py:274
  84.5 5.9 %all-to-all-start.1 = ((bf16[64,32,128]{2,1,0:T(8,128)(2,1)}), bf16[64,32,128]{2,1,0:T(8,128)(2,1)S(1)}, u32[]{:S(2)}, u32[]{:S(2)}) async-start(bf16[64,32,128]{2,1,0:T(8,128)(2,1)} %shard_map.123), calls=%async_computation.1 | async-start | bytes 1048576 | tf_op jit(solution)/shard_map/all_to_all | solution.py:169
  90.4 0.0 copy-done.12
  90.5 0.1 copy.22.gates_ref
  90.5 0.0 copy-done.9
  90.5 0.1 copy.21.ids_ref
  90.6 0.0 copy-done.1
  90.6 0.0 copy-done.2
  90.6 0.0 copy-done.4
  90.6 0.0 copy-done.6
  90.6 0.8 shard_map.121.l_ref
  91.5 2.6 %shard_map.127 = bf16[16,8192]{1,0:T(8,128)(2,1)} custom-call(s32[16,2]{1,0:T(8,128)S(1)} %copy.21.ids_ref, s32[2,16]{1,0:T(2,128)S(1)} %bitcast.12, f32[16,2]{1,0:T(8,128)S(1)} %copy.22.gates_ref, bf16[64,8192]{1,0:T(8,128)(2,1)S(1)} %bitcast.10), custom_call_target="tpu_custom_call" | custom-call | flops 16777216 | bytes 1048576 | tf_op jit(solution)/shard_map/pallas_call | solution.py:278
  94.1 13.5 %all-to-all-done.1 = bf16[64,32,128]{2,1,0:T(8,128)(2,1)S(1)} async-done(((bf16[64,32,128]{2,1,0:T(8,128)(2,1)}), bf16[64,32,128]{2,1,0:T(8,128)(2,1)S(1)}, u32[]{:S(2)}, u32[]{:S(2)}) %all-to-all-start.1) | async-done | bytes 524320 | tf_op jit(solution)/shard_map/all_to_all | solution.py:169
  107.5 1.5 %shard_map.124 = bf16[128,2048]{1,0:T(8,128)(2,1)} custom-call(f32[128,2048]{1,0:T(8,128)S(1)} %shard_map.121.l_ref, bf16[2048,128]{1,0:T(8,128)(2,1)S(1)} %bitcast.11, bf16[128,128]{1,0:T(8,128)(2,1)S(1)} %copy-done.2, f32[16,128]{1,0:T(8,128)S(1)} %copy-done.6), custom_call_target="tpu_custom_call" | custom-call | flops 67108864 | bytes 2097152 | tf_op jit(solution)/shard_map/pallas_call | solution.py:155
  109.0 0.0 all-gather.3.cloned.1.call-done
  109.0 0.0 copy-done.11
  109.0 0.0 copy-start.10
  109.0 2.2 %copy-done.10 = bf16[16384,128]{1,0:T(8,128)(2,1)S(1)} copy-done((bf16[16384,128]{1,0:T(8,128)(2,1)S(1)}, bf16[16384,128]{1,0:T(8,128)(2,1)}, u32[]{:S(2)}) %copy-start.10) | copy-done | bytes 4194328
  111.2 11.4 %shard_map.126 = bf16[128,512]{1,0:T(8,128)(2,1)} custom-call(s32[1]{0:T(128)} %bitcast.1.me_ref, bf16[128,512]{1,0:T(8,128)(2,1)S(1)} %copy-done.11, bf16[64,256,128]{2,1,0:T(8,128)(2,1)S(1)} %bitcast.13), custom_call_target="tpu_custom_call" | custom-call | flops 2147483648 | bytes 4194304 | tf_op jit(solution)/shard_map/pallas_call | solution.py:230
Async XLA Ops:
  7.2 101.8 %all-gather.3.cloned.1.call-start = ((), (), s32[]{:S(2)}) async-start(), calls=%async_computation.3 | async-start | bytes 4259840 | tf_op jit(solution)/shard_map/all_gather | solution.py:227
  7.2 0.8 copy-start.7
  8.0 0.8 copy-start.8
  9.5 1.0 copy-start
  10.5 0.8 copy-start.3
  11.3 0.7 copy-start.5
  13.5 30.3 %all-to-all-start = ((bf16[64,40,128]{2,1,0:T(8,128)(2,1)}), bf16[64,40,128]{2,1,0:T(8,128)(2,1)S(1)}, u32[]{:S(2)}, u32[]{:S(2)}) async-start(bf16[64,40,128]{2,1,0:T(8,128)(2,1)} %shard_map.122), calls=%async_computation | async-start | bytes 1310720 | tf_op jit(solution)/shard_map/all_to_all | solution.py:167
  24.0 66.5 %copy-start.12 = (f32[16,2]{0,1:T(2,128)S(1)}, f32[16,2]{0,1:T(2,128)}, u32[]{:S(2)}) copy-start(f32[16,2]{0,1:T(2,128)} %param.18) | copy-start | bytes 388
  24.0 66.6 %copy-start.9 = (s32[16,2]{0,1:T(2,128)S(1)}, s32[16,2]{0,1:T(2,128)}, u32[]{:S(2)}) copy-start(s32[16,2]{0,1:T(2,128)} %param.17) | copy-start | bytes 388
  24.0 66.6 %copy-start.1 = (bf16[128,2048]{1,0:T(8,128)(2,1)S(1)}, bf16[128,2048]{1,0:T(8,128)(2,1)}, u32[]{:S(2)}) copy-start(bf16[128,2048]{1,0:T(8,128)(2,1)} %x_ref.3) | copy-start | bytes 1572868
  24.0 66.6 %copy-start.2 = (bf16[128,128]{1,0:T(8,128)(2,1)S(1)}, bf16[128,128]{1,0:T(8,128)(2,1)}, u32[]{:S(2)}) copy-start(bf16[128,128]{1,0:T(8,128)(2,1)} %c_ref.3) | copy-start | bytes 98308
  24.0 66.6 %copy-start.4 = (bf16[128,128]{1,0:T(8,128)(2,1)S(1)}, bf16[128,128]{1,0:T(8,128)(2,1)}, u32[]{:S(2)}) copy-start(bf16[128,128]{1,0:T(8,128)(2,1)} %b_ref.3) | copy-start | bytes 98308
  24.0 66.6 %copy-start.6 = (f32[16,128]{1,0:T(8,128)S(1)}, f32[16,128]{1,0:T(8,128)}, u32[]{:S(2)}) copy-start(f32[16,128]{1,0:T(8,128)} %d_ref.5) | copy-start | bytes 24580
  43.8 40.8 %all-to-all-start.2 = ((bf16[8,8,8192]{2,1,0:T(8,128)(2,1)}), bf16[8,8,8192]{2,1,0:T(8,128)(2,1)S(1)}, u32[]{:S(2)}, u32[]{:S(2)}) async-start(bf16[8,8,8192]{2,1,0:T(8,128)(2,1)} %copy.20), calls=%async_computation.2 | async-start | bytes 2097152 | tf_op jit(solution)/shard_map/all_to_all | solution.py:274
  55.2 53.8 %copy-start.11 = (bf16[128,512]{1,0:T(8,128)(2,1)S(1)}, bf16[128,512]{1,0:T(8,128)(2,1)}, u32[]{:S(2)}) copy-start(bf16[128,512]{1,0:T(8,128)(2,1)} %q_ref.1) | copy-start | bytes 393220
  84.5 23.0 %all-to-all-start.1 = ((bf16[64,32,128]{2,1,0:T(8,128)(2,1)}), bf16[64,32,128]{2,1,0:T(8,128)(2,1)S(1)}, u32[]{:S(2)}, u32[]{:S(2)}) async-start(bf16[64,32,128]{2,1,0:T(8,128)(2,1)} %shard_map.123), calls=%async_computation.1 | async-start | bytes 1048576 | tf_op jit(solution)/shard_map/all_to_all | solution.py:169
  109.0 2.2 %copy-start.10 = (bf16[16384,128]{1,0:T(8,128)(2,1)S(1)}, bf16[16384,128]{1,0:T(8,128)(2,1)}, u32[]{:S(2)}) copy-start(bf16[16384,128]{1,0:T(8,128)(2,1)} %all-gather.3.cloned.1.call-done) | copy-start | bytes 12582916
Sparse Core Ops, SparseCore 0:
  11.9 91.6 all-gather.2

commit v2 on v1

v2 whole, which is shorter than its diff:
```python
import math

import jax
import jax.numpy as jnp
from jax import lax
from jax.experimental import pallas as pl
from jax.experimental.pallas import tpu as pltpu
from jax.sharding import PartitionSpec as P

HD = 128
L = 128
MH = 16
NCTX = 64
QH = 4
CAP = 4
LOG2E = 1.4426950408889634
F32 = jnp.float32
BF16 = jnp.bfloat16
VM = pl.BlockSpec(memory_space=pltpu.VMEM)
SM = pl.BlockSpec(memory_space=pltpu.SMEM)
ANY = pl.BlockSpec(memory_space=pl.ANY)


def params(mib=40):
    return pltpu.CompilerParams(vmem_limit_bytes=mib * 2**20)


def cost(flops, nbytes):
    return pl.CostEstimate(flops=flops, bytes_accessed=nbytes, transcendentals=0)


def tri(lower):
    r = lax.broadcasted_iota(jnp.int32, (L, L), 0)
    c = lax.broadcasted_iota(jnp.int32, (L, L), 1)
    return (c <= r) if lower else (r <= c)


def row_cumulative(decay):
    return jnp.dot(
        decay, tri(False).astype(F32), precision=lax.Precision.HIGHEST, preferred_element_type=F32
    )


def col_cumulative(decay):
    return lax.dot_general(
        tri(True).astype(F32),
        decay,
        (((1,), (1,)), ((), ())),
        precision=lax.Precision.HIGHEST,
        preferred_element_type=F32,
    )


PIECE = 16
KV = 2 * PIECE
SL = 32
CHUNK = KV + SL + 8


def send_kernel(x_ref, b_ref, d_ref, k_ref, v_ref, o_ref):
    cum = row_cumulative(d_ref[...])
    tail = jnp.exp(cum[:, L - 1 :] - cum)
    block_decay = jnp.exp(cum[:, L - 1 :])
    bt = b_ref[...].astype(F32).T
    row = lax.broadcasted_iota(jnp.int32, (8, L), 0)
    pieces = L // PIECE
    for h in range(MH):
        wb = (tail[h : h + 1, :] * bt).astype(BF16)
        s = jnp.dot(wb, x_ref[:, h * HD : (h + 1) * HD], preferred_element_type=F32)
        d = jnp.broadcast_to(block_decay[h : h + 1, :], (8, L))
        hi = d.astype(BF16).astype(F32)
        mid = (d - hi).astype(BF16).astype(F32)
        lo = d - hi - mid
        terms = jnp.where(row == 0, hi, jnp.where(row == 1, mid, jnp.where(row == 2, lo, 0.0)))
        for q in range(4):
            j = h * 4 + q
            rows = slice((j % pieces) * PIECE, (j % pieces + 1) * PIECE)
            o_ref[j, 0:PIECE, :] = k_ref[rows, :]
            o_ref[j, PIECE:KV, :] = v_ref[rows, :]
            o_ref[j, KV:CHUNK, :] = jnp.concatenate(
                [s[q * SL : (q + 1) * SL], terms], axis=0
            ).astype(BF16)


def chunks_to_send(x_in, b_in, decay_log, k_in, v_in):
    return pl.pallas_call(
        send_kernel,
        out_shape=jax.ShapeDtypeStruct((NCTX, CHUNK, HD), BF16),
        in_specs=[VM] * 5,
        out_specs=VM,
        compiler_params=params(),
        cost_estimate=cost(1 << 26, 1 << 21),
    )(x_in, b_in, decay_log, k_in, v_in)


def take_kernel(s_ref, *refs):
    own_ref, o_ref = refs[-2:]
    own_ref[...] = s_ref[:, :KV, :]

    def step(k, e):
        o_ref[k] = e.astype(BF16)
        block = s_ref[k, KV:CHUNK, :].astype(F32)
        d = block[SL : SL + 1] + block[SL + 1 : SL + 2] + block[SL + 2 : SL + 3]
        return d * e + block[:SL]

    lax.fori_loop(0, NCTX, step, jnp.zeros((SL, HD), F32), unroll=8)


def take_received(received, after):
    return pl.pallas_call(
        take_kernel,
        out_shape=[
            jax.ShapeDtypeStruct((NCTX, KV, HD), BF16),
            jax.ShapeDtypeStruct((NCTX, SL, HD), BF16),
        ],
        in_specs=[VM] + [ANY] * len(after),
        out_specs=[VM, VM],
        compiler_params=params(),
        cost_estimate=cost(1 << 20, 1 << 21),
    )(received, *after)


def local_kernel(x_ref, b_ref, c_ref, d_ref, o_ref):
    cum = row_cumulative(d_ref[...])
    cum_col = col_cumulative(d_ref[...])
    cross = lax.dot_general(
        c_ref[...], b_ref[...], (((1,), (1,)), ((), ())), preferred_element_type=F32
    )
    mask = tri(True)
    for h in range(MH):
        gap = jnp.where(mask, cum_col[:, h : h + 1] - cum[h : h + 1, :], -1e30)
        w = (jnp.exp(gap) * cross).astype(BF16)
        o_ref[:, h * HD : (h + 1) * HD] = jnp.dot(
            w, x_ref[:, h * HD : (h + 1) * HD], preferred_element_type=F32
        )


def local_part(x_in, b_in, c_in, decay_log):
    return pl.pallas_call(
        local_kernel,
        out_shape=jax.ShapeDtypeStruct((L, MH * HD), F32),
        in_specs=[VM] * 4,
        out_specs=VM,
        compiler_params=params(),
        cost_estimate=cost(1 << 28, 1 << 21),
    )(x_in, b_in, c_in, decay_log)


def join_kernel(l_ref, e_ref, c_ref, d_ref, o_ref):
    grow = jnp.exp(col_cumulative(d_ref[...]))
    c = c_ref[...]
    for h in range(MH):
        cols = slice(h * HD, (h + 1) * HD)
        readout = jnp.dot(c, e_ref[cols, :], preferred_element_type=F32)
        o_ref[:, cols] = (l_ref[:, cols] + grow[:, h : h + 1] * readout).astype(BF16)


def join_mamba(local, entering, c_in, decay_log):
    return pl.pallas_call(
        join_kernel,
        out_shape=jax.ShapeDtypeStruct((L, MH * HD), BF16),
        in_specs=[VM] * 4,
        out_specs=VM,
        compiler_params=params(),
        cost_estimate=cost(1 << 26, 1 << 21),
    )(local, entering, c_in, decay_log)


ROWS = QH * L
SCALE2 = LOG2E / math.sqrt(HD)


def stacked_queries(q_ref):
    return jnp.concatenate([q_ref[:, g * HD : (g + 1) * HD] for g in range(QH)], axis=0)


def accumulate(state, s, v):
    m_old, total, acc = state
    m = jnp.maximum(m_old, jnp.max(s, axis=1, keepdims=True))
    factor = jnp.exp2((m_old - m) * SCALE2)
    p = jnp.exp2((s - m) * SCALE2)
    part = p[:, :L]
    for j in range(1, p.shape[1] // L):
        part = part + p[:, j * L : (j + 1) * L]
    added = jnp.dot(p.astype(BF16), v, preferred_element_type=F32)
    return m, total * factor + part, acc * factor + added


def scores(q, k):
    return lax.dot_general(q, k, (((1,), (1,)), ((), ())), preferred_element_type=F32)


def attend_kernel(n_sets, first, last, me_ref, q_ref, *refs):
    refs = list(refs)
    if first:
        k_ref, v_ref = refs[:2]
        refs = refs[2:]
    else:
        m_in, l_in, a_in = refs[:3]
        refs = refs[3:]
    sets, refs = refs[:n_sets], refs[n_sets:]
    if last:
        o_ref = refs[0]
        m_ref, l_ref, a_ref = refs[1:]
    else:
        m_ref, l_ref, a_ref = refs
    me = me_ref[0]
    q = stacked_queries(q_ref)
    if first:
        s = scores(q, k_ref[...])
        t = lax.broadcasted_iota(jnp.int32, s.shape, 0) % L
        u = lax.broadcasted_iota(jnp.int32, s.shape, 1)
        s = jnp.where(u <= t, s, -1e30)
        m = jnp.max(s, axis=1, keepdims=True)
        p = jnp.exp2((s - m) * SCALE2)
        m_ref[...] = jnp.broadcast_to(m, (ROWS, L))
        l_ref[...] = p
        a_ref[...] = jnp.dot(p.astype(BF16), v_ref[...], preferred_element_type=F32)
    else:
        m_ref[...] = m_in[...]
        l_ref[...] = l_in[...]
        a_ref[...] = a_in[...]
    shards_in = KEYS // PIECE
    for ref in sets:
        for at in range(ref.shape[0] // shards_in):
            half = at % (NCTX // shards_in)

            def work(ref=ref, at=at, half=half):
                pick = slice(at * shards_in, (at + 1) * shards_in)
                k = ref[pick, 0:PIECE, :].reshape(KEYS, HD)
                v = ref[pick, PIECE:KV, :].reshape(KEYS, HD)
                s = scores(q, k)
                shard = half * shards_in + lax.broadcasted_iota(jnp.int32, (1, KEYS), 1) // PIECE
                s = s + jnp.where(shard < me, 0.0, -1e30)
                m, total, acc = accumulate((m_ref[:, :1], l_ref[...], a_ref[...]), s, v)
                m_ref[...] = jnp.broadcast_to(m, (ROWS, L))
                l_ref[...] = total
                a_ref[...] = acc

            pl.when(half * shards_in < me)(work)
    if last:
        out = a_ref[...] / jnp.sum(l_ref[...], axis=1, keepdims=True)
        for g in range(QH):
            o_ref[:, g * HD : (g + 1) * HD] = out[g * L : (g + 1) * L].astype(BF16)


KEYS = 512


def attend(me, q_in, before, sets, last=False):
    carry = [jax.ShapeDtypeStruct((ROWS, L), F32)] * 3
    first = len(before) == 2

    def kernel(*refs):
        attend_kernel(len(sets), first, last, *refs)

    return pl.pallas_call(
        kernel,
        out_shape=jax.ShapeDtypeStruct((L, QH * HD), BF16) if last else carry,
        in_specs=[SM] + [VM] * (1 + len(before) + len(sets)),
        out_specs=VM if last else [VM] * 3,
        scratch_shapes=[pltpu.VMEM((ROWS, L), F32)] * 3 if last else [],
        compiler_params=params(),
        cost_estimate=cost(1 << 28, len(sets) << 22),
    )(me, q_in, *before, *sets)


CHIPS_X = 4


def along_x(step):
    pairs = []
    for i in range(NCTX):
        y, x, c = i // (2 * CHIPS_X), i // 2 % CHIPS_X, i % 2
        pairs.append((i, (y * CHIPS_X + (x + step) % CHIPS_X) * 2 + c))
    return pairs


def other_core(value):
    return lax.ppermute(value, "ctx", [(i, i ^ 1) for i in range(NCTX)])


def context_parts(x_in, b_in, c_in, decay_log, q_in, k_in, v_in, expert_out):
    me = lax.axis_index("ctx").astype(jnp.int32).reshape(1)
    chunks = chunks_to_send(x_in, b_in, decay_log, k_in, v_in)
    received = lax.all_to_all(chunks, "ctx", split_axis=0, concat_axis=0, tiled=True)
    blocks = expert_blocks(expert_out, chunks)
    own, entering = take_received(received, blocks[1:])
    half = NCTX // 2
    right = lax.ppermute(own, "ctx", along_x(1))
    left = lax.ppermute(own, "ctx", along_x(-1))
    far = jnp.concatenate(
        [
            lax.ppermute(right[:half], "ctx", along_x(1)),
            lax.ppermute(left[half:], "ctx", along_x(-1)),
        ]
    )
    near = jnp.concatenate([own, right, left])
    near_other = other_core(near)
    far_other = other_core(far)

    entering = lax.all_to_all(entering, "ctx", split_axis=0, concat_axis=0, tiled=True)
    local = local_part(x_in, b_in, c_in, decay_log)
    mamba_out = join_mamba(local, entering.reshape(MH * L, HD), c_in, decay_log)

    carry = attend(me, q_in, [k_in, v_in], [own, right, left])
    carry = attend(me, q_in, carry, [far, near_other])
    attn_out = attend(me, q_in, carry, [far_other], last=True)
    return mamba_out, attn_out, blocks


def blocks_kernel(me_ref, e_ref, after_ref, *outs):
    for d, o_ref in enumerate(outs):
        to = lax.rem(me_ref[0] + d, len(outs))
        o_ref[...] = jnp.concatenate(
            [e_ref[0, i, to].astype(F32) for i in range(e_ref.shape[1])], axis=0
        ).astype(BF16)


def combine_kernel(me_ref, ids_ref, idst_ref, gates_ref, *refs):
    rows_refs, o_ref = refs[:-1], refs[-1]
    peers = len(rows_refs)
    rows = jnp.concatenate([r[...].astype(F32) for r in rows_refs], axis=0).astype(BF16)
    owned = rows.shape[0] // (peers * CAP)
    count = ids_ref.shape[0]
    ids, idst, gates = ids_ref[...], idst_ref[...], gates_ref[...]
    t = lax.broadcasted_iota(jnp.int32, (count, count), 0)
    u = lax.broadcasted_iota(jnp.int32, (count, count), 1)
    place = lax.broadcasted_iota(jnp.int32, (count, rows.shape[0]), 1)
    out = None
    for k in range(2):
        mine = ids[:, k : k + 1]
        slot = jnp.zeros((count, 1), jnp.int32)
        for j in range(2):
            before = (u < t) if j >= k else (u <= t)
            same = jnp.logical_and(before, idst[j : j + 1, :] == mine)
            slot = slot + jnp.sum(same.astype(jnp.int32), axis=1, keepdims=True)
        distance = (me_ref[0] - mine // owned + peers) % peers
        number = (distance * owned + mine % owned) * CAP + slot
        pick = (place == number).astype(F32).astype(BF16)
        row = jnp.dot(pick, rows, preferred_element_type=F32)
        term = gates[:, k : k + 1] * row
        out = term if out is None else out + term
    o_ref[...] = out.astype(BF16)


def expert_blocks(expert_out, after):
    owned, peers, cap, width = expert_out.shape[1:]
    me = lax.axis_index("grp").astype(jnp.int32).reshape(1)
    held = pl.pallas_call(
        blocks_kernel,
        out_shape=[jax.ShapeDtypeStruct((owned * cap, width), BF16)] * peers,
        in_specs=[SM, VM, ANY],
        out_specs=[VM] * peers,
        compiler_params=params(),
        cost_estimate=cost(1 << 20, 1 << 21),
    )(me, expert_out, after)
    blocks = [held[0]]
    for d in range(1, peers):
        pairs = [(i, (i + d) % peers) for i in range(peers)]
        blocks.append(lax.ppermute(held[d], "grp", pairs))
    return blocks


def expert_part(expert_ids, gates, blocks):
    me = lax.axis_index("grp").astype(jnp.int32).reshape(1)
    peers = len(blocks)
    rows, width = blocks[0].shape
    count = expert_ids.shape[0]
    block = 2048
    return pl.pallas_call(
        combine_kernel,
        grid=(width // block,),
        out_shape=jax.ShapeDtypeStruct((count, width), BF16),
        in_specs=[
            SM,
            pl.BlockSpec((count, 2), lambda i: (0, 0)),
            pl.BlockSpec((2, count), lambda i: (0, 0)),
            pl.BlockSpec((count, 2), lambda i: (0, 0)),
        ]
        + [pl.BlockSpec((rows, block), lambda i: (0, i))] * peers,
        out_specs=pl.BlockSpec((count, block), lambda i: (0, i)),
        compiler_params=params(),
        cost_estimate=cost(1 << 24, 1 << 20),
    )(me, expert_ids, expert_ids.T, gates, *blocks)


def shards(x_in, b_in, c_in, decay_log, q_in, k_in, v_in, expert_ids, gates, expert_out):
    mamba_out, attn_out, blocks = context_parts(
        x_in, b_in, c_in, decay_log, q_in, k_in, v_in, expert_out
    )
    moe_out = expert_part(expert_ids, gates, blocks)
    return (mamba_out, attn_out, moe_out)


def solution(mesh):
    return jax.shard_map(
        shards,
        mesh=mesh,
        in_specs=(
            P("ctx", "grp"),
            P("ctx", None),
            P("ctx", None),
            P("grp", "ctx"),
            P("ctx", "grp"),
            P("ctx", "grp"),
            P("ctx", "grp"),
            P(("ctx", "grp"), None),
            P(("ctx", "grp"), None),
            P("ctx", "grp", None, None, None),
        ),
        out_specs=(P("ctx", "grp"), P("ctx", "grp"), P(("ctx", "grp"), None)),
        check_vma=False,
    )
```

time: 130 us -> 155 us (1.19)
  the two profiles are of different devices: /device:TPU:57 before, /device:TPU:115 now
where the time goes in v2:
time: 155 us; the launch traced here: 154 us
  starting transfers between devices  68.6 us (44%)
  waiting for transfers between devices  36.9 us (24%)
  Pallas kernels  27.9 us (18%)
  local copies, waits for them, and re-layouts  17.9 us (12%)
    ppermute x7, starting transfers between devices, expert_blocks(): blocks.append(lax.ppermute(held[d], 'grp', pairs))  30.7 us
    pallas_call x3, Pallas kernels, attend(): pl.pallas_call(kernel, out_shape=jax.ShapeDtypeStruct((L, QH * HD), BF16)...  20.2 us
    unnamed x67, local copies, waits for them, and re-layouts  17.1 us
    ppermute x7, waiting for transfers between devices, expert_blocks(): blocks.append(lax.ppermute(held[d], 'grp', pairs))  14.5 us
    all_to_all x1, starting transfers between devices, context_parts(): lax.all_to_all(chunks, 'ctx', split_axis=0, concat_axis=0, tiled=True)  10.6 us
    all_to_all x1, starting transfers between devices, context_parts(): lax.all_to_all(entering, 'ctx', split_axis=0, concat_axis=0, tiled=True)  10.2 us
    ppermute x1, waiting for transfers between devices, context_parts(): right = lax.ppermute(own, 'ctx', along_x(1))  9.6 us
    ppermute x1, waiting for transfers between devices, context_parts(): lax.ppermute(right[:half], 'ctx', along_x(1))  7.19 us
  transfers between devices with their start and end apart: 15, of which 7 were waited for; matrix products, arithmetic and copies ran while one was open for 1% of the time, Pallas kernels for 14%

profile of v2, /device:TPU:115, one launch (start us, length us, event | category | flops | bytes accessed | tf_op | source)
XLA Modules:
  0.0 153.6 jit_solution(17728980546067142105)
XLA Ops:
  0.6 1.0 copy-done
  1.7 0.8 copy-done.16
  2.4 0.8 copy-done.20
  3.2 0.8 copy-done.22
  4.6 1.7 %shard_map.122.after_ref = bf16[64,72,128]{2,1,0:T(8,128)(2,1)} custom-call(bf16[128,2048]{1,0:T(8,128)(2,1)S(1)} %copy-done, bf16[128,128]{1,0:T(8,128)(2,1)S(1)} %copy-done.16, f32[16,128]{1,0:T(8,128)S(1)} %copy-done.26, bf16[128,128]{1,0:T(8,128)(2,1)S(1)} %copy-done.20, bf16[128,128]{1,0:T(8,128)(2,1)S(1)} %copy-done.22), custom_call_target="tpu_custom_call" | custom-call | flops 67108864 | bytes 2097152 | tf_op jit(solution)/shard_map/pallas_call | solution.py:86
  6.4 10.6 %all-to-all-start = ((bf16[64,72,128]{2,1,0:T(8,128)(2,1)}), bf16[64,72,128]{2,1,0:T(8,128)(2,1)S(1)}, u32[]{:S(2)}, u32[]{:S(2)}) async-start(bf16[64,72,128]{2,1,0:T(8,128)(2,1)} %shard_map.122.after_ref), calls=%async_computation | async-start | bytes 2359296 | tf_op jit(solution)/shard_map/all_to_all | solution.py:286
  17.9 4.0 %collective-permute-start = (bf16[8,8192]{1,0:T(8,128)(2,1)S(1)}, bf16[8,8192]{1,0:T(8,128)(2,1)S(1)}, u32[]{:S(2)}, u32[]{:S(2)}) collective-permute-start(bf16[8,8192]{1,0:T(8,128)(2,1)S(1)} %get-tuple-element.19), channel_id=1, source_target_pairs={{0,1},{1,2},{2,3},{3,4},{4,5},{5,6},{6,7},{7,0},{8,9},{9,10},{10,1... | collective-permute-start | bytes 393224 | tf_op jit(solution)/shard_map/ppermute | solution.py:361
  21.9 7.0 %collective-permute-start.1 = (bf16[8,8192]{1,0:T(8,128)(2,1)S(1)}, bf16[8,8192]{1,0:T(8,128)(2,1)S(1)}, u32[]{:S(2)}, u32[]{:S(2)}) collective-permute-start(bf16[8,8192]{1,0:T(8,128)(2,1)S(1)} %get-tuple-element.20), channel_id=1, source_target_pairs={{0,2},{1,3},{2,4},{3,5},{4,6},{5,7},{6,0},{7,1},{8,10},{9,11},{10,... | collective-permute-start | bytes 393224 | tf_op jit(solution)/shard_map/ppermute | solution.py:361
  29.0 4.9 %collective-permute-start.2 = (bf16[8,8192]{1,0:T(8,128)(2,1)S(1)}, bf16[8,8192]{1,0:T(8,128)(2,1)S(1)}, u32[]{:S(2)}, u32[]{:S(2)}) collective-permute-start(bf16[8,8192]{1,0:T(8,128)(2,1)S(1)} %get-tuple-element.21), channel_id=1, source_target_pairs={{0,3},{1,4},{2,5},{3,6},{4,7},{5,0},{6,1},{7,2},{8,11},{9,12},{10,... | collective-permute-start | bytes 393224 | tf_op jit(solution)/shard_map/ppermute | solution.py:361
  33.9 1.9 %collective-permute-start.3 = (bf16[8,8192]{1,0:T(8,128)(2,1)S(1)}, bf16[8,8192]{1,0:T(8,128)(2,1)S(1)}, u32[]{:S(2)}, u32[]{:S(2)}) collective-permute-start(bf16[8,8192]{1,0:T(8,128)(2,1)S(1)} %get-tuple-element.22), channel_id=1, source_target_pairs={{0,4},{1,5},{2,6},{3,7},{4,0},{5,1},{6,2},{7,3},{8,12},{9,13},{10,... | collective-permute-start | bytes 393224 | tf_op jit(solution)/shard_map/ppermute | solution.py:361
  35.8 6.1 %collective-permute-start.4 = (bf16[8,8192]{1,0:T(8,128)(2,1)S(1)}, bf16[8,8192]{1,0:T(8,128)(2,1)S(1)}, u32[]{:S(2)}, u32[]{:S(2)}) collective-permute-start(bf16[8,8192]{1,0:T(8,128)(2,1)S(1)} %get-tuple-element.23), channel_id=1, source_target_pairs={{0,5},{1,6},{2,7},{3,0},{4,1},{5,2},{6,3},{7,4},{8,13},{9,14},{10,... | collective-permute-start | bytes 393224 | tf_op jit(solution)/shard_map/ppermute | solution.py:361
  41.9 3.4 %collective-permute-start.5 = (bf16[8,8192]{1,0:T(8,128)(2,1)S(1)}, bf16[8,8192]{1,0:T(8,128)(2,1)S(1)}, u32[]{:S(2)}, u32[]{:S(2)}) collective-permute-start(bf16[8,8192]{1,0:T(8,128)(2,1)S(1)} %get-tuple-element.24), channel_id=1, source_target_pairs={{0,6},{1,7},{2,0},{3,1},{4,2},{5,3},{6,4},{7,5},{8,14},{9,15},{10,... | collective-permute-start | bytes 393224 | tf_op jit(solution)/shard_map/ppermute | solution.py:361
  45.3 3.4 %collective-permute-start.6 = (bf16[8,8192]{1,0:T(8,128)(2,1)S(1)}, bf16[8,8192]{1,0:T(8,128)(2,1)S(1)}, u32[]{:S(2)}, u32[]{:S(2)}) collective-permute-start(bf16[8,8192]{1,0:T(8,128)(2,1)S(1)} %get-tuple-element.25), channel_id=1, source_target_pairs={{0,7},{1,0},{2,1},{3,2},{4,3},{5,4},{6,5},{7,6},{8,15},{9,8},{10,9... | collective-permute-start | bytes 393224 | tf_op jit(solution)/shard_map/ppermute | solution.py:361
  48.7 6.5 %collective-permute-done.4.refs_4_.refs_5_ = bf16[8,8192]{1,0:T(8,128)(2,1)S(1)} collective-permute-done((bf16[8,8192]{1,0:T(8,128)(2,1)S(1)}, bf16[8,8192]{1,0:T(8,128)(2,1)S(1)}, u32[]{:S(2)}, u32[]{:S(2)}) %collective-permute-start.4) | collective-permute-done | bytes 131104 | tf_op jit(solution)/shard_map/ppermute | solution.py:361
  55.2 1.8 %collective-permute-done.5.refs_5_.refs_6_ = bf16[8,8192]{1,0:T(8,128)(2,1)S(1)} collective-permute-done((bf16[8,8192]{1,0:T(8,128)(2,1)S(1)}, bf16[8,8192]{1,0:T(8,128)(2,1)S(1)}, u32[]{:S(2)}, u32[]{:S(2)}) %collective-permute-start.5) | collective-permute-done | bytes 131104 | tf_op jit(solution)/shard_map/ppermute | solution.py:361
  57.0 6.2 %collective-permute-done.6.refs_6_.refs_7_ = bf16[8,8192]{1,0:T(8,128)(2,1)S(1)} collective-permute-done((bf16[8,8192]{1,0:T(8,128)(2,1)S(1)}, bf16[8,8192]{1,0:T(8,128)(2,1)S(1)}, u32[]{:S(2)}, u32[]{:S(2)}) %collective-permute-start.6) | collective-permute-done | bytes 131104 | tf_op jit(solution)/shard_map/ppermute | solution.py:361
  63.3 1.0 shard_map.124
  64.3 3.1 %collective-permute-start.7 = (bf16[64,32,128]{2,1,0:T(8,128)(2,1)S(1)}, bf16[64,32,128]{2,1,0:T(8,128)(2,1)S(1)}, u32[]{:S(2)}, u32[]{:S(2)}) collective-permute-start(bf16[64,32,128]{2,1,0:T(8,128)(2,1)S(1)} %get-tuple-element.27.refs_4_), channel_id=1, source_target_pairs={{0,16},{8,24},{16,32},{24,40},{32,48},{40,56},{48,0},{56,8},{64,80... | collective-permute-start | bytes 1572872 | tf_op jit(solution)/shard_map/ppermute | solution.py:290
  67.4 2.2 %collective-permute-start.8 = (bf16[64,32,128]{2,1,0:T(8,128)(2,1)S(1)}, bf16[64,32,128]{2,1,0:T(8,128)(2,1)S(1)}, u32[]{:S(2)}, u32[]{:S(2)}) collective-permute-start(bf16[64,32,128]{2,1,0:T(8,128)(2,1)S(1)} %get-tuple-element.27.refs_4_), channel_id=1, source_target_pairs={{0,48},{8,56},{16,0},{24,8},{32,16},{40,24},{48,32},{56,40},{64,11... | collective-permute-start | bytes 1572872 | tf_op jit(solution)/shard_map/ppermute | solution.py:291
  69.6 9.6 %collective-permute-done.7.refs_5_ = bf16[64,32,128]{2,1,0:T(8,128)(2,1)S(1)} collective-permute-done((bf16[64,32,128]{2,1,0:T(8,128)(2,1)S(1)}, bf16[64,32,128]{2,1,0:T(8,128)(2,1)S(1)}, u32[]{:S(2)}, u32[]{:S(2)}) %collective-permute-start.7) | collective-permute-done | bytes 524320 | tf_op jit(solution)/shard_map/ppermute | solution.py:290
  79.2 2.8 %collective-permute-done.8.refs_6_ = bf16[64,32,128]{2,1,0:T(8,128)(2,1)S(1)} collective-permute-done((bf16[64,32,128]{2,1,0:T(8,128)(2,1)S(1)}, bf16[64,32,128]{2,1,0:T(8,128)(2,1)S(1)}, u32[]{:S(2)}, u32[]{:S(2)}) %collective-permute-start.8) | collective-permute-done | bytes 524320 | tf_op jit(solution)/shard_map/ppermute | solution.py:291
  82.0 1.3 pad_maximum_fusion
  83.3 3.6 %collective-permute-start.11 = (bf16[192,32,128]{2,1,0:T(8,128)(2,1)}, bf16[192,32,128]{2,1,0:T(8,128)(2,1)}, u32[]{:S(2)}, u32[]{:S(2)}) collective-permute-start(bf16[192,32,128]{2,1,0:T(8,128)(2,1)} %pad_maximum_fusion), channel_id=1, source_target_pairs={{0,8},{8,0},{16,24},{24,16},{32,40},{40,32},{48,56},{56,48},{64,72... | collective-permute-start | bytes 4718600 | tf_op jit(solution)/shard_map/ppermute | solution.py:280
  87.0 10.2 %all-to-all-start.1 = ((bf16[64,32,128]{2,1,0:T(8,128)(2,1)}), bf16[64,32,128]{2,1,0:T(8,128)(2,1)S(1)}, u32[]{:S(2)}, u32[]{:S(2)}) async-start(bf16[64,32,128]{2,1,0:T(8,128)(2,1)} %get-tuple-element.26), calls=%async_computation.1 | async-start | bytes 1048576 | tf_op jit(solution)/shard_map/all_to_all | solution.py:302
  97.2 3.1 %collective-permute-start.9 = (bf16[32,32,128]{2,1,0:T(8,128)(2,1)S(1)}, bf16[32,32,128]{2,1,0:T(8,128)(2,1)S(1)}, u32[]{:S(2)}, u32[]{:S(2)}) collective-permute-start(bf16[32,32,128]{2,1,0:T(8,128)(2,1)S(1)} %slice.8), channel_id=1, source_target_pairs={{0,16},{8,24},{16,32},{24,40},{32,48},{40,56},{48,0},{56,8},{64,80... | collective-permute-start | bytes 786440 | tf_op jit(solution)/shard_map/ppermute | solution.py:294
  100.3 2.2 %collective-permute-start.10 = (bf16[32,32,128]{2,1,0:T(8,128)(2,1)S(1)}, bf16[32,32,128]{2,1,0:T(8,128)(2,1)S(1)}, u32[]{:S(2)}, u32[]{:S(2)}) collective-permute-start(bf16[32,32,128]{2,1,0:T(8,128)(2,1)S(1)} %slice.9), channel_id=1, source_target_pairs={{0,48},{8,56},{16,0},{24,8},{32,16},{40,24},{48,32},{56,40},{64,11... | collective-permute-start | bytes 786440 | tf_op jit(solution)/shard_map/ppermute | solution.py:295
  102.5 7.2 %collective-permute-done.9 = bf16[32,32,128]{2,1,0:T(8,128)(2,1)S(1)} collective-permute-done((bf16[32,32,128]{2,1,0:T(8,128)(2,1)S(1)}, bf16[32,32,128]{2,1,0:T(8,128)(2,1)S(1)}, u32[]{:S(2)}, u32[]{:S(2)}) %collective-permute-start.9) | collective-permute-done | bytes 262176 | tf_op jit(solution)/shard_map/ppermute | solution.py:294
  109.7 0.7 constant_dynamic-update-slice_fusion.1
  110.4 2.8 %collective-permute-done.10 = bf16[32,32,128]{2,1,0:T(8,128)(2,1)S(1)} collective-permute-done((bf16[32,32,128]{2,1,0:T(8,128)(2,1)S(1)}, bf16[32,32,128]{2,1,0:T(8,128)(2,1)S(1)}, u32[]{:S(2)}, u32[]{:S(2)}) %collective-permute-start.10) | collective-permute-done | bytes 262176 | tf_op jit(solution)/shard_map/ppermute | solution.py:295
  113.9 3.0 %collective-permute-start.12 = (bf16[64,32,128]{2,1,0:T(8,128)(2,1)}, bf16[64,32,128]{2,1,0:T(8,128)(2,1)}, u32[]{:S(2)}, u32[]{:S(2)}) collective-permute-start(bf16[64,32,128]{2,1,0:T(8,128)(2,1)} %constant_dynamic-update-slice_fusion.refs_5_), channel_id=1, source_target_pairs={{0,8},{8,0},{16,24},{24,16},{32,40},{40,32},{48,56},{56,48},{64,72... | collective-permute-start | bytes 1572872 | tf_op jit(solution)/shard_map/ppermute | solution.py:280
  117.7 0.8 copy-done.17
  118.5 0.8 copy-done.18
  119.2 0.8 shard_map.121.l_ref
  120.1 0.9 copy-done.7
  121.0 0.9 copy-done.9
  121.9 0.9 copy-done.11
  122.8 0.9 copy-done.13
  123.7 0.9 copy-done.15
  124.6 0.9 copy-done.25
  126.2 2.5 %shard_map.129 = bf16[16,8192]{1,0:T(8,128)(2,1)} custom-call(s32[1]{0:T(128)} %bitcast.me_ref, s32[16,2]{1,0:T(8,128)S(1)} %copy.13.ids_ref, s32[2,16]{1,0:T(2,128)S(1)} %bitcast.5, f32[16,2]{1,0:T(8,128)S(1)} %copy-done.28, bf16[8,8192]{1,0:T(8,128)(2,1)S(1)} %copy-done.25, bf16[8,8192]{1,0:T(8,128)(2,1)S(1)} %collective-permute-done.refs_0_.refs_1_, ...), custom_call_target="tpu_custom_call" | custom-call | flops 16777216 | bytes 1048576 | tf_op jit(solution)/shard_map/pallas_call | solution.py:371
  128.7 1.0 copy-done.3
  129.7 0.8 copy-done.21
  130.5 0.8 copy-done.23
  131.2 6.5 %shard_map.126 = (f32[512,128]{1,0:T(8,128)S(1)}, f32[512,128]{1,0:T(8,128)S(1)}, f32[512,128]{1,0:T(8,128)S(1)}) custom-call(s32[1]{0:T(128)} %bitcast.2.refs_0_, bf16[128,512]{1,0:T(8,128)(2,1)S(1)} %copy-done.4, bf16[128,128]{1,0:T(8,128)(2,1)S(1)} %copy-done.21, bf16[128,128]{1,0:T(8,128)(2,1)S(1)} %copy-done.23, bf16[64,32,128]{2,1,0:T(8,128)(2,1)S(1)} %copy-done.3, ...), custom_call_target="tpu_custom_call" | custom-call | flops 268435456 | bytes 12582912 | tf_op jit(solution)/shard_map/pallas_call | solution.py:257
  137.7 0.8 copy-done.19
  138.5 1.4 shard_map.125
  139.9 9.8 %shard_map.127 = (f32[512,128]{1,0:T(8,128)S(1)}, f32[512,128]{1,0:T(8,128)S(1)}, f32[512,128]{1,0:T(8,128)S(1)}) custom-call(s32[1]{0:T(128)} %bitcast.2.refs_0_, bf16[128,512]{1,0:T(8,128)(2,1)S(1)} %copy-done.4, f32[512,128]{1,0:T(8,128)S(1)} %get-tuple-element.28.refs_2_, f32[512,128]{1,0:T(8,128)S(1)} %get-tuple-element.29.refs_3_, ...), custom_call_target="tpu_custom_call" | custom-call | flops 268435456 | bytes 8388608 | tf_op jit(solution)/shard_map/pallas_call | solution.py:257
  149.7 3.9 %shard_map.128 = bf16[128,512]{1,0:T(8,128)(2,1)} custom-call(s32[1]{0:T(128)} %bitcast.2.refs_0_, bf16[128,512]{1,0:T(8,128)(2,1)S(1)} %copy-done.4, f32[512,128]{1,0:T(8,128)S(1)} %get-tuple-element.31.refs_2_, f32[512,128]{1,0:T(8,128)S(1)} %get-tuple-element.32.refs_3_, f32[512,128]{1,0:T(8,128)S(1)} %get-tuple-element.33.refs_4_, ...), custom_call_target="tpu_custom_call" | custom-call | flops 268435456 | bytes 4194304 | tf_op jit(solution)/shard_map/pallas_call | solution.py:257
  (62 shorter events, 3.9 us)
Async XLA Ops:
  0.6 1.0 copy-start
  1.7 0.8 copy-start.16
  2.4 0.8 copy-start.20
  3.2 0.8 copy-start.22
  3.9 0.7 copy-start.26
  6.4 10.7 %copy-start.5 = (bf16[1,2,8,4,8192]{4,3,2,1,0:T(4,128)(2,1)S(1)}, bf16[1,2,8,4,8192]{4,3,2,1,0:T(4,128)(2,1)}, u32[]{:S(2)}) copy-start(bf16[1,2,8,4,8192]{4,3,2,1,0:T(4,128)(2,1)} %e_ref.1) | copy-start | bytes 3145732
  6.4 56.9 %all-to-all-start = ((bf16[64,72,128]{2,1,0:T(8,128)(2,1)}), bf16[64,72,128]{2,1,0:T(8,128)(2,1)S(1)}, u32[]{:S(2)}, u32[]{:S(2)}) async-start(bf16[64,72,128]{2,1,0:T(8,128)(2,1)} %shard_map.122.after_ref), calls=%async_computation | async-start | bytes 2359296 | tf_op jit(solution)/shard_map/all_to_all | solution.py:286
  17.3 0.7 copy-start.24
  17.9 24.0 %collective-permute-start = (bf16[8,8192]{1,0:T(8,128)(2,1)S(1)}, bf16[8,8192]{1,0:T(8,128)(2,1)S(1)}, u32[]{:S(2)}, u32[]{:S(2)}) collective-permute-start(bf16[8,8192]{1,0:T(8,128)(2,1)S(1)} %get-tuple-element.19), channel_id=1, source_target_pairs={{0,1},{1,2},{2,3},{3,4},{4,5},{5,6},{6,7},{7,0},{8,9},{9,10},{10,1... | collective-permute-start | bytes 393224 | tf_op jit(solution)/shard_map/ppermute | solution.py:361
  21.9 23.4 %collective-permute-start.1 = (bf16[8,8192]{1,0:T(8,128)(2,1)S(1)}, bf16[8,8192]{1,0:T(8,128)(2,1)S(1)}, u32[]{:S(2)}, u32[]{:S(2)}) collective-permute-start(bf16[8,8192]{1,0:T(8,128)(2,1)S(1)} %get-tuple-element.20), channel_id=1, source_target_pairs={{0,2},{1,3},{2,4},{3,5},{4,6},{5,7},{6,0},{7,1},{8,10},{9,11},{10,... | collective-permute-start | bytes 393224 | tf_op jit(solution)/shard_map/ppermute | solution.py:361
  29.0 19.7 %collective-permute-start.2 = (bf16[8,8192]{1,0:T(8,128)(2,1)S(1)}, bf16[8,8192]{1,0:T(8,128)(2,1)S(1)}, u32[]{:S(2)}, u32[]{:S(2)}) collective-permute-start(bf16[8,8192]{1,0:T(8,128)(2,1)S(1)} %get-tuple-element.21), channel_id=1, source_target_pairs={{0,3},{1,4},{2,5},{3,6},{4,7},{5,0},{6,1},{7,2},{8,11},{9,12},{10,... | collective-permute-start | bytes 393224 | tf_op jit(solution)/shard_map/ppermute | solution.py:361
  33.9 14.8 %collective-permute-start.3 = (bf16[8,8192]{1,0:T(8,128)(2,1)S(1)}, bf16[8,8192]{1,0:T(8,128)(2,1)S(1)}, u32[]{:S(2)}, u32[]{:S(2)}) collective-permute-start(bf16[8,8192]{1,0:T(8,128)(2,1)S(1)} %get-tuple-element.22), channel_id=1, source_target_pairs={{0,4},{1,5},{2,6},{3,7},{4,0},{5,1},{6,2},{7,3},{8,12},{9,13},{10,... | collective-permute-start | bytes 393224 | tf_op jit(solution)/shard_map/ppermute | solution.py:361
  35.8 19.4 %collective-permute-start.4 = (bf16[8,8192]{1,0:T(8,128)(2,1)S(1)}, bf16[8,8192]{1,0:T(8,128)(2,1)S(1)}, u32[]{:S(2)}, u32[]{:S(2)}) collective-permute-start(bf16[8,8192]{1,0:T(8,128)(2,1)S(1)} %get-tuple-element.23), channel_id=1, source_target_pairs={{0,5},{1,6},{2,7},{3,0},{4,1},{5,2},{6,3},{7,4},{8,13},{9,14},{10,... | collective-permute-start | bytes 393224 | tf_op jit(solution)/shard_map/ppermute | solution.py:361
  41.9 15.1 %collective-permute-start.5 = (bf16[8,8192]{1,0:T(8,128)(2,1)S(1)}, bf16[8,8192]{1,0:T(8,128)(2,1)S(1)}, u32[]{:S(2)}, u32[]{:S(2)}) collective-permute-start(bf16[8,8192]{1,0:T(8,128)(2,1)S(1)} %get-tuple-element.24), channel_id=1, source_target_pairs={{0,6},{1,7},{2,0},{3,1},{4,2},{5,3},{6,4},{7,5},{8,14},{9,15},{10,... | collective-permute-start | bytes 393224 | tf_op jit(solution)/shard_map/ppermute | solution.py:361
  45.3 17.9 %collective-permute-start.6 = (bf16[8,8192]{1,0:T(8,128)(2,1)S(1)}, bf16[8,8192]{1,0:T(8,128)(2,1)S(1)}, u32[]{:S(2)}, u32[]{:S(2)}) collective-permute-start(bf16[8,8192]{1,0:T(8,128)(2,1)S(1)} %get-tuple-element.25), channel_id=1, source_target_pairs={{0,7},{1,0},{2,1},{3,2},{4,3},{5,4},{6,5},{7,6},{8,15},{9,8},{10,9... | collective-permute-start | bytes 393224 | tf_op jit(solution)/shard_map/ppermute | solution.py:361
  48.7 34.6 %copy-start.6 = (bf16[8,8192]{1,0:T(8,128)(2,1)}, bf16[8,8192]{1,0:T(8,128)(2,1)S(1)}, u32[]{:S(2)}) copy-start(bf16[8,8192]{1,0:T(8,128)(2,1)S(1)} %collective-permute-done.2.refs_2_.refs_3_) | copy-start | bytes 393220
  48.7 34.6 %copy-start.8 = (bf16[8,8192]{1,0:T(8,128)(2,1)}, bf16[8,8192]{1,0:T(8,128)(2,1)S(1)}, u32[]{:S(2)}) copy-start(bf16[8,8192]{1,0:T(8,128)(2,1)S(1)} %collective-permute-done.3.refs_3_.refs_4_) | copy-start | bytes 393220
  55.2 28.1 %copy-start.10 = (bf16[8,8192]{1,0:T(8,128)(2,1)}, bf16[8,8192]{1,0:T(8,128)(2,1)S(1)}, u32[]{:S(2)}) copy-start(bf16[8,8192]{1,0:T(8,128)(2,1)S(1)} %collective-permute-done.4.refs_4_.refs_5_) | copy-start | bytes 393220
  57.0 26.3 %copy-start.12 = (bf16[8,8192]{1,0:T(8,128)(2,1)}, bf16[8,8192]{1,0:T(8,128)(2,1)S(1)}, u32[]{:S(2)}) copy-start(bf16[8,8192]{1,0:T(8,128)(2,1)S(1)} %collective-permute-done.5.refs_5_.refs_6_) | copy-start | bytes 393220
  63.3 20.1 %copy-start.14 = (bf16[8,8192]{1,0:T(8,128)(2,1)}, bf16[8,8192]{1,0:T(8,128)(2,1)S(1)}, u32[]{:S(2)}) copy-start(bf16[8,8192]{1,0:T(8,128)(2,1)S(1)} %collective-permute-done.6.refs_6_.refs_7_) | copy-start | bytes 393220
  64.3 19.0 %copy-start.2 = (bf16[64,32,128]{2,1,0:T(8,128)(2,1)}, bf16[64,32,128]{2,1,0:T(8,128)(2,1)S(1)}, u32[]{:S(2)}) copy-start(bf16[64,32,128]{2,1,0:T(8,128)(2,1)S(1)} %get-tuple-element.27.refs_4_) | copy-start | bytes 1572868
  64.3 14.9 %collective-permute-start.7 = (bf16[64,32,128]{2,1,0:T(8,128)(2,1)S(1)}, bf16[64,32,128]{2,1,0:T(8,128)(2,1)S(1)}, u32[]{:S(2)}, u32[]{:S(2)}) collective-permute-start(bf16[64,32,128]{2,1,0:T(8,128)(2,1)S(1)} %get-tuple-element.27.refs_4_), channel_id=1, source_target_pairs={{0,16},{8,24},{16,32},{24,40},{32,48},{40,56},{48,0},{56,8},{64,80... | collective-permute-start | bytes 1572872 | tf_op jit(solution)/shard_map/ppermute | solution.py:290
  67.4 14.6 %collective-permute-start.8 = (bf16[64,32,128]{2,1,0:T(8,128)(2,1)S(1)}, bf16[64,32,128]{2,1,0:T(8,128)(2,1)S(1)}, u32[]{:S(2)}, u32[]{:S(2)}) collective-permute-start(bf16[64,32,128]{2,1,0:T(8,128)(2,1)S(1)} %get-tuple-element.27.refs_4_), channel_id=1, source_target_pairs={{0,48},{8,56},{16,0},{24,8},{32,16},{40,24},{48,32},{56,40},{64,11... | collective-permute-start | bytes 1572872 | tf_op jit(solution)/shard_map/ppermute | solution.py:291
  83.3 56.6 %collective-permute-start.11 = (bf16[192,32,128]{2,1,0:T(8,128)(2,1)}, bf16[192,32,128]{2,1,0:T(8,128)(2,1)}, u32[]{:S(2)}, u32[]{:S(2)}) collective-permute-start(bf16[192,32,128]{2,1,0:T(8,128)(2,1)} %pad_maximum_fusion), channel_id=1, source_target_pairs={{0,8},{8,0},{16,24},{24,16},{32,40},{40,32},{48,56},{56,48},{64,72... | collective-permute-start | bytes 4718600 | tf_op jit(solution)/shard_map/ppermute | solution.py:280
  86.9 30.0 %copy-start.29 = (s32[16,2]{0,1:T(2,128)S(1)}, s32[16,2]{0,1:T(2,128)}, u32[]{:S(2)}) copy-start(s32[16,2]{0,1:T(2,128)} %param.17) | copy-start | bytes 388
  86.9 30.1 %copy-start.31 = (f32[16,2]{0,1:T(2,128)S(1)}, f32[16,2]{0,1:T(2,128)}, u32[]{:S(2)}) copy-start(f32[16,2]{0,1:T(2,128)} %param.18) | copy-start | bytes 388
  86.9 30.8 %copy-start.1 = (bf16[128,2048]{1,0:T(8,128)(2,1)S(1)}, bf16[128,2048]{1,0:T(8,128)(2,1)}, u32[]{:S(2)}) copy-start(bf16[128,2048]{1,0:T(8,128)(2,1)} %x_ref.3) | copy-start | bytes 1572868
  87.0 30.8 %copy-start.27 = (f32[16,128]{1,0:T(8,128)S(1)}, f32[16,128]{1,0:T(8,128)}, u32[]{:S(2)}) copy-start(f32[16,128]{1,0:T(8,128)} %d_ref.5) | copy-start | bytes 24580
  87.0 50.7 %all-to-all-start.1 = ((bf16[64,32,128]{2,1,0:T(8,128)(2,1)}), bf16[64,32,128]{2,1,0:T(8,128)(2,1)S(1)}, u32[]{:S(2)}, u32[]{:S(2)}) async-start(bf16[64,32,128]{2,1,0:T(8,128)(2,1)} %get-tuple-element.26), calls=%async_computation.1 | async-start | bytes 1048576 | tf_op jit(solution)/shard_map/all_to_all | solution.py:302
  97.2 12.5 %collective-permute-start.9 = (bf16[32,32,128]{2,1,0:T(8,128)(2,1)S(1)}, bf16[32,32,128]{2,1,0:T(8,128)(2,1)S(1)}, u32[]{:S(2)}, u32[]{:S(2)}) collective-permute-start(bf16[32,32,128]{2,1,0:T(8,128)(2,1)S(1)} %slice.8), channel_id=1, source_target_pairs={{0,16},{8,24},{16,32},{24,40},{32,48},{40,56},{48,0},{56,8},{64,80... | collective-permute-start | bytes 786440 | tf_op jit(solution)/shard_map/ppermute | solution.py:294
  100.3 12.9 %collective-permute-start.10 = (bf16[32,32,128]{2,1,0:T(8,128)(2,1)S(1)}, bf16[32,32,128]{2,1,0:T(8,128)(2,1)S(1)}, u32[]{:S(2)}, u32[]{:S(2)}) collective-permute-start(bf16[32,32,128]{2,1,0:T(8,128)(2,1)S(1)} %slice.9), channel_id=1, source_target_pairs={{0,48},{8,56},{16,0},{24,8},{32,16},{40,24},{48,32},{56,40},{64,11... | collective-permute-start | bytes 786440 | tf_op jit(solution)/shard_map/ppermute | solution.py:295
  113.9 14.8 %copy-start.4 = (bf16[128,512]{1,0:T(8,128)(2,1)S(1)}, bf16[128,512]{1,0:T(8,128)(2,1)}, u32[]{:S(2)}) copy-start(bf16[128,512]{1,0:T(8,128)(2,1)} %refs_1_.5) | copy-start | bytes 393220
  113.9 35.8 %collective-permute-start.12 = (bf16[64,32,128]{2,1,0:T(8,128)(2,1)}, bf16[64,32,128]{2,1,0:T(8,128)(2,1)}, u32[]{:S(2)}, u32[]{:S(2)}) collective-permute-start(bf16[64,32,128]{2,1,0:T(8,128)(2,1)} %constant_dynamic-update-slice_fusion.refs_5_), channel_id=1, source_target_pairs={{0,8},{8,0},{16,24},{24,16},{32,40},{40,32},{48,56},{56,48},{64,72... | collective-permute-start | bytes 1572872 | tf_op jit(solution)/shard_map/ppermute | solution.py:280
  117.7 0.8 copy-start.17
  118.5 0.8 copy-start.18
  119.2 0.8 copy-start.28
  120.1 0.9 copy-start.7
  121.0 0.9 copy-start.9
  121.9 0.9 copy-start.11
  122.8 0.9 copy-start.13
  123.7 0.9 copy-start.15
  124.6 0.9 copy-start.25
  125.5 0.7 copy-start.30
  128.7 1.0 copy-start.3
  129.7 0.8 copy-start.21
  130.5 0.8 copy-start.23
  137.7 0.8 copy-start.19

commit v3 on v2

--- a/solution.py
+++ b/solution.py
@@ -21,7 +21,10 @@
 ANY = pl.BlockSpec(memory_space=pl.ANY)
 
 
-def params(mib=40):
+LARGE, SMALL = 60, 16
+
+
+def params(mib=SMALL):
     return pltpu.CompilerParams(vmem_limit_bytes=mib * 2**20)
 
 
@@ -88,7 +91,7 @@
         out_shape=jax.ShapeDtypeStruct((NCTX, CHUNK, HD), BF16),
         in_specs=[VM] * 5,
         out_specs=VM,
-        compiler_params=params(),
+        compiler_params=params(LARGE),
         cost_estimate=cost(1 << 26, 1 << 21),
     )(x_in, b_in, decay_log, k_in, v_in)
 
@@ -141,12 +144,16 @@
         out_shape=jax.ShapeDtypeStruct((L, MH * HD), F32),
         in_specs=[VM] * 4,
         out_specs=VM,
-        compiler_params=params(),
+        compiler_params=params(LARGE),
         cost_estimate=cost(1 << 28, 1 << 21),
     )(x_in, b_in, c_in, decay_log)
 
 
-def join_kernel(l_ref, e_ref, c_ref, d_ref, o_ref):
+JOIN_COST = 1 << 35
+
+
+def join_kernel(l_ref, e_ref, c_ref, d_ref, *refs):
+    o_ref = refs[-1]
     grow = jnp.exp(col_cumulative(d_ref[...]))
     c = c_ref[...]
     for h in range(MH):
@@ -155,15 +162,15 @@
         o_ref[:, cols] = (l_ref[:, cols] + grow[:, h : h + 1] * readout).astype(BF16)
 
 
-def join_mamba(local, entering, c_in, decay_log):
+def join_mamba(local, entering, c_in, decay_log, after):
     return pl.pallas_call(
         join_kernel,
         out_shape=jax.ShapeDtypeStruct((L, MH * HD), BF16),
-        in_specs=[VM] * 4,
+        in_specs=[VM] * 4 + [ANY] * len(after),
         out_specs=VM,
         compiler_params=params(),
-        cost_estimate=cost(1 << 26, 1 << 21),
-    )(local, entering, c_in, decay_log)
+        cost_estimate=cost(JOIN_COST, 1 << 21),
+    )(local, entering, c_in, decay_log, *after)
 
 
 ROWS = QH * L
@@ -190,79 +197,77 @@
     return lax.dot_general(q, k, (((1,), (1,)), ((), ())), preferred_element_type=F32)
 
 
-def attend_kernel(n_sets, first, last, me_ref, q_ref, *refs):
-    refs = list(refs)
-    if first:
-        k_ref, v_ref = refs[:2]
-        refs = refs[2:]
-    else:
-        m_in, l_in, a_in = refs[:3]
-        refs = refs[3:]
+def open_kernel(q_ref, k_ref, v_ref, s_ref, m_ref, l_ref, a_ref):
+    q = stacked_queries(q_ref)
+    s_ref[...] = q
+    s = scores(q, k_ref[...])
+    t = lax.broadcasted_iota(jnp.int32, s.shape, 0) % L
+    u = lax.broadcasted_iota(jnp.int32, s.shape, 1)
+    s = jnp.where(u <= t, s, -1e30)
+    m = jnp.max(s, axis=1, keepdims=True)
+    p = jnp.exp2((s - m) * SCALE2)
+    m_ref[...] = jnp.broadcast_to(m, (ROWS, L))
+    l_ref[...] = p
+    a_ref[...] = jnp.dot(p.astype(BF16), v_ref[...], preferred_element_type=F32)
+
+
+def open_attention(q_in, k_in, v_in):
+    return pl.pallas_call(
+        open_kernel,
+        out_shape=[jax.ShapeDtypeStruct((ROWS, HD), BF16)]
+        + [jax.ShapeDtypeStruct((ROWS, L), F32)] * 3,
+        in_specs=[VM] * 3,
+        out_specs=[VM] * 4,
+        compiler_params=params(LARGE),
+        cost_estimate=cost(1 << 27, 1 << 20),
+    )(q_in, k_in, v_in)
+
+
+def attend_kernel(n_sets, last, me_ref, q_ref, m_in, l_in, a_in, *refs):
     sets, refs = refs[:n_sets], refs[n_sets:]
     if last:
-        o_ref = refs[0]
-        m_ref, l_ref, a_ref = refs[1:]
+        o_ref, m_ref, l_ref, a_ref = refs
     else:
         m_ref, l_ref, a_ref = refs
     me = me_ref[0]
-    q = stacked_queries(q_ref)
-    if first:
-        s = scores(q, k_ref[...])
-        t = lax.broadcasted_iota(jnp.int32, s.shape, 0) % L
-        u = lax.broadcasted_iota(jnp.int32, s.shape, 1)
-        s = jnp.where(u <= t, s, -1e30)
-        m = jnp.max(s, axis=1, keepdims=True)
-        p = jnp.exp2((s - m) * SCALE2)
-        m_ref[...] = jnp.broadcast_to(m, (ROWS, L))
-        l_ref[...] = p
-        a_ref[...] = jnp.dot(p.astype(BF16), v_ref[...], preferred_element_type=F32)
-    else:
-        m_ref[...] = m_in[...]
-        l_ref[...] = l_in[...]
-        a_ref[...] = a_in[...]
-    shards_in = KEYS // PIECE
+    q = q_ref[...]
+    m_ref[...] = m_in[...]
+    l_ref[...] = l_in[...]
+    a_ref[...] = a_in[...]
+    keys = NCTX * PIECE
+    shard = lax.broadcasted_iota(jnp.int32, (1, keys), 1) // PIECE
+    bias = jnp.where(shard < me, 0.0, -1e30)
     for ref in sets:
-        for at in range(ref.shape[0] // shards_in):
-            half = at % (NCTX // shards_in)
-
-            def work(ref=ref, at=at, half=half):
-                pick = slice(at * shards_in, (at + 1) * shards_in)
-                k = ref[pick, 0:PIECE, :].reshape(KEYS, HD)
-                v = ref[pick, PIECE:KV, :].reshape(KEYS, HD)
-                s = scores(q, k)
-                shard = half * shards_in + lax.broadcasted_iota(jnp.int32, (1, KEYS), 1) // PIECE
-                s = s + jnp.where(shard < me, 0.0, -1e30)
-                m, total, acc = accumulate((m_ref[:, :1], l_ref[...], a_ref[...]), s, v)
-                m_ref[...] = jnp.broadcast_to(m, (ROWS, L))
-                l_ref[...] = total
-                a_ref[...] = acc
-
-            pl.when(half * shards_in < me)(work)
+        for at in range(ref.shape[0] // NCTX):
+            pick = slice(at * NCTX, (at + 1) * NCTX)
+            k = ref[pick, 0:PIECE, :].reshape(keys, HD)
+            v = ref[pick, PIECE:KV, :].reshape(keys, HD)
+            s = scores(q, k) + bias
+            m, total, acc = accumulate((m_ref[:, :1], l_ref[...], a_ref[...]), s, v)
+            m_ref[...] = jnp.broadcast_to(m, (ROWS, L))
+            l_ref[...] = total
+            a_ref[...] = acc
     if last:
         out = a_ref[...] / jnp.sum(l_ref[...], axis=1, keepdims=True)
         for g in range(QH):
             o_ref[:, g * HD : (g + 1) * HD] = out[g * L : (g + 1) * L].astype(BF16)
 
 
-KEYS = 512
-
-
-def attend(me, q_in, before, sets, last=False):
-    carry = [jax.ShapeDtypeStruct((ROWS, L), F32)] * 3
-    first = len(before) == 2
+def attend(me, queries, carry, sets, last=False):
+    after = [jax.ShapeDtypeStruct((ROWS, L), F32)] * 3
 
     def kernel(*refs):
-        attend_kernel(len(sets), first, last, *refs)
+        attend_kernel(len(sets), last, *refs)
 
     return pl.pallas_call(
         kernel,
-        out_shape=jax.ShapeDtypeStruct((L, QH * HD), BF16) if last else carry,
-        in_specs=[SM] + [VM] * (1 + len(before) + len(sets)),
+        out_shape=jax.ShapeDtypeStruct((L, QH * HD), BF16) if last else after,
+        in_specs=[SM] + [VM] * (4 + len(sets)),
         out_specs=VM if last else [VM] * 3,
         scratch_shapes=[pltpu.VMEM((ROWS, L), F32)] * 3 if last else [],
         compiler_params=params(),
         cost_estimate=cost(1 << 28, len(sets) << 22),
-    )(me, q_in, *before, *sets)
+    )(me, queries, *carry, *sets)
 
 
 CHIPS_X = 4
@@ -283,9 +288,12 @@
 def context_parts(x_in, b_in, c_in, decay_log, q_in, k_in, v_in, expert_out):
     me = lax.axis_index("ctx").astype(jnp.int32).reshape(1)
     chunks = chunks_to_send(x_in, b_in, decay_log, k_in, v_in)
+    queries, *carry = open_attention(q_in, k_in, v_in)
     received = lax.all_to_all(chunks, "ctx", split_axis=0, concat_axis=0, tiled=True)
     blocks = expert_blocks(expert_out, chunks)
-    own, entering = take_received(received, blocks[1:])
+    local = local_part(x_in, b_in, c_in, decay_log)
+    sooner = [blocks[d] for d in (1, 7, 2, 6) if d < len(blocks)]
+    own, entering = take_received(received, [local, queries, *sooner])
     half = NCTX // 2
     right = lax.ppermute(own, "ctx", along_x(1))
     left = lax.ppermute(own, "ctx", along_x(-1))
@@ -300,12 +308,12 @@
     far_other = other_core(far)
 
     entering = lax.all_to_all(entering, "ctx", split_axis=0, concat_axis=0, tiled=True)
-    local = local_part(x_in, b_in, c_in, decay_log)
-    mamba_out = join_mamba(local, entering.reshape(MH * L, HD), c_in, decay_log)
-
-    carry = attend(me, q_in, [k_in, v_in], [own, right, left])
-    carry = attend(me, q_in, carry, [far, near_other])
-    attn_out = attend(me, q_in, carry, [far_other], last=True)
+    later = [blocks[d] for d in (3, 5, 4) if d < len(blocks)]
+    mamba_out = join_mamba(local, entering.reshape(MH * L, HD), c_in, decay_log, later)
+
+    carry = attend(me, queries, carry, [own, right, left])
+    carry = attend(me, queries, carry, [far, near_other])
+    attn_out = attend(me, queries, carry, [far_other], last=True)
     return mamba_out, attn_out, blocks
 
 
@@ -318,7 +326,7 @@
 
 
 def combine_kernel(me_ref, ids_ref, idst_ref, gates_ref, *refs):
-    rows_refs, o_ref = refs[:-1], refs[-1]
+    rows_refs, o_ref = refs[:-2], refs[-1]
     peers = len(rows_refs)
     rows = jnp.concatenate([r[...].astype(F32) for r in rows_refs], axis=0).astype(BF16)
     owned = rows.shape[0] // (peers * CAP)
@@ -352,7 +360,7 @@
         out_shape=[jax.ShapeDtypeStruct((owned * cap, width), BF16)] * peers,
         in_specs=[SM, VM, ANY],
         out_specs=[VM] * peers,
-        compiler_params=params(),
+        compiler_params=params(LARGE),
         cost_estimate=cost(1 << 20, 1 << 21),
     )(me, expert_out, after)
     blocks = [held[0]]
@@ -362,7 +370,7 @@
     return blocks
 
 
-def expert_part(expert_ids, gates, blocks):
+def expert_part(expert_ids, gates, blocks, after):
     me = lax.axis_index("grp").astype(jnp.int32).reshape(1)
     peers = len(blocks)
     rows, width = blocks[0].shape
@@ -378,18 +386,19 @@
             pl.BlockSpec((2, count), lambda i: (0, 0)),
             pl.BlockSpec((count, 2), lambda i: (0, 0)),
         ]
-        + [pl.BlockSpec((rows, block), lambda i: (0, i))] * peers,
+        + [pl.BlockSpec((rows, block), lambda i: (0, i))] * peers
+        + [ANY],
         out_specs=pl.BlockSpec((count, block), lambda i: (0, i)),
         compiler_params=params(),
         cost_estimate=cost(1 << 24, 1 << 20),
-    )(me, expert_ids, expert_ids.T, gates, *blocks)
+    )(me, expert_ids, expert_ids.T, gates, *blocks, after)
 
 
 def shards(x_in, b_in, c_in, decay_log, q_in, k_in, v_in, expert_ids, gates, expert_out):
     mamba_out, attn_out, blocks = context_parts(
         x_in, b_in, c_in, decay_log, q_in, k_in, v_in, expert_out
     )
-    moe_out = expert_part(expert_ids, gates, blocks)
+    moe_out = expert_part(expert_ids, gates, blocks, mamba_out)
     return (mamba_out, attn_out, moe_out)
 
 

time: 155 us -> 135 us (0.87)
  the two profiles are of different devices: /device:TPU:115 before, /device:TPU:1 now
where the time goes in v3:
time: 135 us; the launch traced here: 133 us
  starting transfers between devices  76.9 us (57%)
  Pallas kernels  28.9 us (21%)
  waiting for transfers between devices  18.1 us (13%)
  local copies, waits for them, and re-layouts  6.97 us (5%)
    ppermute x7, starting transfers between devices, expert_blocks(): blocks.append(lax.ppermute(held[d], 'grp', pairs))  37.4 us
    ppermute x1, waiting for transfers between devices, context_parts(): right = lax.ppermute(own, 'ctx', along_x(1))  14.7 us
    pallas_call x3, Pallas kernels, attend(): pl.pallas_call(kernel, out_shape=jax.ShapeDtypeStruct((L, QH * HD), BF16)...  11.7 us
    all_to_all x1, starting transfers between devices, context_parts(): lax.all_to_all(chunks, 'ctx', split_axis=0, concat_axis=0, tiled=True)  11.6 us
    all_to_all x1, starting transfers between devices, context_parts(): lax.all_to_all(entering, 'ctx', split_axis=0, concat_axis=0, tiled=True)  8.49 us
    ppermute x2, starting transfers between devices, other_core(): return lax.ppermute(value, 'ctx', [(i, i ^ 1) for i in range(NCTX)])  6.48 us
    unnamed x51, local copies, waits for them, and re-layouts  6.19 us
    ppermute x1, starting transfers between devices, context_parts(): lax.ppermute(left[half:], 'ctx', along_x(-1))  4.57 us
  transfers between devices with their start and end apart: 15, of which 3 were waited for; matrix products, arithmetic and copies ran while one was open for 3% of the time, Pallas kernels for 17%

profile of v3, /device:TPU:1, one launch (start us, length us, event | category | flops | bytes accessed | tf_op | source)
XLA Modules:
  0.0 133.3 jit_solution(13972181910696458667)
XLA Ops:
  0.6 2.8 %shard_map.122.after_ref = bf16[64,72,128]{2,1,0:T(8,128)(2,1)} custom-call(bf16[128,2048]{1,0:T(8,128)(2,1)} %x_ref.3, bf16[128,128]{1,0:T(8,128)(2,1)} %b_ref.3, f32[16,128]{1,0:T(8,128)} %d_ref.5, bf16[128,128]{1,0:T(8,128)(2,1)} %k_ref.3, bf16[128,128]{1,0:T(8,128)(2,1)} %v_ref.3), custom_call_target="tpu_custom_call" | custom-call | flops 67108864 | bytes 2097152 | tf_op jit(solution)/shard_map/pallas_call | solution.py:89
  3.4 11.6 %all-to-all-start = ((bf16[64,72,128]{2,1,0:T(8,128)(2,1)}), bf16[64,72,128]{2,1,0:T(8,128)(2,1)S(1)}, u32[]{:S(2)}, u32[]{:S(2)}) async-start(bf16[64,72,128]{2,1,0:T(8,128)(2,1)} %shard_map.122.after_ref), calls=%async_computation | async-start | bytes 2359296 | tf_op jit(solution)/shard_map/all_to_all | solution.py:292
  15.0 2.2 %shard_map.124 = (bf16[8,8192]{1,0:T(8,128)(2,1)}, bf16[8,8192]{1,0:T(8,128)(2,1)}, bf16[8,8192]{1,0:T(8,128)(2,1)}, bf16[8,8192]{1,0:T(8,128)(2,1)}, bf16[8,819...) custom-call(s32[1]{0:T(128)} %bitcast.me_ref, ...), custom_call_target="tpu_custom_call" | custom-call | flops 1048576 | bytes 2097152 | tf_op jit(solution)/shard_map/pallas_call | solution.py:358
  17.2 4.0 %collective-permute-start = (bf16[8,8192]{1,0:T(8,128)(2,1)}, bf16[8,8192]{1,0:T(8,128)(2,1)S(1)}, u32[]{:S(2)}, u32[]{:S(2)}) collective-permute-start(bf16[8,8192]{1,0:T(8,128)(2,1)} %get-tuple-element.24), channel_id=1, source_target_pairs={{0,1},{1,2},{2,3},{3,4},{4,5},{5,6},{6,7},{7,0},{8,9},{9,10},{10,1... | collective-permute-start | bytes 393224 | tf_op jit(solution)/shard_map/ppermute | solution.py:369
  21.2 8.6 %collective-permute-start.1 = (bf16[8,8192]{1,0:T(8,128)(2,1)}, bf16[8,8192]{1,0:T(8,128)(2,1)S(1)}, u32[]{:S(2)}, u32[]{:S(2)}) collective-permute-start(bf16[8,8192]{1,0:T(8,128)(2,1)} %get-tuple-element.25), channel_id=1, source_target_pairs={{0,7},{1,0},{2,1},{3,2},{4,3},{5,4},{6,5},{7,6},{8,15},{9,8},{10,9... | collective-permute-start | bytes 393224 | tf_op jit(solution)/shard_map/ppermute | solution.py:369
  29.8 1.9 %collective-permute-start.2 = (bf16[8,8192]{1,0:T(8,128)(2,1)}, bf16[8,8192]{1,0:T(8,128)(2,1)S(1)}, u32[]{:S(2)}, u32[]{:S(2)}) collective-permute-start(bf16[8,8192]{1,0:T(8,128)(2,1)} %get-tuple-element.26), channel_id=1, source_target_pairs={{0,2},{1,3},{2,4},{3,5},{4,6},{5,7},{6,0},{7,1},{8,10},{9,11},{10,... | collective-permute-start | bytes 393224 | tf_op jit(solution)/shard_map/ppermute | solution.py:369
  31.8 5.5 %collective-permute-start.3 = (bf16[8,8192]{1,0:T(8,128)(2,1)}, bf16[8,8192]{1,0:T(8,128)(2,1)S(1)}, u32[]{:S(2)}, u32[]{:S(2)}) collective-permute-start(bf16[8,8192]{1,0:T(8,128)(2,1)} %get-tuple-element.27), channel_id=1, source_target_pairs={{0,6},{1,7},{2,0},{3,1},{4,2},{5,3},{6,4},{7,5},{8,14},{9,15},{10,... | collective-permute-start | bytes 393224 | tf_op jit(solution)/shard_map/ppermute | solution.py:369
  37.2 2.1 %shard_map.123 = (bf16[512,128]{1,0:T(8,128)(2,1)}, f32[512,128]{1,0:T(8,128)}, f32[512,128]{1,0:T(8,128)}, f32[512,128]{1,0:T(8,128)}) custom-call(bf16[128,512]{1,0:T(8,128)(2,1)} %q_ref.1, bf16[128,128]{1,0:T(8,128)(2,1)} %k_ref.3, bf16[128,128]{1,0:T(8,128)(2,1)} %v_ref.3), custom_call_target="tpu_custom_call" | custom-call | flops 134217728 | bytes 1048576 | tf_op jit(solution)/shard_map/pallas_call | solution.py:215
  39.3 2.9 %shard_map.121.refs_0_.l_ref = f32[128,2048]{1,0:T(8,128)} custom-call(bf16[128,2048]{1,0:T(8,128)(2,1)} %x_ref.3, bf16[128,128]{1,0:T(8,128)(2,1)} %b_ref.3, bf16[128,128]{1,0:T(8,128)(2,1)} %c_ref.3, f32[16,128]{1,0:T(8,128)} %d_ref.5), custom_call_target="tpu_custom_call" | custom-call | flops 268435456 | bytes 2097152 | tf_op jit(solution)/shard_map/pallas_call | solution.py:142
  42.2 0.0 collective-permute-done.refs_2_.refs_1_
  42.2 0.0 collective-permute-done.1.refs_3_.refs_7_
  42.2 0.0 collective-permute-done.2.refs_4_.refs_2_
  42.2 1.0 collective-permute-done.3.refs_5_.refs_6_
  43.3 2.4 %all-to-all-done.s_ref = bf16[64,72,128]{2,1,0:T(8,128)(2,1)S(1)} async-done(((bf16[64,72,128]{2,1,0:T(8,128)(2,1)}), bf16[64,72,128]{2,1,0:T(8,128)(2,1)S(1)}, u32[]{:S(2)}, u32[]{:S(2)}) %all-to-all-start) | async-done | bytes 1179680 | tf_op jit(solution)/shard_map/all_to_all | solution.py:292
  45.6 1.2 copy-done
  46.9 1.0 shard_map.125
  47.9 8.5 %all-to-all-start.1 = ((bf16[64,32,128]{2,1,0:T(8,128)(2,1)}), bf16[64,32,128]{2,1,0:T(8,128)(2,1)}, u32[]{:S(2)}, u32[]{:S(2)}) async-start(bf16[64,32,128]{2,1,0:T(8,128)(2,1)} %get-tuple-element.28), calls=%async_computation.1 | async-start | bytes 1048576 | tf_op jit(solution)/shard_map/all_to_all | solution.py:310
  56.4 3.3 %collective-permute-start.7 = (bf16[64,32,128]{2,1,0:T(8,128)(2,1)S(1)}, bf16[64,32,128]{2,1,0:T(8,128)(2,1)S(1)}, u32[]{:S(2)}, u32[]{:S(2)}) collective-permute-start(bf16[64,32,128]{2,1,0:T(8,128)(2,1)S(1)} %get-tuple-element.35.refs_5_), channel_id=1, source_target_pairs={{0,16},{8,24},{16,32},{24,40},{32,48},{40,56},{48,0},{56,8},{64,80... | collective-permute-start | bytes 1572872 | tf_op jit(solution)/shard_map/ppermute | solution.py:298
  59.7 3.2 %collective-permute-start.8 = (bf16[64,32,128]{2,1,0:T(8,128)(2,1)S(1)}, bf16[64,32,128]{2,1,0:T(8,128)(2,1)S(1)}, u32[]{:S(2)}, u32[]{:S(2)}) collective-permute-start(bf16[64,32,128]{2,1,0:T(8,128)(2,1)S(1)} %get-tuple-element.35.refs_5_), channel_id=1, source_target_pairs={{0,48},{8,56},{16,0},{24,8},{32,16},{40,24},{48,32},{56,40},{64,11... | collective-permute-start | bytes 1572872 | tf_op jit(solution)/shard_map/ppermute | solution.py:299
  62.9 14.7 %collective-permute-done.7.refs_6_ = bf16[64,32,128]{2,1,0:T(8,128)(2,1)S(1)} collective-permute-done((bf16[64,32,128]{2,1,0:T(8,128)(2,1)S(1)}, bf16[64,32,128]{2,1,0:T(8,128)(2,1)S(1)}, u32[]{:S(2)}, u32[]{:S(2)}) %collective-permute-start.7) | collective-permute-done | bytes 524320 | tf_op jit(solution)/shard_map/ppermute | solution.py:298
  77.6 0.7 slice.8
  78.4 1.9 %collective-permute-start.9 = (bf16[32,32,128]{2,1,0:T(8,128)(2,1)}, bf16[32,32,128]{2,1,0:T(8,128)(2,1)}, u32[]{:S(2)}, u32[]{:S(2)}) collective-permute-start(bf16[32,32,128]{2,1,0:T(8,128)(2,1)} %slice.8), channel_id=1, source_target_pairs={{0,16},{8,24},{16,32},{24,40},{32,48},{40,56},{48,0},{56,8},{64,80... | collective-permute-start | bytes 786440 | tf_op jit(solution)/shard_map/ppermute | solution.py:302
  80.3 6.1 %collective-permute-start.4 = (bf16[8,8192]{1,0:T(8,128)(2,1)}, bf16[8,8192]{1,0:T(8,128)(2,1)}, u32[]{:S(2)}, u32[]{:S(2)}) collective-permute-start(bf16[8,8192]{1,0:T(8,128)(2,1)} %get-tuple-element.29), channel_id=1, source_target_pairs={{0,3},{1,4},{2,5},{3,6},{4,7},{5,0},{6,1},{7,2},{8,11},{9,12},{10,... | collective-permute-start | bytes 393224 | tf_op jit(solution)/shard_map/ppermute | solution.py:369
  86.4 5.0 %collective-permute-start.5 = (bf16[8,8192]{1,0:T(8,128)(2,1)}, bf16[8,8192]{1,0:T(8,128)(2,1)}, u32[]{:S(2)}, u32[]{:S(2)}) collective-permute-start(bf16[8,8192]{1,0:T(8,128)(2,1)} %get-tuple-element.30), channel_id=1, source_target_pairs={{0,5},{1,6},{2,7},{3,0},{4,1},{5,2},{6,3},{7,4},{8,13},{9,14},{10,... | collective-permute-start | bytes 393224 | tf_op jit(solution)/shard_map/ppermute | solution.py:369
  91.3 6.4 %collective-permute-start.6 = (bf16[8,8192]{1,0:T(8,128)(2,1)}, bf16[8,8192]{1,0:T(8,128)(2,1)}, u32[]{:S(2)}, u32[]{:S(2)}) collective-permute-start(bf16[8,8192]{1,0:T(8,128)(2,1)} %get-tuple-element.31), channel_id=1, source_target_pairs={{0,4},{1,5},{2,6},{3,7},{4,0},{5,1},{6,2},{7,3},{8,12},{9,13},{10,... | collective-permute-start | bytes 393224 | tf_op jit(solution)/shard_map/ppermute | solution.py:369
  97.7 0.1 copy.14.gates_ref
  97.8 0.7 copy.13.ids_ref
  98.5 0.0 collective-permute-done.8.refs_7_
  98.5 4.6 %collective-permute-start.10 = (bf16[32,32,128]{2,1,0:T(8,128)(2,1)S(1)}, bf16[32,32,128]{2,1,0:T(8,128)(2,1)S(1)}, u32[]{:S(2)}, u32[]{:S(2)}) collective-permute-start(bf16[32,32,128]{2,1,0:T(8,128)(2,1)S(1)} %slice.9), channel_id=1, source_target_pairs={{0,48},{8,56},{16,0},{24,8},{32,16},{40,24},{48,32},{56,40},{64,11... | collective-permute-start | bytes 786440 | tf_op jit(solution)/shard_map/ppermute | solution.py:303
  103.1 3.6 %shard_map.127 = (f32[512,128]{1,0:T(8,128)S(1)}, f32[512,128]{1,0:T(8,128)S(1)}, f32[512,128]{1,0:T(8,128)S(1)}) custom-call(s32[1]{0:T(128)} %bitcast.2.refs_0_, bf16[512,128]{1,0:T(8,128)(2,1)S(1)} %copy-done.2, f32[512,128]{1,0:T(8,128)S(1)} %copy-done.14, f32[512,128]{1,0:T(8,128)S(1)} %copy-done.15, f32[512,128]{1,0:T(8,128)S(1)} %copy-done.16, ...), custom_call_target="tpu_custom_call" | custom-call | flops 268435456 | bytes 12582912 | tf_op jit(solution)/shard_map/pallas_call | solution.py:262
  106.8 0.7 copy-done.8
  107.4 0.7 copy-done.10
  108.1 1.3 %pad_maximum_fusion = bf16[192,32,128]{2,1,0:T(8,128)(2,1)} fusion(bf16[64,32,128]{2,1,0:T(8,128)(2,1)S(1)} %collective-permute-done.8.refs_7_, bf16[64,32,128]{2,1,0:T(8,128)(2,1)S(1)} %collective-permute-done.7.refs_6_, bf16[64,32,128]{2,1,0:T(8,128)(2,1)S(1)} %get-tuple-element.35.refs_5_), kind=kLoop, calls=%fused_computation | loop fusion | flops 1572864 | bytes 3145728 | tf_op jit(solution)/shard_map/concatenate | solution.py:306
  109.5 4.4 %collective-permute-start.11 = (bf16[192,32,128]{2,1,0:T(8,128)(2,1)}, bf16[192,32,128]{2,1,0:T(8,128)(2,1)S(1)}, u32[]{:S(2)}, u32[]{:S(2)}) collective-permute-start(bf16[192,32,128]{2,1,0:T(8,128)(2,1)} %pad_maximum_fusion), channel_id=1, source_target_pairs={{0,8},{8,0},{16,24},{24,16},{32,40},{40,32},{48,56},{56,48},{64,72... | collective-permute-start | bytes 4718600 | tf_op jit(solution)/shard_map/ppermute | solution.py:285
  113.9 1.0 constant_dynamic-update-slice_fusion.1
  114.8 0.0 collective-permute-done.10
  114.9 2.1 %collective-permute-start.12 = (bf16[64,32,128]{2,1,0:T(8,128)(2,1)S(1)}, bf16[64,32,128]{2,1,0:T(8,128)(2,1)}, u32[]{:S(2)}, u32[]{:S(2)}) collective-permute-start(bf16[64,32,128]{2,1,0:T(8,128)(2,1)S(1)} %constant_dynamic-update-slice_fusion.refs_5_), channel_id=1, source_target_pairs={{0,8},{8,0},{16,24},{24,16},{32,40},{40,32},{48,56},{56,48},{64,72... | collective-permute-start | bytes 1572872 | tf_op jit(solution)/shard_map/ppermute | solution.py:285
  117.0 0.0 collective-permute-done.5.refs_1_.refs_5_
  117.0 0.0 collective-permute-done.6.refs_2_.refs_4_
  117.1 0.0 copy-start.20
  117.1 0.7 copy-done.20
  117.8 0.0 copy-start.22
  117.9 2.6 %shard_map.126.refs_8_ = bf16[128,2048]{1,0:T(8,128)(2,1)} custom-call(f32[128,2048]{1,0:T(8,128)S(1)} %copy-done.1, bf16[2048,128]{1,0:T(8,128)(2,1)} %bitcast.1.e_ref, bf16[128,128]{1,0:T(8,128)(2,1)S(1)} %copy-done.20, f32[16,128]{1,0:T(8,128)S(1)} %copy-done.18, bf16[8,8192]{1,0:T(8,128)(2,1)} %collective-permute-done.4.refs_0_.refs_3_, ...), custom_call_target="tpu_custom_call" | custom-call | flops 34359738368 | bytes 2097152 | tf_op jit(solution)/shard_map/pallas_call | solution.py:166
  120.5 0.0 copy-start.7
  120.5 1.0 copy-done.7
  121.5 3.7 %shard_map.130 = bf16[16,8192]{1,0:T(8,128)(2,1)} custom-call(s32[1]{0:T(128)} %bitcast.me_ref, s32[16,2]{1,0:T(8,128)S(1)} %copy-done.19, s32[2,16]{1,0:T(2,128)S(1)} %bitcast.4, f32[16,2]{1,0:T(8,128)S(1)} %copy.14.gates_ref, bf16[8,8192]{1,0:T(8,128)(2,1)S(1)} %copy-done.17, bf16[8,8192]{1,0:T(8,128)(2,1)S(1)} %collective-permute-done.refs_2_.refs_1_, ...), custom_call_target="tpu_custom_call" | custom-call | flops 16777216 | bytes 1048576 | tf_op jit(solution)/shard_map/pallas_call | solution.py:379
  125.2 5.0 %shard_map.128 = (f32[512,128]{1,0:T(8,128)S(1)}, f32[512,128]{1,0:T(8,128)S(1)}, f32[512,128]{1,0:T(8,128)S(1)}) custom-call(s32[1]{0:T(128)} %bitcast.2.refs_0_, bf16[512,128]{1,0:T(8,128)(2,1)S(1)} %copy-done.2, f32[512,128]{1,0:T(8,128)S(1)} %copy-done.9, f32[512,128]{1,0:T(8,128)S(1)} %copy-done.11, f32[512,128]{1,0:T(8,128)S(1)} %copy-done.13, ...), custom_call_target="tpu_custom_call" | custom-call | flops 268435456 | bytes 8388608 | tf_op jit(solution)/shard_map/pallas_call | solution.py:262
  130.2 3.1 %shard_map.129 = bf16[128,512]{1,0:T(8,128)(2,1)} custom-call(s32[1]{0:T(128)} %bitcast.2.refs_0_, bf16[512,128]{1,0:T(8,128)(2,1)S(1)} %copy-done.2, f32[512,128]{1,0:T(8,128)S(1)} %get-tuple-element.39.refs_2_, f32[512,128]{1,0:T(8,128)S(1)} %get-tuple-element.40.refs_3_, f32[512,128]{1,0:T(8,128)S(1)} %get-tuple-element.41.refs_4_, ...), custom_call_target="tpu_custom_call" | custom-call | flops 268435456 | bytes 4194304 | tf_op jit(solution)/shard_map/pallas_call | solution.py:262
  (47 shorter events, 0.1 us)
Async XLA Ops:
  3.4 42.2 %all-to-all-start = ((bf16[64,72,128]{2,1,0:T(8,128)(2,1)}), bf16[64,72,128]{2,1,0:T(8,128)(2,1)S(1)}, u32[]{:S(2)}, u32[]{:S(2)}) async-start(bf16[64,72,128]{2,1,0:T(8,128)(2,1)} %shard_map.122.after_ref), calls=%async_computation | async-start | bytes 2359296 | tf_op jit(solution)/shard_map/all_to_all | solution.py:292
  17.2 25.0 %collective-permute-start = (bf16[8,8192]{1,0:T(8,128)(2,1)}, bf16[8,8192]{1,0:T(8,128)(2,1)S(1)}, u32[]{:S(2)}, u32[]{:S(2)}) collective-permute-start(bf16[8,8192]{1,0:T(8,128)(2,1)} %get-tuple-element.24), channel_id=1, source_target_pairs={{0,1},{1,2},{2,3},{3,4},{4,5},{5,6},{6,7},{7,0},{8,9},{9,10},{10,1... | collective-permute-start | bytes 393224 | tf_op jit(solution)/shard_map/ppermute | solution.py:369
  21.2 21.0 %collective-permute-start.1 = (bf16[8,8192]{1,0:T(8,128)(2,1)}, bf16[8,8192]{1,0:T(8,128)(2,1)S(1)}, u32[]{:S(2)}, u32[]{:S(2)}) collective-permute-start(bf16[8,8192]{1,0:T(8,128)(2,1)} %get-tuple-element.25), channel_id=1, source_target_pairs={{0,7},{1,0},{2,1},{3,2},{4,3},{5,4},{6,5},{7,6},{8,15},{9,8},{10,9... | collective-permute-start | bytes 393224 | tf_op jit(solution)/shard_map/ppermute | solution.py:369
  29.8 12.4 %collective-permute-start.2 = (bf16[8,8192]{1,0:T(8,128)(2,1)}, bf16[8,8192]{1,0:T(8,128)(2,1)S(1)}, u32[]{:S(2)}, u32[]{:S(2)}) collective-permute-start(bf16[8,8192]{1,0:T(8,128)(2,1)} %get-tuple-element.26), channel_id=1, source_target_pairs={{0,2},{1,3},{2,4},{3,5},{4,6},{5,7},{6,0},{7,1},{8,10},{9,11},{10,... | collective-permute-start | bytes 393224 | tf_op jit(solution)/shard_map/ppermute | solution.py:369
  31.8 11.5 %collective-permute-start.3 = (bf16[8,8192]{1,0:T(8,128)(2,1)}, bf16[8,8192]{1,0:T(8,128)(2,1)S(1)}, u32[]{:S(2)}, u32[]{:S(2)}) collective-permute-start(bf16[8,8192]{1,0:T(8,128)(2,1)} %get-tuple-element.27), channel_id=1, source_target_pairs={{0,6},{1,7},{2,0},{3,1},{4,2},{5,3},{6,4},{7,5},{8,14},{9,15},{10,... | collective-permute-start | bytes 393224 | tf_op jit(solution)/shard_map/ppermute | solution.py:369
  39.3 6.3 %copy-start.2 = (bf16[512,128]{1,0:T(8,128)(2,1)S(1)}, bf16[512,128]{1,0:T(8,128)(2,1)}, u32[]{:S(2)}) copy-start(bf16[512,128]{1,0:T(8,128)(2,1)} %get-tuple-element.23.refs_1_) | copy-start | bytes 393220
  42.2 5.7 %copy-start.3 = (bf16[8,8192]{1,0:T(8,128)(2,1)}, bf16[8,8192]{1,0:T(8,128)(2,1)S(1)}, u32[]{:S(2)}) copy-start(bf16[8,8192]{1,0:T(8,128)(2,1)S(1)} %collective-permute-done.2.refs_4_.refs_2_) | copy-start | bytes 393220
  43.2 4.7 %copy-start.5 = (bf16[8,8192]{1,0:T(8,128)(2,1)}, bf16[8,8192]{1,0:T(8,128)(2,1)S(1)}, u32[]{:S(2)}) copy-start(bf16[8,8192]{1,0:T(8,128)(2,1)S(1)} %collective-permute-done.3.refs_5_.refs_6_) | copy-start | bytes 393220
  45.6 1.2 copy-start
  46.9 50.9 %copy-start.23 = (f32[16,2]{0,1:T(2,128)S(1)}, f32[16,2]{0,1:T(2,128)}, u32[]{:S(2)}) copy-start(f32[16,2]{0,1:T(2,128)} %param.18) | copy-start | bytes 388
  46.9 50.9 %copy-start.21 = (s32[16,2]{0,1:T(2,128)S(1)}, s32[16,2]{0,1:T(2,128)}, u32[]{:S(2)}) copy-start(s32[16,2]{0,1:T(2,128)} %param.17) | copy-start | bytes 388
  47.9 55.2 %copy-start.14 = (f32[512,128]{1,0:T(8,128)S(1)}, f32[512,128]{1,0:T(8,128)}, u32[]{:S(2)}) copy-start(f32[512,128]{1,0:T(8,128)} %get-tuple-element.32.refs_2_) | copy-start | bytes 786436
  47.9 55.2 %copy-start.15 = (f32[512,128]{1,0:T(8,128)S(1)}, f32[512,128]{1,0:T(8,128)}, u32[]{:S(2)}) copy-start(f32[512,128]{1,0:T(8,128)} %get-tuple-element.33.refs_3_) | copy-start | bytes 786436
  47.9 55.2 %copy-start.16 = (f32[512,128]{1,0:T(8,128)S(1)}, f32[512,128]{1,0:T(8,128)}, u32[]{:S(2)}) copy-start(f32[512,128]{1,0:T(8,128)} %get-tuple-element.34.refs_4_) | copy-start | bytes 786436
  47.9 69.1 %all-to-all-start.1 = ((bf16[64,32,128]{2,1,0:T(8,128)(2,1)}), bf16[64,32,128]{2,1,0:T(8,128)(2,1)}, u32[]{:S(2)}, u32[]{:S(2)}) async-start(bf16[64,32,128]{2,1,0:T(8,128)(2,1)} %get-tuple-element.28), calls=%async_computation.1 | async-start | bytes 1048576 | tf_op jit(solution)/shard_map/all_to_all | solution.py:310
  56.4 21.2 %collective-permute-start.7 = (bf16[64,32,128]{2,1,0:T(8,128)(2,1)S(1)}, bf16[64,32,128]{2,1,0:T(8,128)(2,1)S(1)}, u32[]{:S(2)}, u32[]{:S(2)}) collective-permute-start(bf16[64,32,128]{2,1,0:T(8,128)(2,1)S(1)} %get-tuple-element.35.refs_5_), channel_id=1, source_target_pairs={{0,16},{8,24},{16,32},{24,40},{32,48},{40,56},{48,0},{56,8},{64,80... | collective-permute-start | bytes 1572872 | tf_op jit(solution)/shard_map/ppermute | solution.py:298
  59.7 38.8 %collective-permute-start.8 = (bf16[64,32,128]{2,1,0:T(8,128)(2,1)S(1)}, bf16[64,32,128]{2,1,0:T(8,128)(2,1)S(1)}, u32[]{:S(2)}, u32[]{:S(2)}) collective-permute-start(bf16[64,32,128]{2,1,0:T(8,128)(2,1)S(1)} %get-tuple-element.35.refs_5_), channel_id=1, source_target_pairs={{0,48},{8,56},{16,0},{24,8},{32,16},{40,24},{48,32},{56,40},{64,11... | collective-permute-start | bytes 1572872 | tf_op jit(solution)/shard_map/ppermute | solution.py:299
  78.4 31.1 %collective-permute-start.9 = (bf16[32,32,128]{2,1,0:T(8,128)(2,1)}, bf16[32,32,128]{2,1,0:T(8,128)(2,1)}, u32[]{:S(2)}, u32[]{:S(2)}) collective-permute-start(bf16[32,32,128]{2,1,0:T(8,128)(2,1)} %slice.8), channel_id=1, source_target_pairs={{0,16},{8,24},{16,32},{24,40},{32,48},{40,56},{48,0},{56,8},{64,80... | collective-permute-start | bytes 786440 | tf_op jit(solution)/shard_map/ppermute | solution.py:302
  80.3 36.7 %collective-permute-start.4 = (bf16[8,8192]{1,0:T(8,128)(2,1)}, bf16[8,8192]{1,0:T(8,128)(2,1)}, u32[]{:S(2)}, u32[]{:S(2)}) collective-permute-start(bf16[8,8192]{1,0:T(8,128)(2,1)} %get-tuple-element.29), channel_id=1, source_target_pairs={{0,3},{1,4},{2,5},{3,6},{4,7},{5,0},{6,1},{7,2},{8,11},{9,12},{10,... | collective-permute-start | bytes 393224 | tf_op jit(solution)/shard_map/ppermute | solution.py:369
  86.4 30.6 %collective-permute-start.5 = (bf16[8,8192]{1,0:T(8,128)(2,1)}, bf16[8,8192]{1,0:T(8,128)(2,1)}, u32[]{:S(2)}, u32[]{:S(2)}) collective-permute-start(bf16[8,8192]{1,0:T(8,128)(2,1)} %get-tuple-element.30), channel_id=1, source_target_pairs={{0,5},{1,6},{2,7},{3,0},{4,1},{5,2},{6,3},{7,4},{8,13},{9,14},{10,... | collective-permute-start | bytes 393224 | tf_op jit(solution)/shard_map/ppermute | solution.py:369
  91.3 25.7 %collective-permute-start.6 = (bf16[8,8192]{1,0:T(8,128)(2,1)}, bf16[8,8192]{1,0:T(8,128)(2,1)}, u32[]{:S(2)}, u32[]{:S(2)}) collective-permute-start(bf16[8,8192]{1,0:T(8,128)(2,1)} %get-tuple-element.31), channel_id=1, source_target_pairs={{0,4},{1,5},{2,6},{3,7},{4,0},{5,1},{6,2},{7,3},{8,12},{9,13},{10,... | collective-permute-start | bytes 393224 | tf_op jit(solution)/shard_map/ppermute | solution.py:369
  98.5 16.3 %collective-permute-start.10 = (bf16[32,32,128]{2,1,0:T(8,128)(2,1)S(1)}, bf16[32,32,128]{2,1,0:T(8,128)(2,1)S(1)}, u32[]{:S(2)}, u32[]{:S(2)}) collective-permute-start(bf16[32,32,128]{2,1,0:T(8,128)(2,1)S(1)} %slice.9), channel_id=1, source_target_pairs={{0,48},{8,56},{16,0},{24,8},{32,16},{40,24},{48,32},{56,40},{64,11... | collective-permute-start | bytes 786440 | tf_op jit(solution)/shard_map/ppermute | solution.py:303
  106.7 0.7 copy-start.8
  107.4 0.7 copy-start.10
  108.1 1.4 %copy-start.12 = (f32[512,128]{1,0:T(8,128)}, f32[512,128]{1,0:T(8,128)S(1)}, u32[]{:S(2)}) copy-start(f32[512,128]{1,0:T(8,128)S(1)} %get-tuple-element.38.refs_4_) | copy-start | bytes 786436
  108.1 8.9 %copy-start.1 = (f32[128,2048]{1,0:T(8,128)S(1)}, f32[128,2048]{1,0:T(8,128)}, u32[]{:S(2)}) copy-start(f32[128,2048]{1,0:T(8,128)} %shard_map.121.refs_0_.l_ref) | copy-start | bytes 3145732
  108.1 8.9 %copy-start.18 = (f32[16,128]{1,0:T(8,128)S(1)}, f32[16,128]{1,0:T(8,128)}, u32[]{:S(2)}) copy-start(f32[16,128]{1,0:T(8,128)} %d_ref.5) | copy-start | bytes 24580
  109.5 15.7 %collective-permute-start.11 = (bf16[192,32,128]{2,1,0:T(8,128)(2,1)}, bf16[192,32,128]{2,1,0:T(8,128)(2,1)S(1)}, u32[]{:S(2)}, u32[]{:S(2)}) collective-permute-start(bf16[192,32,128]{2,1,0:T(8,128)(2,1)} %pad_maximum_fusion), channel_id=1, source_target_pairs={{0,8},{8,0},{16,24},{24,16},{32,40},{40,32},{48,56},{56,48},{64,72... | collective-permute-start | bytes 4718600 | tf_op jit(solution)/shard_map/ppermute | solution.py:285
  114.9 15.3 %collective-permute-start.12 = (bf16[64,32,128]{2,1,0:T(8,128)(2,1)S(1)}, bf16[64,32,128]{2,1,0:T(8,128)(2,1)}, u32[]{:S(2)}, u32[]{:S(2)}) collective-permute-start(bf16[64,32,128]{2,1,0:T(8,128)(2,1)S(1)} %constant_dynamic-update-slice_fusion.refs_5_), channel_id=1, source_target_pairs={{0,8},{8,0},{16,24},{24,16},{32,40},{40,32},{48,56},{56,48},{64,72... | collective-permute-start | bytes 1572872 | tf_op jit(solution)/shard_map/ppermute | solution.py:285
  117.1 0.8 copy-start.20
  117.8 2.6 %copy-start.4 = (bf16[8,8192]{1,0:T(8,128)(2,1)S(1)}, bf16[8,8192]{1,0:T(8,128)(2,1)}, u32[]{:S(2)}) copy-start(bf16[8,8192]{1,0:T(8,128)(2,1)} %copy-done.3) | copy-start | bytes 393220
  117.8 2.6 %copy-start.6 = (bf16[8,8192]{1,0:T(8,128)(2,1)S(1)}, bf16[8,8192]{1,0:T(8,128)(2,1)}, u32[]{:S(2)}) copy-start(bf16[8,8192]{1,0:T(8,128)(2,1)} %copy-done.5) | copy-start | bytes 393220
  117.8 2.6 %copy-start.17 = (bf16[8,8192]{1,0:T(8,128)(2,1)S(1)}, bf16[8,8192]{1,0:T(8,128)(2,1)}, u32[]{:S(2)}) copy-start(bf16[8,8192]{1,0:T(8,128)(2,1)} %get-tuple-element.42.refs_0_) | copy-start | bytes 393220
  117.8 2.6 %copy-start.19 = (s32[16,2]{1,0:T(8,128)S(1)}, s32[16,2]{1,0:T(8,128)}, u32[]{:S(2)}) copy-start(s32[16,2]{1,0:T(8,128)} %copy.13.ids_ref) | copy-start | bytes 388
  117.8 2.6 %copy-start.22 = (s32[16,2]{0,1:T(2,128)S(1)}, s32[16,2]{0,1:T(2,128)}, u32[]{:S(2)}) copy-start(s32[16,2]{0,1:T(2,128)} %param.17) | copy-start | bytes 388
  117.9 7.4 %copy-start.9 = (f32[512,128]{1,0:T(8,128)S(1)}, f32[512,128]{1,0:T(8,128)}, u32[]{:S(2)}) copy-start(f32[512,128]{1,0:T(8,128)} %copy-done.8) | copy-start | bytes 786436
  117.9 7.4 %copy-start.11 = (f32[512,128]{1,0:T(8,128)S(1)}, f32[512,128]{1,0:T(8,128)}, u32[]{:S(2)}) copy-start(f32[512,128]{1,0:T(8,128)} %copy-done.10) | copy-start | bytes 786436
  117.9 7.4 %copy-start.13 = (f32[512,128]{1,0:T(8,128)S(1)}, f32[512,128]{1,0:T(8,128)}, u32[]{:S(2)}) copy-start(f32[512,128]{1,0:T(8,128)} %copy-done.12) | copy-start | bytes 786436
  120.5 1.0 copy-start.7

commit v4 on v3

--- a/solution.py
+++ b/solution.py
@@ -21,7 +21,7 @@
 ANY = pl.BlockSpec(memory_space=pl.ANY)
 
 
-LARGE, SMALL = 60, 16
+LARGE, SMALL = 60, 24
 
 
 def params(mib=SMALL):
@@ -57,7 +57,7 @@
 PIECE = 16
 KV = 2 * PIECE
 SL = 32
-CHUNK = KV + SL + 8
+CHUNK = 2 * KV + SL + 8
 
 
 def send_kernel(x_ref, b_ref, d_ref, k_ref, v_ref, o_ref):
@@ -77,10 +77,11 @@
         terms = jnp.where(row == 0, hi, jnp.where(row == 1, mid, jnp.where(row == 2, lo, 0.0)))
         for q in range(4):
             j = h * 4 + q
-            rows = slice((j % pieces) * PIECE, (j % pieces + 1) * PIECE)
-            o_ref[j, 0:PIECE, :] = k_ref[rows, :]
-            o_ref[j, PIECE:KV, :] = v_ref[rows, :]
-            o_ref[j, KV:CHUNK, :] = jnp.concatenate(
+            for turn in range(2):
+                at = (j + turn * pieces // 2) % pieces * PIECE
+                o_ref[j, turn * KV : turn * KV + PIECE, :] = k_ref[at : at + PIECE, :]
+                o_ref[j, turn * KV + PIECE : (turn + 1) * KV, :] = v_ref[at : at + PIECE, :]
+            o_ref[j, 2 * KV : CHUNK, :] = jnp.concatenate(
                 [s[q * SL : (q + 1) * SL], terms], axis=0
             ).astype(BF16)
 
@@ -97,12 +98,13 @@
 
 
 def take_kernel(s_ref, *refs):
-    own_ref, o_ref = refs[-2:]
+    own_ref, opposite_ref, o_ref = refs[-3:]
     own_ref[...] = s_ref[:, :KV, :]
+    opposite_ref[...] = s_ref[:, KV : 2 * KV, :]
 
     def step(k, e):
         o_ref[k] = e.astype(BF16)
-        block = s_ref[k, KV:CHUNK, :].astype(F32)
+        block = s_ref[k, 2 * KV : CHUNK, :].astype(F32)
         d = block[SL : SL + 1] + block[SL + 1 : SL + 2] + block[SL + 2 : SL + 3]
         return d * e + block[:SL]
 
@@ -113,11 +115,12 @@
     return pl.pallas_call(
         take_kernel,
         out_shape=[
+            jax.ShapeDtypeStruct((NCTX, KV, HD), BF16),
             jax.ShapeDtypeStruct((NCTX, KV, HD), BF16),
             jax.ShapeDtypeStruct((NCTX, SL, HD), BF16),
         ],
         in_specs=[VM] + [ANY] * len(after),
-        out_specs=[VM, VM],
+        out_specs=[VM] * 3,
         compiler_params=params(),
         cost_estimate=cost(1 << 20, 1 << 21),
     )(received, *after)
@@ -152,8 +155,7 @@
 JOIN_COST = 1 << 35
 
 
-def join_kernel(l_ref, e_ref, c_ref, d_ref, *refs):
-    o_ref = refs[-1]
+def join_kernel(l_ref, e_ref, c_ref, d_ref, o_ref):
     grow = jnp.exp(col_cumulative(d_ref[...]))
     c = c_ref[...]
     for h in range(MH):
@@ -162,15 +164,15 @@
         o_ref[:, cols] = (l_ref[:, cols] + grow[:, h : h + 1] * readout).astype(BF16)
 
 
-def join_mamba(local, entering, c_in, decay_log, after):
+def join_mamba(local, entering, c_in, decay_log):
     return pl.pallas_call(
         join_kernel,
         out_shape=jax.ShapeDtypeStruct((L, MH * HD), BF16),
-        in_specs=[VM] * 4 + [ANY] * len(after),
+        in_specs=[VM] * 4,
         out_specs=VM,
         compiler_params=params(),
         cost_estimate=cost(JOIN_COST, 1 << 21),
-    )(local, entering, c_in, decay_log, *after)
+    )(local, entering, c_in, decay_log)
 
 
 ROWS = QH * L
@@ -197,9 +199,10 @@
     return lax.dot_general(q, k, (((1,), (1,)), ((), ())), preferred_element_type=F32)
 
 
-def open_kernel(q_ref, k_ref, v_ref, s_ref, m_ref, l_ref, a_ref):
+def open_kernel(q_ref, q2_ref, k_ref, v_ref, s_ref, s2_ref, m_ref, l_ref, a_ref):
     q = stacked_queries(q_ref)
     s_ref[...] = q
+    s2_ref[...] = stacked_queries(q2_ref)
     s = scores(q, k_ref[...])
     t = lax.broadcasted_iota(jnp.int32, s.shape, 0) % L
     u = lax.broadcasted_iota(jnp.int32, s.shape, 1)
@@ -211,63 +214,95 @@
     a_ref[...] = jnp.dot(p.astype(BF16), v_ref[...], preferred_element_type=F32)
 
 
-def open_attention(q_in, k_in, v_in):
+PART = jax.ShapeDtypeStruct((ROWS, L), F32)
+
+
+def open_attention(q_in, q_other, k_in, v_in):
     return pl.pallas_call(
         open_kernel,
-        out_shape=[jax.ShapeDtypeStruct((ROWS, HD), BF16)]
-        + [jax.ShapeDtypeStruct((ROWS, L), F32)] * 3,
-        in_specs=[VM] * 3,
-        out_specs=[VM] * 4,
+        out_shape=[jax.ShapeDtypeStruct((ROWS, HD), BF16)] * 2 + [PART] * 3,
+        in_specs=[VM] * 4,
+        out_specs=[VM] * 5,
         compiler_params=params(LARGE),
         cost_estimate=cost(1 << 27, 1 << 20),
-    )(q_in, k_in, v_in)
-
-
-def attend_kernel(n_sets, last, me_ref, q_ref, m_in, l_in, a_in, *refs):
+    )(q_in, q_other, k_in, v_in)
+
+
+def attend_kernel(n_sets, fresh, pack, other, me_ref, q_ref, *refs):
+    if not fresh:
+        m_in, l_in, a_in = refs[:3]
+        refs = refs[3:]
     sets, refs = refs[:n_sets], refs[n_sets:]
-    if last:
+    if pack:
         o_ref, m_ref, l_ref, a_ref = refs
     else:
         m_ref, l_ref, a_ref = refs
-    me = me_ref[0]
+    me = (me_ref[0] ^ 1) if other else me_ref[0]
     q = q_ref[...]
-    m_ref[...] = m_in[...]
-    l_ref[...] = l_in[...]
-    a_ref[...] = a_in[...]
+    if fresh:
+        m_ref[...] = jnp.full((ROWS, L), -1e30, F32)
+        l_ref[...] = jnp.zeros((ROWS, L), F32)
+        a_ref[...] = jnp.zeros((ROWS, HD), F32)
+    else:
+        m_ref[...] = m_in[...]
+        l_ref[...] = l_in[...]
+        a_ref[...] = a_in[...]
     keys = NCTX * PIECE
     shard = lax.broadcasted_iota(jnp.int32, (1, keys), 1) // PIECE
     bias = jnp.where(shard < me, 0.0, -1e30)
-    for ref in sets:
-        for at in range(ref.shape[0] // NCTX):
-            pick = slice(at * NCTX, (at + 1) * NCTX)
-            k = ref[pick, 0:PIECE, :].reshape(keys, HD)
-            v = ref[pick, PIECE:KV, :].reshape(keys, HD)
+
+    @pl.when(me > 0)
+    def _():
+        for ref in sets:
+            k = ref[:, 0:PIECE, :].reshape(keys, HD)
+            v = ref[:, PIECE:KV, :].reshape(keys, HD)
             s = scores(q, k) + bias
             m, total, acc = accumulate((m_ref[:, :1], l_ref[...], a_ref[...]), s, v)
             m_ref[...] = jnp.broadcast_to(m, (ROWS, L))
             l_ref[...] = total
             a_ref[...] = acc
-    if last:
-        out = a_ref[...] / jnp.sum(l_ref[...], axis=1, keepdims=True)
-        for g in range(QH):
-            o_ref[:, g * HD : (g + 1) * HD] = out[g * L : (g + 1) * L].astype(BF16)
-
-
-def attend(me, queries, carry, sets, last=False):
-    after = [jax.ShapeDtypeStruct((ROWS, L), F32)] * 3
-
+
+    if pack:
+        lane = lax.broadcasted_iota(jnp.int32, (ROWS, L), 1)
+        total = jnp.sum(l_ref[...], axis=1, keepdims=True)
+        o_ref[:, :HD] = a_ref[...]
+        o_ref[:, HD:] = jnp.where(lane < L // 2, m_ref[...], total)
+
+
+def attend(me, queries, carry, sets, other=False, pack=False):
     def kernel(*refs):
-        attend_kernel(len(sets), last, *refs)
+        attend_kernel(len(sets), not carry, pack, other, *refs)
 
     return pl.pallas_call(
         kernel,
-        out_shape=jax.ShapeDtypeStruct((L, QH * HD), BF16) if last else after,
-        in_specs=[SM] + [VM] * (4 + len(sets)),
-        out_specs=VM if last else [VM] * 3,
-        scratch_shapes=[pltpu.VMEM((ROWS, L), F32)] * 3 if last else [],
+        out_shape=jax.ShapeDtypeStruct((ROWS, HD + L), F32) if pack else [PART] * 3,
+        in_specs=[SM] + [VM] * (1 + len(carry) + len(sets)),
+        out_specs=VM if pack else [VM] * 3,
+        scratch_shapes=[pltpu.VMEM((ROWS, L), F32)] * 3 if pack else [],
         compiler_params=params(),
-        cost_estimate=cost(1 << 28, len(sets) << 22),
+        cost_estimate=cost(1 << 28, len(sets) << 20),
     )(me, queries, *carry, *sets)
+
+
+def merge_kernel(m_ref, l_ref, a_ref, p_ref, o_ref):
+    m1, m2 = m_ref[:, :1], p_ref[:, HD : HD + 1]
+    m = jnp.maximum(m1, m2)
+    f1, f2 = jnp.exp2((m1 - m) * SCALE2), jnp.exp2((m2 - m) * SCALE2)
+    total = jnp.sum(l_ref[...], axis=1, keepdims=True) * f1 + p_ref[:, HD + L - 1 :] * f2
+    out = (a_ref[...] * f1 + p_ref[:, :HD] * f2) / total
+    for g in range(QH):
+        o_ref[:, g * HD : (g + 1) * HD] = out[g * L : (g + 1) * L].astype(BF16)
+
+
+def merge_attention(carry, part):
+    return pl.pallas_call(
+        merge_kernel,
+        out_shape=jax.ShapeDtypeStruct((L, QH * HD), BF16),
+        in_specs=[VM] * 4,
+        out_specs=VM,
+        compiler_params=params(),
+        cost_estimate=cost(1 << 20, 1 << 20),
+    )(*carry, part)
 
 
 CHIPS_X = 4
@@ -288,33 +323,24 @@
 def context_parts(x_in, b_in, c_in, decay_log, q_in, k_in, v_in, expert_out):
     me = lax.axis_index("ctx").astype(jnp.int32).reshape(1)
     chunks = chunks_to_send(x_in, b_in, decay_log, k_in, v_in)
-    queries, *carry = open_attention(q_in, k_in, v_in)
     received = lax.all_to_all(chunks, "ctx", split_axis=0, concat_axis=0, tiled=True)
     blocks = expert_blocks(expert_out, chunks)
+    q_other = other_core(q_in)
+    q_own, q_other, *carry = open_attention(q_in, q_other, k_in, v_in)
     local = local_part(x_in, b_in, c_in, decay_log)
-    sooner = [blocks[d] for d in (1, 7, 2, 6) if d < len(blocks)]
-    own, entering = take_received(received, [local, queries, *sooner])
-    half = NCTX // 2
+    own, opposite, entering = take_received(received, [local, q_own, *blocks[1:]])
     right = lax.ppermute(own, "ctx", along_x(1))
     left = lax.ppermute(own, "ctx", along_x(-1))
-    far = jnp.concatenate(
-        [
-            lax.ppermute(right[:half], "ctx", along_x(1)),
-            lax.ppermute(left[half:], "ctx", along_x(-1)),
-        ]
-    )
-    near = jnp.concatenate([own, right, left])
-    near_other = other_core(near)
-    far_other = other_core(far)
 
     entering = lax.all_to_all(entering, "ctx", split_axis=0, concat_axis=0, tiled=True)
-    later = [blocks[d] for d in (3, 5, 4) if d < len(blocks)]
-    mamba_out = join_mamba(local, entering.reshape(MH * L, HD), c_in, decay_log, later)
-
-    carry = attend(me, queries, carry, [own, right, left])
-    carry = attend(me, queries, carry, [far, near_other])
-    attn_out = attend(me, queries, carry, [far_other], last=True)
-    return mamba_out, attn_out, blocks
+    mamba_out = join_mamba(local, entering.reshape(MH * L, HD), c_in, decay_log)
+
+    carry = attend(me, q_own, carry, [own, opposite])
+    carry_other = attend(me, q_other, [], [own, opposite], other=True)
+    part = attend(me, q_other, carry_other, [right, left], other=True, pack=True)
+    part = other_core(part)
+    carry = attend(me, q_own, carry, [right, left])
+    return mamba_out, merge_attention(carry, part), blocks
 
 
 def blocks_kernel(me_ref, e_ref, after_ref, *outs):
@@ -326,7 +352,7 @@
 
 
 def combine_kernel(me_ref, ids_ref, idst_ref, gates_ref, *refs):
-    rows_refs, o_ref = refs[:-2], refs[-1]
+    rows_refs, o_ref = refs[:-1], refs[-1]
     peers = len(rows_refs)
     rows = jnp.concatenate([r[...].astype(F32) for r in rows_refs], axis=0).astype(BF16)
     owned = rows.shape[0] // (peers * CAP)
@@ -363,14 +389,14 @@
         compiler_params=params(LARGE),
         cost_estimate=cost(1 << 20, 1 << 21),
     )(me, expert_out, after)
-    blocks = [held[0]]
-    for d in range(1, peers):
+    blocks = list(held)
+    for d in sorted(range(1, peers), key=lambda d: -min(d, peers - d)):
         pairs = [(i, (i + d) % peers) for i in range(peers)]
-        blocks.append(lax.ppermute(held[d], "grp", pairs))
+        blocks[d] = lax.ppermute(held[d], "grp", pairs)
     return blocks
 
 
-def expert_part(expert_ids, gates, blocks, after):
+def expert_part(expert_ids, gates, blocks):
     me = lax.axis_index("grp").astype(jnp.int32).reshape(1)
     peers = len(blocks)
     rows, width = blocks[0].shape
@@ -386,19 +412,18 @@
             pl.BlockSpec((2, count), lambda i: (0, 0)),
             pl.BlockSpec((count, 2), lambda i: (0, 0)),
         ]
-        + [pl.BlockSpec((rows, block), lambda i: (0, i))] * peers
-        + [ANY],
+        + [pl.BlockSpec((rows, block), lambda i: (0, i))] * peers,
         out_specs=pl.BlockSpec((count, block), lambda i: (0, i)),
         compiler_params=params(),
         cost_estimate=cost(1 << 24, 1 << 20),
-    )(me, expert_ids, expert_ids.T, gates, *blocks, after)
+    )(me, expert_ids, expert_ids.T, gates, *blocks)
 
 
 def shards(x_in, b_in, c_in, decay_log, q_in, k_in, v_in, expert_ids, gates, expert_out):
     mamba_out, attn_out, blocks = context_parts(
         x_in, b_in, c_in, decay_log, q_in, k_in, v_in, expert_out
     )
-    moe_out = expert_part(expert_ids, gates, blocks, mamba_out)
+    moe_out = expert_part(expert_ids, gates, blocks)
     return (mamba_out, attn_out, moe_out)
 
 

time: 135 us -> 118 us (0.87)
  starting transfers between devices: 76.9 us -> 69.3 us
  waiting for transfers between devices: 18.1 us -> 10.9 us
  local copies, waits for them, and re-layouts: 6.97 us -> 13 us
  Pallas kernels: 28.9 us -> 23.3 us
    ppermute x9 -> x7, starting transfers between devices: 43.9 us -> 31.6 us  [expert_blocks(): blocks[d] = lax.ppermute(held[d], 'grp', pairs)]
    ppermute x1, waiting for transfers between devices: 14.7 us -> 2.95 us  [context_parts(): right = lax.ppermute(own, 'ctx', along_x(1))]
    unnamed x51 -> x66, local copies, waits for them, and re-layouts: 6.19 us -> 13 us
    ppermute x9 -> x7, waiting for transfers between devices: 1.02 us -> 7.65 us  [expert_blocks(): blocks[d] = lax.ppermute(held[d], 'grp', pairs)]
    pallas_call x3 -> x5, Pallas kernels: 11.7 us -> 6.81 us  [the longest x4 5.67 us: attend(): pl.pallas_call(kernel, out_shape=jax.ShapeDtypeStruct((ROWS, HD + L), F32...]
    all_to_all x1, starting transfers between devices: 8.49 us -> 11.1 us  [context_parts(): lax.all_to_all(entering, 'ctx', split_axis=0, concat_axis=0, tiled=True)]
    all_to_all x1, waiting for transfers between devices: 2.38 us -> 0.01 us  [context_parts(): lax.all_to_all(chunks, 'ctx', split_axis=0, concat_axis=0, tiled=True)]
    ppermute x2, starting transfers between devices: 6.48 us -> 8.51 us  [other_core(): return lax.ppermute(value, 'ctx', [(i, i ^ 1) for i in range(NCTX)])]
  transfers between devices with their start and end apart: 15 -> 13, of which waited for: 3 -> 4; matrix products, arithmetic and copies ran while one was open for 3% -> 0% of each run, Pallas kernels for 17% -> 15%
where the time goes in v4:
time: 118 us
  starting transfers between devices  69.3 us (59%)
  Pallas kernels  23.3 us (20%)
  local copies, waits for them, and re-layouts  13 us (11%)
  waiting for transfers between devices  10.9 us (9%)
    ppermute x7, starting transfers between devices, expert_blocks(): blocks[d] = lax.ppermute(held[d], 'grp', pairs)  31.6 us
    unnamed x66, local copies, waits for them, and re-layouts  13 us
    all_to_all x1, starting transfers between devices, context_parts(): lax.all_to_all(chunks, 'ctx', split_axis=0, concat_axis=0, tiled=True)  11.6 us
    all_to_all x1, starting transfers between devices, context_parts(): lax.all_to_all(entering, 'ctx', split_axis=0, concat_axis=0, tiled=True)  11.1 us
    ppermute x2, starting transfers between devices, other_core(): return lax.ppermute(value, 'ctx', [(i, i ^ 1) for i in range(NCTX)])  8.51 us
    ppermute x7, waiting for transfers between devices, expert_blocks(): blocks[d] = lax.ppermute(held[d], 'grp', pairs)  7.65 us
    pallas_call x4, Pallas kernels, attend(): pl.pallas_call(kernel, out_shape=jax.ShapeDtypeStruct((ROWS, HD + L), F32...  5.67 us
    ppermute x1, starting transfers between devices, context_parts(): right = lax.ppermute(own, 'ctx', along_x(1))  3.29 us
  transfers between devices with their start and end apart: 13, of which 4 were waited for; matrix products, arithmetic and copies ran while one was open for 0% of the time, Pallas kernels for 15%

profile of v4, /device:TPU:1, one launch (start us, length us, event | category | flops | bytes accessed | tf_op | source)
XLA Modules:
  0.0 117.5 jit_solution(6602963118652557045)
XLA Ops:
  0.6 3.0 %shard_map.122.after_ref = bf16[64,104,128]{2,1,0:T(8,128)(2,1)} custom-call(bf16[128,2048]{1,0:T(8,128)(2,1)} %x_ref.3, bf16[128,128]{1,0:T(8,128)(2,1)} %b_ref.3, f32[16,128]{1,0:T(8,128)} %d_ref.5, bf16[128,128]{1,0:T(8,128)(2,1)} %k_ref.3, bf16[128,128]{1,0:T(8,128)(2,1)} %v_ref.3), custom_call_target="tpu_custom_call" | custom-call | flops 67108864 | bytes 2097152 | tf_op jit(solution)/shard_map/pallas_call | solution.py:90
  3.7 11.6 %all-to-all-start = ((bf16[64,104,128]{2,1,0:T(8,128)(2,1)}), bf16[64,104,128]{2,1,0:T(8,128)(2,1)S(1)}, u32[]{:S(2)}, u32[]{:S(2)}) async-start(bf16[64,104,128]{2,1,0:T(8,128)(2,1)} %shard_map.122.after_ref), calls=%async_computation | async-start | bytes 3407872 | tf_op jit(solution)/shard_map/all_to_all | solution.py:326
  15.3 0.0 copy-start.30
  15.3 2.3 %shard_map.124 = (bf16[8,8192]{1,0:T(8,128)(2,1)}, bf16[8,8192]{1,0:T(8,128)(2,1)}, bf16[8,8192]{1,0:T(8,128)(2,1)}, bf16[8,8192]{1,0:T(8,128)(2,1)}, bf16[8,819...) custom-call(s32[1]{0:T(128)} %bitcast.me_ref, ...), custom_call_target="tpu_custom_call" | custom-call | flops 1048576 | bytes 2097152 | tf_op jit(solution)/shard_map/pallas_call | solution.py:384
  17.6 4.0 %collective-permute-start.1 = (bf16[8,8192]{1,0:T(8,128)(2,1)}, bf16[8,8192]{1,0:T(8,128)(2,1)S(1)}, u32[]{:S(2)}, u32[]{:S(2)}) collective-permute-start(bf16[8,8192]{1,0:T(8,128)(2,1)} %get-tuple-element.29), channel_id=1, source_target_pairs={{0,1},{1,2},{2,3},{3,4},{4,5},{5,6},{6,7},{7,0},{8,9},{9,10},{10,1... | collective-permute-start | bytes 393224 | tf_op jit(solution)/shard_map/ppermute | solution.py:395
  21.6 5.8 %collective-permute-start.2 = (bf16[8,8192]{1,0:T(8,128)(2,1)}, bf16[8,8192]{1,0:T(8,128)(2,1)S(1)}, u32[]{:S(2)}, u32[]{:S(2)}) collective-permute-start(bf16[8,8192]{1,0:T(8,128)(2,1)} %get-tuple-element.30), channel_id=1, source_target_pairs={{0,2},{1,3},{2,4},{3,5},{4,6},{5,7},{6,0},{7,1},{8,10},{9,11},{10,... | collective-permute-start | bytes 393224 | tf_op jit(solution)/shard_map/ppermute | solution.py:395
  27.4 2.9 %collective-permute-start = (bf16[128,512]{1,0:T(8,128)(2,1)S(1)}, bf16[128,512]{1,0:T(8,128)(2,1)S(1)}, u32[]{:S(2)}, u32[]{:S(2)}) collective-permute-start(bf16[128,512]{1,0:T(8,128)(2,1)S(1)} %copy-done.30), channel_id=1, source_target_pairs={{0,8},{8,0},{16,24},{24,16},{32,40},{40,32},{48,56},{56,48},{64,72... | collective-permute-start | bytes 393224 | tf_op jit(solution)/shard_map/ppermute | solution.py:320
  30.3 7.0 %collective-permute-start.3 = (bf16[8,8192]{1,0:T(8,128)(2,1)}, bf16[8,8192]{1,0:T(8,128)(2,1)S(1)}, u32[]{:S(2)}, u32[]{:S(2)}) collective-permute-start(bf16[8,8192]{1,0:T(8,128)(2,1)} %get-tuple-element.31), channel_id=1, source_target_pairs={{0,3},{1,4},{2,5},{3,6},{4,7},{5,0},{6,1},{7,2},{8,11},{9,12},{10,... | collective-permute-start | bytes 393224 | tf_op jit(solution)/shard_map/ppermute | solution.py:395
  37.4 2.8 %collective-permute-start.4 = (bf16[8,8192]{1,0:T(8,128)(2,1)}, bf16[8,8192]{1,0:T(8,128)(2,1)S(1)}, u32[]{:S(2)}, u32[]{:S(2)}) collective-permute-start(bf16[8,8192]{1,0:T(8,128)(2,1)} %get-tuple-element.32), channel_id=1, source_target_pairs={{0,4},{1,5},{2,6},{3,7},{4,0},{5,1},{6,2},{7,3},{8,12},{9,13},{10,... | collective-permute-start | bytes 393224 | tf_op jit(solution)/shard_map/ppermute | solution.py:395
  40.2 6.4 %collective-permute-start.5 = (bf16[8,8192]{1,0:T(8,128)(2,1)}, bf16[8,8192]{1,0:T(8,128)(2,1)S(1)}, u32[]{:S(2)}, u32[]{:S(2)}) collective-permute-start(bf16[8,8192]{1,0:T(8,128)(2,1)} %get-tuple-element.33), channel_id=1, source_target_pairs={{0,5},{1,6},{2,7},{3,0},{4,1},{5,2},{6,3},{7,4},{8,13},{9,14},{10,... | collective-permute-start | bytes 393224 | tf_op jit(solution)/shard_map/ppermute | solution.py:395
  46.6 3.4 %collective-permute-start.6 = (bf16[8,8192]{1,0:T(8,128)(2,1)}, bf16[8,8192]{1,0:T(8,128)(2,1)S(1)}, u32[]{:S(2)}, u32[]{:S(2)}) collective-permute-start(bf16[8,8192]{1,0:T(8,128)(2,1)} %get-tuple-element.34), channel_id=1, source_target_pairs={{0,6},{1,7},{2,0},{3,1},{4,2},{5,3},{6,4},{7,5},{8,14},{9,15},{10,... | collective-permute-start | bytes 393224 | tf_op jit(solution)/shard_map/ppermute | solution.py:395
  50.0 2.2 %collective-permute-start.7 = (bf16[8,8192]{1,0:T(8,128)(2,1)}, bf16[8,8192]{1,0:T(8,128)(2,1)S(1)}, u32[]{:S(2)}, u32[]{:S(2)}) collective-permute-start(bf16[8,8192]{1,0:T(8,128)(2,1)} %get-tuple-element.35), channel_id=1, source_target_pairs={{0,7},{1,0},{2,1},{3,2},{4,3},{5,4},{6,5},{7,6},{8,15},{9,8},{10,9... | collective-permute-start | bytes 393224 | tf_op jit(solution)/shard_map/ppermute | solution.py:395
  52.2 2.9 %shard_map.121.refs_0_.l_ref = f32[128,2048]{1,0:T(8,128)} custom-call(bf16[128,2048]{1,0:T(8,128)(2,1)} %x_ref.3, bf16[128,128]{1,0:T(8,128)(2,1)} %b_ref.3, bf16[128,128]{1,0:T(8,128)(2,1)} %c_ref.3, f32[16,128]{1,0:T(8,128)} %d_ref.5), custom_call_target="tpu_custom_call" | custom-call | flops 268435456 | bytes 2097152 | tf_op jit(solution)/shard_map/pallas_call | solution.py:145
  55.1 2.2 %shard_map.123 = (bf16[512,128]{1,0:T(8,128)(2,1)}, bf16[512,128]{1,0:T(8,128)(2,1)}, f32[512,128]{1,0:T(8,128)}, f32[512,128]{1,0:T(8,128)}, f32[512,128]{1,0:T(8,128)}) custom-call(bf16[128,512]{1,0:T(8,128)(2,1)} %q_ref.1, bf16[128,512]{1,0:T(8,128)(2,1)} %copy-done.31, bf16[128,128]{1,0:T(8,128)(2,1)} %k_ref.3, bf16[128,128]{1,0:T(8,128)(2,1)} %v_ref.3), custom_call_target="tpu_custom_call" | custom-call | flops 134217728 | bytes 1048576 | tf_op jit(solution)/shard_map/pallas_call | solution.py:221
  57.3 7.4 %collective-permute-done.6.refs_7_.refs_6_ = bf16[8,8192]{1,0:T(8,128)(2,1)S(1)} collective-permute-done((bf16[8,8192]{1,0:T(8,128)(2,1)}, bf16[8,8192]{1,0:T(8,128)(2,1)S(1)}, u32[]{:S(2)}, u32[]{:S(2)}) %collective-permute-start.6) | collective-permute-done | bytes 131104 | tf_op jit(solution)/shard_map/ppermute | solution.py:395
  64.8 0.2 collective-permute-done.7.refs_8_.refs_7_
  65.0 0.7 copy-done.15
  65.6 1.2 %copy-done = f32[128,2048]{1,0:T(8,128)S(1)} copy-done((f32[128,2048]{1,0:T(8,128)S(1)}, f32[128,2048]{1,0:T(8,128)}, u32[]{:S(2)}) %copy-start) | copy-done | bytes 1048600
  66.9 0.9 copy-done.2
  67.8 0.9 copy-done.16
  68.7 1.1 shard_map.125
  69.8 0.6 copy-done.13
  70.4 11.1 %all-to-all-start.1 = ((bf16[64,32,128]{2,1,0:T(8,128)(2,1)}), bf16[64,32,128]{2,1,0:T(8,128)(2,1)}, u32[]{:S(2)}, u32[]{:S(2)}) async-start(bf16[64,32,128]{2,1,0:T(8,128)(2,1)} %get-tuple-element.36), calls=%async_computation.1 | async-start | bytes 1048576 | tf_op jit(solution)/shard_map/all_to_all | solution.py:335
  81.5 3.3 %collective-permute-start.8 = (bf16[64,32,128]{2,1,0:T(8,128)(2,1)S(1)}, bf16[64,32,128]{2,1,0:T(8,128)(2,1)S(1)}, u32[]{:S(2)}, u32[]{:S(2)}) collective-permute-start(bf16[64,32,128]{2,1,0:T(8,128)(2,1)S(1)} %get-tuple-element.40.refs_5_.refs_2_), channel_id=1, source_target_pairs={{0,16},{8,24},{16,32},{24,40},{32,48},{40,56},{48,0},{56,8},{64,80... | collective-permute-start | bytes 1572872 | tf_op jit(solution)/shard_map/ppermute | solution.py:332
  84.8 3.2 %collective-permute-start.9 = (bf16[64,32,128]{2,1,0:T(8,128)(2,1)S(1)}, bf16[64,32,128]{2,1,0:T(8,128)(2,1)S(1)}, u32[]{:S(2)}, u32[]{:S(2)}) collective-permute-start(bf16[64,32,128]{2,1,0:T(8,128)(2,1)S(1)} %get-tuple-element.40.refs_5_.refs_2_), channel_id=1, source_target_pairs={{0,48},{8,56},{16,0},{24,8},{32,16},{40,24},{48,32},{56,40},{64,11... | collective-permute-start | bytes 1572872 | tf_op jit(solution)/shard_map/ppermute | solution.py:333
  88.1 0.1 copy.13.ids_ref
  88.1 0.1 copy.14.gates_ref
  88.2 0.9 copy-done.6
  89.1 0.9 copy-done.8
  90.0 0.9 copy-done.10
  90.9 0.9 copy-done.12
  91.8 0.9 copy-done.14
  92.8 0.9 copy-done.17
  93.7 0.9 copy-done.25
  94.6 2.5 %shard_map.132 = bf16[16,8192]{1,0:T(8,128)(2,1)} custom-call(s32[1]{0:T(128)} %bitcast.me_ref, s32[16,2]{1,0:T(8,128)S(1)} %copy.13.ids_ref, s32[2,16]{1,0:T(2,128)S(1)} %bitcast.4, f32[16,2]{1,0:T(8,128)S(1)} %copy.14.gates_ref, bf16[8,8192]{1,0:T(8,128)(2,1)S(1)} %copy-done.25, bf16[8,8192]{1,0:T(8,128)(2,1)S(1)} %collective-permute-done.1.refs_2_.refs_1_, ...), custom_call_target="tpu_custom_call" | custom-call | flops 16777216 | bytes 1048576 | tf_op jit(solution)/shard_map/pallas_call | solution.py:405
  97.1 0.1 shard_map.129
  97.2 2.6 %shard_map.127 = (f32[512,128]{1,0:T(8,128)S(1)}, f32[512,128]{1,0:T(8,128)S(1)}, f32[512,128]{1,0:T(8,128)S(1)}) custom-call(s32[1]{0:T(128)} %bitcast.2.refs_0_, bf16[512,128]{1,0:T(8,128)(2,1)S(1)} %copy-done.3, f32[512,128]{1,0:T(8,128)S(1)} %copy-done.18, f32[512,128]{1,0:T(8,128)S(1)} %copy-done.19, f32[512,128]{1,0:T(8,128)S(1)} %copy-done.20, ...), custom_call_target="tpu_custom_call" | custom-call | flops 268435456 | bytes 2097152 | tf_op jit(solution)/shard_map/pallas_call | solution.py:276
  99.8 2.9 %collective-permute-done.8.refs_5_ = bf16[64,32,128]{2,1,0:T(8,128)(2,1)S(1)} collective-permute-done((bf16[64,32,128]{2,1,0:T(8,128)(2,1)S(1)}, bf16[64,32,128]{2,1,0:T(8,128)(2,1)S(1)}, u32[]{:S(2)}, u32[]{:S(2)}) %collective-permute-start.8) | collective-permute-done | bytes 524320 | tf_op jit(solution)/shard_map/ppermute | solution.py:332
  102.8 0.3 collective-permute-done.9.refs_6_
  103.0 0.4 shard_map.130
  103.4 5.6 %collective-permute-start.10 = (f32[512,256]{1,0:T(8,128)S(1)}, f32[512,256]{1,0:T(8,128)S(1)}, u32[]{:S(2)}, u32[]{:S(2)}) collective-permute-start(f32[512,256]{1,0:T(8,128)S(1)} %shard_map.130), channel_id=1, source_target_pairs={{0,8},{8,0},{16,24},{24,16},{32,40},{40,32},{48,56},{56,48},{64,72... | collective-permute-start | bytes 1572872 | tf_op jit(solution)/shard_map/ppermute | solution.py:320
  109.0 2.6 %shard_map.128 = (f32[512,128]{1,0:T(8,128)S(1)}, f32[512,128]{1,0:T(8,128)S(1)}, f32[512,128]{1,0:T(8,128)S(1)}) custom-call(s32[1]{0:T(128)} %bitcast.2.refs_0_, bf16[512,128]{1,0:T(8,128)(2,1)S(1)} %copy-done.3, f32[512,128]{1,0:T(8,128)S(1)} %get-tuple-element.42.refs_2_, f32[512,128]{1,0:T(8,128)S(1)} %get-tuple-element.43.refs_3_, ...), custom_call_target="tpu_custom_call" | custom-call | flops 268435456 | bytes 2097152 | tf_op jit(solution)/shard_map/pallas_call | solution.py:276
  111.6 0.7 copy-done.21
  112.3 0.7 copy-done.23
  113.0 0.0 copy-start.27
  113.1 0.7 copy-done.27
  113.8 2.5 %shard_map.126 = bf16[128,2048]{1,0:T(8,128)(2,1)} custom-call(f32[128,2048]{1,0:T(8,128)S(1)} %copy-done.1, bf16[2048,128]{1,0:T(8,128)(2,1)} %bitcast.1.e_ref, bf16[128,128]{1,0:T(8,128)(2,1)S(1)} %copy-done.27, f32[16,128]{1,0:T(8,128)S(1)} %copy-done.26), custom_call_target="tpu_custom_call" | custom-call | flops 34359738368 | bytes 2097152 | tf_op jit(solution)/shard_map/pallas_call | solution.py:168
  116.4 1.1 shard_map.131
  (56 shorter events, 0.1 us)
Async XLA Ops:
  3.7 62.0 %all-to-all-start = ((bf16[64,104,128]{2,1,0:T(8,128)(2,1)}), bf16[64,104,128]{2,1,0:T(8,128)(2,1)S(1)}, u32[]{:S(2)}, u32[]{:S(2)}) async-start(bf16[64,104,128]{2,1,0:T(8,128)(2,1)} %shard_map.122.after_ref), calls=%async_computation | async-start | bytes 3407872 | tf_op jit(solution)/shard_map/all_to_all | solution.py:326
  15.3 12.1 %copy-start.30 = (bf16[128,512]{1,0:T(8,128)(2,1)S(1)}, bf16[128,512]{1,0:T(8,128)(2,1)}, u32[]{:S(2)}) copy-start(bf16[128,512]{1,0:T(8,128)(2,1)} %q_ref.1) | copy-start | bytes 393220
  17.6 22.6 %collective-permute-start.1 = (bf16[8,8192]{1,0:T(8,128)(2,1)}, bf16[8,8192]{1,0:T(8,128)(2,1)S(1)}, u32[]{:S(2)}, u32[]{:S(2)}) collective-permute-start(bf16[8,8192]{1,0:T(8,128)(2,1)} %get-tuple-element.29), channel_id=1, source_target_pairs={{0,1},{1,2},{2,3},{3,4},{4,5},{5,6},{6,7},{7,0},{8,9},{9,10},{10,1... | collective-permute-start | bytes 393224 | tf_op jit(solution)/shard_map/ppermute | solution.py:395
  21.6 25.0 %collective-permute-start.2 = (bf16[8,8192]{1,0:T(8,128)(2,1)}, bf16[8,8192]{1,0:T(8,128)(2,1)S(1)}, u32[]{:S(2)}, u32[]{:S(2)}) collective-permute-start(bf16[8,8192]{1,0:T(8,128)(2,1)} %get-tuple-element.30), channel_id=1, source_target_pairs={{0,2},{1,3},{2,4},{3,5},{4,6},{5,7},{6,0},{7,1},{8,10},{9,11},{10,... | collective-permute-start | bytes 393224 | tf_op jit(solution)/shard_map/ppermute | solution.py:395
  27.4 22.6 %collective-permute-start = (bf16[128,512]{1,0:T(8,128)(2,1)S(1)}, bf16[128,512]{1,0:T(8,128)(2,1)S(1)}, u32[]{:S(2)}, u32[]{:S(2)}) collective-permute-start(bf16[128,512]{1,0:T(8,128)(2,1)S(1)} %copy-done.30), channel_id=1, source_target_pairs={{0,8},{8,0},{16,24},{24,16},{32,40},{40,32},{48,56},{56,48},{64,72... | collective-permute-start | bytes 393224 | tf_op jit(solution)/shard_map/ppermute | solution.py:320
  30.3 27.0 %collective-permute-start.3 = (bf16[8,8192]{1,0:T(8,128)(2,1)}, bf16[8,8192]{1,0:T(8,128)(2,1)S(1)}, u32[]{:S(2)}, u32[]{:S(2)}) collective-permute-start(bf16[8,8192]{1,0:T(8,128)(2,1)} %get-tuple-element.31), channel_id=1, source_target_pairs={{0,3},{1,4},{2,5},{3,6},{4,7},{5,0},{6,1},{7,2},{8,11},{9,12},{10,... | collective-permute-start | bytes 393224 | tf_op jit(solution)/shard_map/ppermute | solution.py:395
  37.4 20.0 %collective-permute-start.4 = (bf16[8,8192]{1,0:T(8,128)(2,1)}, bf16[8,8192]{1,0:T(8,128)(2,1)S(1)}, u32[]{:S(2)}, u32[]{:S(2)}) collective-permute-start(bf16[8,8192]{1,0:T(8,128)(2,1)} %get-tuple-element.32), channel_id=1, source_target_pairs={{0,4},{1,5},{2,6},{3,7},{4,0},{5,1},{6,2},{7,3},{8,12},{9,13},{10,... | collective-permute-start | bytes 393224 | tf_op jit(solution)/shard_map/ppermute | solution.py:395
  40.2 17.1 %collective-permute-start.5 = (bf16[8,8192]{1,0:T(8,128)(2,1)}, bf16[8,8192]{1,0:T(8,128)(2,1)S(1)}, u32[]{:S(2)}, u32[]{:S(2)}) collective-permute-start(bf16[8,8192]{1,0:T(8,128)(2,1)} %get-tuple-element.33), channel_id=1, source_target_pairs={{0,5},{1,6},{2,7},{3,0},{4,1},{5,2},{6,3},{7,4},{8,13},{9,14},{10,... | collective-permute-start | bytes 393224 | tf_op jit(solution)/shard_map/ppermute | solution.py:395
  46.6 23.1 %copy-start.5 = (bf16[8,8192]{1,0:T(8,128)(2,1)}, bf16[8,8192]{1,0:T(8,128)(2,1)S(1)}, u32[]{:S(2)}) copy-start(bf16[8,8192]{1,0:T(8,128)(2,1)S(1)} %collective-permute-done.2.refs_3_.refs_2_) | copy-start | bytes 393220
  46.6 18.2 %collective-permute-start.6 = (bf16[8,8192]{1,0:T(8,128)(2,1)}, bf16[8,8192]{1,0:T(8,128)(2,1)S(1)}, u32[]{:S(2)}, u32[]{:S(2)}) collective-permute-start(bf16[8,8192]{1,0:T(8,128)(2,1)} %get-tuple-element.34), channel_id=1, source_target_pairs={{0,6},{1,7},{2,0},{3,1},{4,2},{5,3},{6,4},{7,5},{8,14},{9,15},{10,... | collective-permute-start | bytes 393224 | tf_op jit(solution)/shard_map/ppermute | solution.py:395
  50.0 5.1 %copy-start.31 = (bf16[128,512]{1,0:T(8,128)(2,1)}, bf16[128,512]{1,0:T(8,128)(2,1)S(1)}, u32[]{:S(2)}) copy-start(bf16[128,512]{1,0:T(8,128)(2,1)S(1)} %collective-permute-done.q2_ref) | copy-start | bytes 393220
  50.0 15.0 %collective-permute-start.7 = (bf16[8,8192]{1,0:T(8,128)(2,1)}, bf16[8,8192]{1,0:T(8,128)(2,1)S(1)}, u32[]{:S(2)}, u32[]{:S(2)}) collective-permute-start(bf16[8,8192]{1,0:T(8,128)(2,1)} %get-tuple-element.35), channel_id=1, source_target_pairs={{0,7},{1,0},{2,1},{3,2},{4,3},{5,4},{6,5},{7,6},{8,15},{9,8},{10,9... | collective-permute-start | bytes 393224 | tf_op jit(solution)/shard_map/ppermute | solution.py:395
  57.3 12.4 %copy-start.7 = (bf16[8,8192]{1,0:T(8,128)(2,1)}, bf16[8,8192]{1,0:T(8,128)(2,1)S(1)}, u32[]{:S(2)}) copy-start(bf16[8,8192]{1,0:T(8,128)(2,1)S(1)} %collective-permute-done.3.refs_4_.refs_3_) | copy-start | bytes 393220
  57.3 12.4 %copy-start.9 = (bf16[8,8192]{1,0:T(8,128)(2,1)}, bf16[8,8192]{1,0:T(8,128)(2,1)S(1)}, u32[]{:S(2)}) copy-start(bf16[8,8192]{1,0:T(8,128)(2,1)S(1)} %collective-permute-done.4.refs_5_.refs_4_) | copy-start | bytes 393220
  57.3 12.4 %copy-start.11 = (bf16[8,8192]{1,0:T(8,128)(2,1)}, bf16[8,8192]{1,0:T(8,128)(2,1)S(1)}, u32[]{:S(2)}) copy-start(bf16[8,8192]{1,0:T(8,128)(2,1)S(1)} %collective-permute-done.5.refs_6_.refs_5_) | copy-start | bytes 393220
  65.0 0.7 copy-start.15
  65.6 1.2 %copy-start = (f32[128,2048]{1,0:T(8,128)S(1)}, f32[128,2048]{1,0:T(8,128)}, u32[]{:S(2)}) copy-start(f32[128,2048]{1,0:T(8,128)} %shard_map.121.refs_0_.l_ref) | copy-start | bytes 3145732
  66.9 0.9 copy-start.2
  67.8 0.9 copy-start.16
  68.7 19.4 %copy-start.28 = (s32[16,2]{0,1:T(2,128)S(1)}, s32[16,2]{0,1:T(2,128)}, u32[]{:S(2)}) copy-start(s32[16,2]{0,1:T(2,128)} %param.17) | copy-start | bytes 388
  68.7 19.5 %copy-start.29 = (f32[16,2]{0,1:T(2,128)S(1)}, f32[16,2]{0,1:T(2,128)}, u32[]{:S(2)}) copy-start(f32[16,2]{0,1:T(2,128)} %param.18) | copy-start | bytes 388
  69.8 0.6 copy-start.13
  70.4 26.7 %copy-start.4 = (bf16[512,128]{1,0:T(8,128)(2,1)S(1)}, bf16[512,128]{1,0:T(8,128)(2,1)}, u32[]{:S(2)}) copy-start(bf16[512,128]{1,0:T(8,128)(2,1)} %get-tuple-element.48.refs_1_) | copy-start | bytes 393220
  70.4 26.8 %copy-start.3 = (bf16[512,128]{1,0:T(8,128)(2,1)S(1)}, bf16[512,128]{1,0:T(8,128)(2,1)}, u32[]{:S(2)}) copy-start(bf16[512,128]{1,0:T(8,128)(2,1)} %get-tuple-element.28.refs_1_) | copy-start | bytes 393220
  70.4 26.8 %copy-start.18 = (f32[512,128]{1,0:T(8,128)S(1)}, f32[512,128]{1,0:T(8,128)}, u32[]{:S(2)}) copy-start(f32[512,128]{1,0:T(8,128)} %get-tuple-element.37.refs_2_) | copy-start | bytes 786436
  70.4 26.8 %copy-start.19 = (f32[512,128]{1,0:T(8,128)S(1)}, f32[512,128]{1,0:T(8,128)}, u32[]{:S(2)}) copy-start(f32[512,128]{1,0:T(8,128)} %get-tuple-element.38.refs_3_) | copy-start | bytes 786436
  70.4 26.8 %copy-start.20 = (f32[512,128]{1,0:T(8,128)S(1)}, f32[512,128]{1,0:T(8,128)}, u32[]{:S(2)}) copy-start(f32[512,128]{1,0:T(8,128)} %get-tuple-element.39.refs_4_) | copy-start | bytes 786436
  70.4 42.6 %all-to-all-start.1 = ((bf16[64,32,128]{2,1,0:T(8,128)(2,1)}), bf16[64,32,128]{2,1,0:T(8,128)(2,1)}, u32[]{:S(2)}, u32[]{:S(2)}) async-start(bf16[64,32,128]{2,1,0:T(8,128)(2,1)} %get-tuple-element.36), calls=%async_computation.1 | async-start | bytes 1048576 | tf_op jit(solution)/shard_map/all_to_all | solution.py:335
  81.5 21.2 %collective-permute-start.8 = (bf16[64,32,128]{2,1,0:T(8,128)(2,1)S(1)}, bf16[64,32,128]{2,1,0:T(8,128)(2,1)S(1)}, u32[]{:S(2)}, u32[]{:S(2)}) collective-permute-start(bf16[64,32,128]{2,1,0:T(8,128)(2,1)S(1)} %get-tuple-element.40.refs_5_.refs_2_), channel_id=1, source_target_pairs={{0,16},{8,24},{16,32},{24,40},{32,48},{40,56},{48,0},{56,8},{64,80... | collective-permute-start | bytes 1572872 | tf_op jit(solution)/shard_map/ppermute | solution.py:332
  84.8 18.2 %collective-permute-start.9 = (bf16[64,32,128]{2,1,0:T(8,128)(2,1)S(1)}, bf16[64,32,128]{2,1,0:T(8,128)(2,1)S(1)}, u32[]{:S(2)}, u32[]{:S(2)}) collective-permute-start(bf16[64,32,128]{2,1,0:T(8,128)(2,1)S(1)} %get-tuple-element.40.refs_5_.refs_2_), channel_id=1, source_target_pairs={{0,48},{8,56},{16,0},{24,8},{32,16},{40,24},{48,32},{56,40},{64,11... | collective-permute-start | bytes 1572872 | tf_op jit(solution)/shard_map/ppermute | solution.py:333
  88.2 0.9 copy-start.6
  89.1 0.9 copy-start.8
  90.0 0.9 copy-start.10
  90.9 0.9 copy-start.12
  91.8 0.9 copy-start.14
  92.8 0.9 copy-start.17
  93.7 0.9 copy-start.25
  103.0 10.0 %copy-start.1 = (f32[128,2048]{1,0:T(8,128)S(1)}, f32[128,2048]{1,0:T(8,128)}, u32[]{:S(2)}) copy-start(f32[128,2048]{1,0:T(8,128)} %shard_map.121.refs_0_.l_ref) | copy-start | bytes 3145732
  103.0 10.0 %copy-start.26 = (f32[16,128]{1,0:T(8,128)S(1)}, f32[16,128]{1,0:T(8,128)}, u32[]{:S(2)}) copy-start(f32[16,128]{1,0:T(8,128)} %d_ref.5) | copy-start | bytes 24580
  103.4 12.9 %collective-permute-start.10 = (f32[512,256]{1,0:T(8,128)S(1)}, f32[512,256]{1,0:T(8,128)S(1)}, u32[]{:S(2)}, u32[]{:S(2)}) collective-permute-start(f32[512,256]{1,0:T(8,128)S(1)} %shard_map.130), channel_id=1, source_target_pairs={{0,8},{8,0},{16,24},{24,16},{32,40},{40,32},{48,56},{56,48},{64,72... | collective-permute-start | bytes 1572872 | tf_op jit(solution)/shard_map/ppermute | solution.py:320
  111.6 0.7 copy-start.21
  112.3 0.7 copy-start.23
  113.0 0.8 copy-start.27
  113.8 2.5 %copy-start.22 = (f32[512,128]{1,0:T(8,128)S(1)}, f32[512,128]{1,0:T(8,128)}, u32[]{:S(2)}) copy-start(f32[512,128]{1,0:T(8,128)} %copy-done.21) | copy-start | bytes 786436
  113.8 2.5 %copy-start.24 = (f32[512,128]{1,0:T(8,128)S(1)}, f32[512,128]{1,0:T(8,128)}, u32[]{:S(2)}) copy-start(f32[512,128]{1,0:T(8,128)} %copy-done.23) | copy-start | bytes 786436

commit v5 on v4

--- a/solution.py
+++ b/solution.py
@@ -18,7 +18,7 @@
 BF16 = jnp.bfloat16
 VM = pl.BlockSpec(memory_space=pltpu.VMEM)
 SM = pl.BlockSpec(memory_space=pltpu.SMEM)
-ANY = pl.BlockSpec(memory_space=pl.ANY)
+TILE = pl.BlockSpec((8, 128), lambda i: (0, 0))
 
 
 LARGE, SMALL = 60, 24
@@ -26,6 +26,10 @@
 
 def params(mib=SMALL):
     return pltpu.CompilerParams(vmem_limit_bytes=mib * 2**20)
+
+
+def full(shape):
+    return pl.BlockSpec(shape, lambda i: (0,) * len(shape))
 
 
 def cost(flops, nbytes):
@@ -119,8 +123,9 @@
             jax.ShapeDtypeStruct((NCTX, KV, HD), BF16),
             jax.ShapeDtypeStruct((NCTX, SL, HD), BF16),
         ],
-        in_specs=[VM] + [ANY] * len(after),
-        out_specs=[VM] * 3,
+        grid=(1,),
+        in_specs=[full(received.shape)] + [TILE] * len(after),
+        out_specs=[full((NCTX, KV, HD)), full((NCTX, KV, HD)), full((NCTX, SL, HD))],
         compiler_params=params(),
         cost_estimate=cost(1 << 20, 1 << 21),
     )(received, *after)
@@ -152,7 +157,7 @@
     )(x_in, b_in, c_in, decay_log)
 
 
-JOIN_COST = 1 << 35
+JOIN_COST = 1 << 26
 
 
 def join_kernel(l_ref, e_ref, c_ref, d_ref, o_ref):
@@ -170,7 +175,7 @@
         out_shape=jax.ShapeDtypeStruct((L, MH * HD), BF16),
         in_specs=[VM] * 4,
         out_specs=VM,
-        compiler_params=params(),
+        compiler_params=params(LARGE),
         cost_estimate=cost(JOIN_COST, 1 << 21),
     )(local, entering, c_in, decay_log)
 
@@ -228,11 +233,11 @@
     )(q_in, q_other, k_in, v_in)
 
 
-def attend_kernel(n_sets, fresh, pack, other, me_ref, q_ref, *refs):
+def attend_kernel(n_sets, n_ties, fresh, pack, other, me_ref, q_ref, *refs):
     if not fresh:
         m_in, l_in, a_in = refs[:3]
         refs = refs[3:]
-    sets, refs = refs[:n_sets], refs[n_sets:]
+    sets, refs = refs[:n_sets], refs[n_sets + n_ties :]
     if pack:
         o_ref, m_ref, l_ref, a_ref = refs
     else:
@@ -269,19 +274,23 @@
         o_ref[:, HD:] = jnp.where(lane < L // 2, m_ref[...], total)
 
 
-def attend(me, queries, carry, sets, other=False, pack=False):
+def attend(me, queries, carry, sets, other=False, pack=False, after=()):
     def kernel(*refs):
-        attend_kernel(len(sets), not carry, pack, other, *refs)
+        attend_kernel(len(sets), len(after), not carry, pack, other, *refs)
 
     return pl.pallas_call(
         kernel,
+        grid=(1,),
         out_shape=jax.ShapeDtypeStruct((ROWS, HD + L), F32) if pack else [PART] * 3,
-        in_specs=[SM] + [VM] * (1 + len(carry) + len(sets)),
-        out_specs=VM if pack else [VM] * 3,
+        in_specs=[SM, full(queries.shape)]
+        + [full(PART.shape)] * len(carry)
+        + [full(s.shape) for s in sets]
+        + [TILE] * len(after),
+        out_specs=full((ROWS, HD + L)) if pack else [full(PART.shape)] * 3,
         scratch_shapes=[pltpu.VMEM((ROWS, L), F32)] * 3 if pack else [],
         compiler_params=params(),
         cost_estimate=cost(1 << 28, len(sets) << 20),
-    )(me, queries, *carry, *sets)
+    )(me, queries, *carry, *sets, *after)
 
 
 def merge_kernel(m_ref, l_ref, a_ref, p_ref, o_ref):
@@ -324,11 +333,13 @@
     me = lax.axis_index("ctx").astype(jnp.int32).reshape(1)
     chunks = chunks_to_send(x_in, b_in, decay_log, k_in, v_in)
     received = lax.all_to_all(chunks, "ctx", split_axis=0, concat_axis=0, tiled=True)
-    blocks = expert_blocks(expert_out, chunks)
     q_other = other_core(q_in)
     q_own, q_other, *carry = open_attention(q_in, q_other, k_in, v_in)
     local = local_part(x_in, b_in, c_in, decay_log)
-    own, opposite, entering = take_received(received, [local, q_own, *blocks[1:]])
+    sent = chunks.reshape(NCTX * CHUNK, HD)
+    blocks = expert_blocks(expert_out, [sent, local, q_own])
+    nearer = [blocks[d] for d in (1, 7, 2, 6, 3, 5) if d < len(blocks)]
+    own, opposite, entering = take_received(received, nearer)
     right = lax.ppermute(own, "ctx", along_x(1))
     left = lax.ppermute(own, "ctx", along_x(-1))
 
@@ -337,13 +348,17 @@
 
     carry = attend(me, q_own, carry, [own, opposite])
     carry_other = attend(me, q_other, [], [own, opposite], other=True)
-    part = attend(me, q_other, carry_other, [right, left], other=True, pack=True)
+    farthest = blocks[4:5]
+    part = attend(
+        me, q_other, carry_other, [right, left], other=True, pack=True, after=[*farthest, carry[0]]
+    )
     part = other_core(part)
     carry = attend(me, q_own, carry, [right, left])
     return mamba_out, merge_attention(carry, part), blocks
 
 
-def blocks_kernel(me_ref, e_ref, after_ref, *outs):
+def blocks_kernel(n_ties, me_ref, e_ref, *refs):
+    outs = refs[n_ties:]
     for d, o_ref in enumerate(outs):
         to = lax.rem(me_ref[0] + d, len(outs))
         o_ref[...] = jnp.concatenate(
@@ -381,16 +396,20 @@
 def expert_blocks(expert_out, after):
     owned, peers, cap, width = expert_out.shape[1:]
     me = lax.axis_index("grp").astype(jnp.int32).reshape(1)
+    def kernel(*refs):
+        blocks_kernel(len(after), *refs)
+
     held = pl.pallas_call(
-        blocks_kernel,
+        kernel,
         out_shape=[jax.ShapeDtypeStruct((owned * cap, width), BF16)] * peers,
-        in_specs=[SM, VM, ANY],
-        out_specs=[VM] * peers,
+        grid=(1,),
+        in_specs=[SM, full(expert_out.shape)] + [TILE] * len(after),
+        out_specs=[full((owned * cap, width))] * peers,
         compiler_params=params(LARGE),
         cost_estimate=cost(1 << 20, 1 << 21),
-    )(me, expert_out, after)
+    )(me, expert_out, *after)
     blocks = list(held)
-    for d in sorted(range(1, peers), key=lambda d: -min(d, peers - d)):
+    for d in sorted(range(1, peers), key=lambda d: min(d, peers - d)):
         pairs = [(i, (i + d) % peers) for i in range(peers)]
         blocks[d] = lax.ppermute(held[d], "grp", pairs)
     return blocks
@@ -414,7 +433,7 @@
         ]
         + [pl.BlockSpec((rows, block), lambda i: (0, i))] * peers,
         out_specs=pl.BlockSpec((count, block), lambda i: (0, i)),
-        compiler_params=params(),
+        compiler_params=params(LARGE),
         cost_estimate=cost(1 << 24, 1 << 20),
     )(me, expert_ids, expert_ids.T, gates, *blocks)
 

time: 118 us -> 115 us (0.975)
  the two profiles are of different devices: /device:TPU:1 before, /device:TPU:67 now
where the time goes in v5:
time: 115 us; the launch traced here: 114 us
  starting transfers between devices  66.8 us (58%)
  Pallas kernels  29.7 us (26%)
  waiting for transfers between devices  10.4 us (9%)
  local copies, waits for them, and re-layouts  6.2 us (5%)
    ppermute x7, starting transfers between devices, expert_blocks(): blocks[d] = lax.ppermute(held[d], 'grp', pairs)  29.5 us
    all_to_all x1, starting transfers between devices, context_parts(): lax.all_to_all(entering, 'ctx', split_axis=0, concat_axis=0, tiled=True)  16 us
    all_to_all x1, starting transfers between devices, context_parts(): lax.all_to_all(chunks, 'ctx', split_axis=0, concat_axis=0, tiled=True)  11.1 us
    pallas_call x4, Pallas kernels, attend(): pl.pallas_call(kernel, grid=(1,), out_shape=jax.ShapeDtypeStruct((ROWS, H...  10.4 us
    ppermute x7, waiting for transfers between devices, expert_blocks(): blocks[d] = lax.ppermute(held[d], 'grp', pairs)  10.4 us
    unnamed x40, local copies, waits for them, and re-layouts  6.2 us
    ppermute x2, starting transfers between devices, other_core(): return lax.ppermute(value, 'ctx', [(i, i ^ 1) for i in range(NCTX)])  4.73 us
    pallas_call x1, Pallas kernels, expert_part(): pl.pallas_call(combine_kernel, grid=(width // block,), out_shape=jax.Shap...  3.9 us
  transfers between devices with their start and end apart: 13, of which 3 were waited for; matrix products, arithmetic and copies ran while one was open for 1% of the time, Pallas kernels for 21%

profile of v5, /device:TPU:67, one launch (start us, length us, event | category | flops | bytes accessed | tf_op | source)
XLA Modules:
  0.0 114.0 jit_solution(17044845204939476025)
XLA Ops:
  0.6 3.0 %shard_map.122 = bf16[64,104,128]{2,1,0:T(8,128)(2,1)} custom-call(bf16[128,2048]{1,0:T(8,128)(2,1)} %x_ref.3, bf16[128,128]{1,0:T(8,128)(2,1)} %b_ref.3, f32[16,128]{1,0:T(8,128)} %d_ref.5, bf16[128,128]{1,0:T(8,128)(2,1)} %k_ref.3, bf16[128,128]{1,0:T(8,128)(2,1)} %v_ref.3), custom_call_target="tpu_custom_call" | custom-call | flops 67108864 | bytes 2097152 | tf_op jit(solution)/shard_map/pallas_call | solution.py:94
  3.6 11.1 %all-to-all-start = ((bf16[64,104,128]{2,1,0:T(8,128)(2,1)}), bf16[64,104,128]{2,1,0:T(8,128)(2,1)S(1)}, u32[]{:S(2)}, u32[]{:S(2)}) async-start(bf16[64,104,128]{2,1,0:T(8,128)(2,1)} %shard_map.122), calls=%async_computation | async-start | bytes 3407872 | tf_op jit(solution)/shard_map/all_to_all | solution.py:335
  14.8 2.3 %collective-permute-start = (bf16[128,512]{1,0:T(8,128)(2,1)S(1)}, bf16[128,512]{1,0:T(8,128)(2,1)S(1)}, u32[]{:S(2)}, u32[]{:S(2)}) collective-permute-start(bf16[128,512]{1,0:T(8,128)(2,1)S(1)} %copy-done.17), channel_id=1, source_target_pairs={{0,8},{8,0},{16,24},{24,16},{32,40},{40,32},{48,56},{56,48},{64,72... | collective-permute-start | bytes 393224 | tf_op jit(solution)/shard_map/ppermute | solution.py:329
  17.0 2.8 %shard_map.121.refs_3_.l_ref = f32[128,2048]{1,0:T(8,128)} custom-call(bf16[128,2048]{1,0:T(8,128)(2,1)} %x_ref.3, bf16[128,128]{1,0:T(8,128)(2,1)} %b_ref.3, bf16[128,128]{1,0:T(8,128)(2,1)} %c_ref.3, f32[16,128]{1,0:T(8,128)} %d_ref.5), custom_call_target="tpu_custom_call" | custom-call | flops 268435456 | bytes 2097152 | tf_op jit(solution)/shard_map/pallas_call | solution.py:150
  19.9 0.0 collective-permute-done.q2_ref
  19.9 0.7 copy-done.18
  20.5 2.2 %shard_map.123 = (bf16[512,128]{1,0:T(8,128)(2,1)}, bf16[512,128]{1,0:T(8,128)(2,1)}, f32[512,128]{1,0:T(8,128)}, f32[512,128]{1,0:T(8,128)}, f32[512,128]{1,0:T(8,128)}) custom-call(bf16[128,512]{1,0:T(8,128)(2,1)} %q_ref.1, bf16[128,512]{1,0:T(8,128)(2,1)} %copy-done.18, bf16[128,128]{1,0:T(8,128)(2,1)} %k_ref.3, bf16[128,128]{1,0:T(8,128)(2,1)} %v_ref.3), custom_call_target="tpu_custom_call" | custom-call | flops 134217728 | bytes 1048576 | tf_op jit(solution)/shard_map/pallas_call | solution.py:226
  22.7 2.2 %shard_map.124 = (bf16[8,8192]{1,0:T(8,128)(2,1)}, bf16[8,8192]{1,0:T(8,128)(2,1)}, bf16[8,8192]{1,0:T(8,128)(2,1)}, bf16[8,8192]{1,0:T(8,128)(2,1)}, bf16[8,819...) custom-call(s32[1]{0:T(128)} %bitcast.refs_0_.me_ref, ...), custom_call_target="tpu_custom_call" | custom-call | flops 1048576 | bytes 2097152 | tf_op jit(solution)/shard_map/pallas_call | solution.py:402
  24.9 4.0 %collective-permute-start.1 = (bf16[8,8192]{1,0:T(8,128)(2,1)}, bf16[8,8192]{1,0:T(8,128)(2,1)S(1)}, u32[]{:S(2)}, u32[]{:S(2)}) collective-permute-start(bf16[8,8192]{1,0:T(8,128)(2,1)} %get-tuple-element.29), channel_id=1, source_target_pairs={{0,1},{1,2},{2,3},{3,4},{4,5},{5,6},{6,7},{7,0},{8,9},{9,10},{10,1... | collective-permute-start | bytes 393224 | tf_op jit(solution)/shard_map/ppermute | solution.py:414
  28.9 1.9 %collective-permute-start.2 = (bf16[8,8192]{1,0:T(8,128)(2,1)}, bf16[8,8192]{1,0:T(8,128)(2,1)S(1)}, u32[]{:S(2)}, u32[]{:S(2)}) collective-permute-start(bf16[8,8192]{1,0:T(8,128)(2,1)} %get-tuple-element.30), channel_id=1, source_target_pairs={{0,7},{1,0},{2,1},{3,2},{4,3},{5,4},{6,5},{7,6},{8,15},{9,8},{10,9... | collective-permute-start | bytes 393224 | tf_op jit(solution)/shard_map/ppermute | solution.py:414
  30.9 7.0 %collective-permute-start.3 = (bf16[8,8192]{1,0:T(8,128)(2,1)}, bf16[8,8192]{1,0:T(8,128)(2,1)S(1)}, u32[]{:S(2)}, u32[]{:S(2)}) collective-permute-start(bf16[8,8192]{1,0:T(8,128)(2,1)} %get-tuple-element.31), channel_id=1, source_target_pairs={{0,2},{1,3},{2,4},{3,5},{4,6},{5,7},{6,0},{7,1},{8,10},{9,11},{10,... | collective-permute-start | bytes 393224 | tf_op jit(solution)/shard_map/ppermute | solution.py:414
  37.9 4.0 %collective-permute-start.4 = (bf16[8,8192]{1,0:T(8,128)(2,1)}, bf16[8,8192]{1,0:T(8,128)(2,1)S(1)}, u32[]{:S(2)}, u32[]{:S(2)}) collective-permute-start(bf16[8,8192]{1,0:T(8,128)(2,1)} %get-tuple-element.32), channel_id=1, source_target_pairs={{0,6},{1,7},{2,0},{3,1},{4,2},{5,3},{6,4},{7,5},{8,14},{9,15},{10,... | collective-permute-start | bytes 393224 | tf_op jit(solution)/shard_map/ppermute | solution.py:414
  41.9 5.8 %collective-permute-start.5 = (bf16[8,8192]{1,0:T(8,128)(2,1)}, bf16[8,8192]{1,0:T(8,128)(2,1)S(1)}, u32[]{:S(2)}, u32[]{:S(2)}) collective-permute-start(bf16[8,8192]{1,0:T(8,128)(2,1)} %get-tuple-element.33), channel_id=1, source_target_pairs={{0,3},{1,4},{2,5},{3,6},{4,7},{5,0},{6,1},{7,2},{8,11},{9,12},{10,... | collective-permute-start | bytes 393224 | tf_op jit(solution)/shard_map/ppermute | solution.py:414
  47.7 0.0 collective-permute-done.1.refs_0_.refs_1_
  47.7 2.7 %collective-permute-start.6 = (bf16[8,8192]{1,0:T(8,128)(2,1)}, bf16[8,8192]{1,0:T(8,128)(2,1)S(1)}, u32[]{:S(2)}, u32[]{:S(2)}) collective-permute-start(bf16[8,8192]{1,0:T(8,128)(2,1)} %get-tuple-element.34), channel_id=1, source_target_pairs={{0,5},{1,6},{2,7},{3,0},{4,1},{5,2},{6,3},{7,4},{8,13},{9,14},{10,... | collective-permute-start | bytes 393224 | tf_op jit(solution)/shard_map/ppermute | solution.py:414
  50.4 0.0 collective-permute-done.2.refs_1_.refs_7_
  50.4 0.0 collective-permute-done.3.refs_2_
  50.4 0.0 collective-permute-done.4.refs_3_.refs_6_
  50.5 2.5 %collective-permute-done.5.refs_4_.refs_3_ = bf16[8,8192]{1,0:T(8,128)(2,1)S(1)} collective-permute-done((bf16[8,8192]{1,0:T(8,128)(2,1)}, bf16[8,8192]{1,0:T(8,128)(2,1)S(1)}, u32[]{:S(2)}, u32[]{:S(2)}) %collective-permute-start.5) | collective-permute-done | bytes 131104 | tf_op jit(solution)/shard_map/ppermute | solution.py:414
  52.9 6.2 %collective-permute-done.6.refs_5_ = bf16[8,8192]{1,0:T(8,128)(2,1)S(1)} collective-permute-done((bf16[8,8192]{1,0:T(8,128)(2,1)}, bf16[8,8192]{1,0:T(8,128)(2,1)S(1)}, u32[]{:S(2)}, u32[]{:S(2)}) %collective-permute-start.6) | collective-permute-done | bytes 131104 | tf_op jit(solution)/shard_map/ppermute | solution.py:414
  59.1 0.6 copy-done.7
  59.7 0.0 all-to-all-done.s_ref
  59.7 0.9 copy-done.8
  60.6 1.1 shard_map.125
  61.7 3.2 %collective-permute-start.7 = (bf16[64,32,128]{2,1,0:T(8,128)(2,1)S(1)}, bf16[64,32,128]{2,1,0:T(8,128)(2,1)S(1)}, u32[]{:S(2)}, u32[]{:S(2)}) collective-permute-start(bf16[64,32,128]{2,1,0:T(8,128)(2,1)S(1)} %get-tuple-element.39.refs_5_.refs_2_), channel_id=1, source_target_pairs={{0,16},{8,24},{16,32},{24,40},{32,48},{40,56},{48,0},{56,8},{64,80... | collective-permute-start | bytes 1572872 | tf_op jit(solution)/shard_map/ppermute | solution.py:343
  64.9 2.2 %collective-permute-start.8 = (bf16[64,32,128]{2,1,0:T(8,128)(2,1)S(1)}, bf16[64,32,128]{2,1,0:T(8,128)(2,1)S(1)}, u32[]{:S(2)}, u32[]{:S(2)}) collective-permute-start(bf16[64,32,128]{2,1,0:T(8,128)(2,1)S(1)} %get-tuple-element.39.refs_5_.refs_2_), channel_id=1, source_target_pairs={{0,48},{8,56},{16,0},{24,8},{32,16},{40,24},{48,32},{56,40},{64,11... | collective-permute-start | bytes 1572872 | tf_op jit(solution)/shard_map/ppermute | solution.py:344
  67.2 16.0 %all-to-all-start.1 = ((bf16[64,32,128]{2,1,0:T(8,128)(2,1)}), bf16[64,32,128]{2,1,0:T(8,128)(2,1)}, u32[]{:S(2)}, u32[]{:S(2)}) async-start(bf16[64,32,128]{2,1,0:T(8,128)(2,1)} %get-tuple-element.35), calls=%async_computation.1 | async-start | bytes 1048576 | tf_op jit(solution)/shard_map/all_to_all | solution.py:346
  83.2 4.2 %collective-permute-start.9 = (bf16[8,8192]{1,0:T(8,128)(2,1)}, bf16[8,8192]{1,0:T(8,128)(2,1)S(1)}, u32[]{:S(2)}, u32[]{:S(2)}) collective-permute-start(bf16[8,8192]{1,0:T(8,128)(2,1)} %get-tuple-element.51), channel_id=1, source_target_pairs={{0,4},{1,5},{2,6},{3,7},{4,0},{5,1},{6,2},{7,3},{8,12},{9,13},{10,... | collective-permute-start | bytes 393224 | tf_op jit(solution)/shard_map/ppermute | solution.py:414
  87.4 2.6 %shard_map.129 = (f32[512,128]{1,0:T(8,128)S(1)}, f32[512,128]{1,0:T(8,128)S(1)}, f32[512,128]{1,0:T(8,128)S(1)}) custom-call(s32[1]{0:T(128)} %bitcast.3.refs_0_, bf16[512,128]{1,0:T(8,128)(2,1)S(1)} %copy-done.1, bf16[64,32,128]{2,1,0:T(8,128)(2,1)S(1)} %get-tuple-element.39.refs_5_.refs_2_, bf16[64,32,128]{2,1,0:T(8,128)(2,1)S(1)} %get-tuple-element.40.refs_6_.refs_3_), custom_call_target="tpu_custom_call" | custom-call | flops 268435456 | bytes 2097152 | tf_op jit(solution)/shard_map/pallas_call | solution.py:281
  90.0 0.9 copy-done.11
  91.0 0.9 copy-done.12
  91.9 2.5 %shard_map.127 = (f32[512,128]{1,0:T(8,128)S(1)}, f32[512,128]{1,0:T(8,128)S(1)}, f32[512,128]{1,0:T(8,128)S(1)}) custom-call(s32[1]{0:T(128)} %bitcast.3.refs_0_, bf16[512,128]{1,0:T(8,128)(2,1)S(1)} %copy-done, f32[512,128]{1,0:T(8,128)S(1)} %copy-done.10, f32[512,128]{1,0:T(8,128)S(1)} %copy-done.11, f32[512,128]{1,0:T(8,128)S(1)} %copy-done.12, ...), custom_call_target="tpu_custom_call" | custom-call | flops 268435456 | bytes 2097152 | tf_op jit(solution)/shard_map/pallas_call | solution.py:281
  94.5 0.0 copy-start.15
  94.5 0.0 copy-start.16
  94.5 1.7 %collective-permute-done.9.refs_7_.refs_4_ = bf16[8,8192]{1,0:T(8,128)(2,1)S(1)} collective-permute-done((bf16[8,8192]{1,0:T(8,128)(2,1)}, bf16[8,8192]{1,0:T(8,128)(2,1)S(1)}, u32[]{:S(2)}, u32[]{:S(2)}) %collective-permute-start.9) | collective-permute-done | bytes 131104 | tf_op jit(solution)/shard_map/ppermute | solution.py:414
  96.2 0.0 collective-permute-done.7.refs_5_
  96.2 0.0 collective-permute-done.8.refs_6_
  96.2 2.7 %shard_map.130 = f32[512,256]{1,0:T(8,128)S(1)} custom-call(s32[1]{0:T(128)} %bitcast.3.refs_0_, bf16[512,128]{1,0:T(8,128)(2,1)S(1)} %copy-done.1, f32[512,128]{1,0:T(8,128)S(1)} %get-tuple-element.48.refs_2_, f32[512,128]{1,0:T(8,128)S(1)} %get-tuple-element.49.refs_3_, f32[512,128]{1,0:T(8,128)S(1)} %get-tuple-element.50.refs_4_, ...), custom_call_target="tpu_custom_call" | custom-call | flops 268435456 | bytes 2097152 | tf_op jit(solution)/shard_map/pallas_call | solution.py:281
  98.9 2.5 %collective-permute-start.10 = (f32[512,256]{1,0:T(8,128)S(1)}, f32[512,256]{1,0:T(8,128)S(1)}, u32[]{:S(2)}, u32[]{:S(2)}) collective-permute-start(f32[512,256]{1,0:T(8,128)S(1)} %shard_map.130), channel_id=1, source_target_pairs={{0,8},{8,0},{16,24},{24,16},{32,40},{40,32},{48,56},{56,48},{64,72... | collective-permute-start | bytes 1572872 | tf_op jit(solution)/shard_map/ppermute | solution.py:329
  101.4 0.7 copy.13.ids_ref
  102.1 0.7 copy.14.gates_ref
  102.8 3.9 %shard_map.132 = bf16[16,8192]{1,0:T(8,128)(2,1)} custom-call(s32[1]{0:T(128)} %bitcast.refs_0_.me_ref, s32[16,2]{1,0:T(8,128)} %copy.13.ids_ref, s32[2,16]{1,0:T(2,128)} %bitcast.6, f32[16,2]{1,0:T(8,128)} %copy.14.gates_ref, bf16[8,8192]{1,0:T(8,128)(2,1)} %get-tuple-element.52.refs_0_, bf16[8,8192]{1,0:T(8,128)(2,1)} %copy-done.2, ...), custom_call_target="tpu_custom_call" | custom-call | flops 16777216 | bytes 1048576 | tf_op jit(solution)/shard_map/pallas_call | solution.py:424
  106.7 2.6 %shard_map.128 = (f32[512,128]{1,0:T(8,128)S(1)}, f32[512,128]{1,0:T(8,128)S(1)}, f32[512,128]{1,0:T(8,128)S(1)}) custom-call(s32[1]{0:T(128)} %bitcast.3.refs_0_, bf16[512,128]{1,0:T(8,128)(2,1)S(1)} %copy-done, f32[512,128]{1,0:T(8,128)S(1)} %get-tuple-element.41.refs_2_.refs_8_, f32[512,128]{1,0:T(8,128)S(1)} %get-tuple-element.42.refs_3_, ...), custom_call_target="tpu_custom_call" | custom-call | flops 268435456 | bytes 2097152 | tf_op jit(solution)/shard_map/pallas_call | solution.py:281
  109.3 0.7 copy-done.13
  109.9 0.0 all-to-all-done.1
  110.0 2.9 %shard_map.126 = bf16[128,2048]{1,0:T(8,128)(2,1)} custom-call(f32[128,2048]{1,0:T(8,128)} %shard_map.121.refs_3_.l_ref, bf16[2048,128]{1,0:T(8,128)(2,1)} %bitcast.2.e_ref, bf16[128,128]{1,0:T(8,128)(2,1)} %c_ref.3, f32[16,128]{1,0:T(8,128)} %d_ref.5), custom_call_target="tpu_custom_call" | custom-call | flops 67108864 | bytes 2097152 | tf_op jit(solution)/shard_map/pallas_call | solution.py:173
  112.8 0.0 collective-permute-done.10.p_ref
  112.8 1.1 %shard_map.131 = bf16[128,512]{1,0:T(8,128)(2,1)} custom-call(f32[512,128]{1,0:T(8,128)S(1)} %get-tuple-element.44.m_ref, f32[512,128]{1,0:T(8,128)S(1)} %get-tuple-element.45.l_ref, f32[512,128]{1,0:T(8,128)S(1)} %copy-done.14, f32[512,256]{1,0:T(8,128)S(1)} %collective-permute-done.10.p_ref), custom_call_target="tpu_custom_call" | custom-call | flops 1048576 | bytes 1048576 | tf_op jit(solution)/shard_map/pallas_call | solution.py:307
  (30 shorter events, 0.1 us)
Async XLA Ops:
  3.6 11.1 %copy-start.17 = (bf16[128,512]{1,0:T(8,128)(2,1)S(1)}, bf16[128,512]{1,0:T(8,128)(2,1)}, u32[]{:S(2)}) copy-start(bf16[128,512]{1,0:T(8,128)(2,1)} %q_ref.1) | copy-start | bytes 393220
  3.6 56.1 %all-to-all-start = ((bf16[64,104,128]{2,1,0:T(8,128)(2,1)}), bf16[64,104,128]{2,1,0:T(8,128)(2,1)S(1)}, u32[]{:S(2)}, u32[]{:S(2)}) async-start(bf16[64,104,128]{2,1,0:T(8,128)(2,1)} %shard_map.122), calls=%async_computation | async-start | bytes 3407872 | tf_op jit(solution)/shard_map/all_to_all | solution.py:335
  14.8 5.1 %collective-permute-start = (bf16[128,512]{1,0:T(8,128)(2,1)S(1)}, bf16[128,512]{1,0:T(8,128)(2,1)S(1)}, u32[]{:S(2)}, u32[]{:S(2)}) collective-permute-start(bf16[128,512]{1,0:T(8,128)(2,1)S(1)} %copy-done.17), channel_id=1, source_target_pairs={{0,8},{8,0},{16,24},{24,16},{32,40},{40,32},{48,56},{56,48},{64,72... | collective-permute-start | bytes 393224 | tf_op jit(solution)/shard_map/ppermute | solution.py:329
  19.9 0.7 copy-start.18
  24.9 22.7 %collective-permute-start.1 = (bf16[8,8192]{1,0:T(8,128)(2,1)}, bf16[8,8192]{1,0:T(8,128)(2,1)S(1)}, u32[]{:S(2)}, u32[]{:S(2)}) collective-permute-start(bf16[8,8192]{1,0:T(8,128)(2,1)} %get-tuple-element.29), channel_id=1, source_target_pairs={{0,1},{1,2},{2,3},{3,4},{4,5},{5,6},{6,7},{7,0},{8,9},{9,10},{10,1... | collective-permute-start | bytes 393224 | tf_op jit(solution)/shard_map/ppermute | solution.py:414
  28.9 21.5 %collective-permute-start.2 = (bf16[8,8192]{1,0:T(8,128)(2,1)}, bf16[8,8192]{1,0:T(8,128)(2,1)S(1)}, u32[]{:S(2)}, u32[]{:S(2)}) collective-permute-start(bf16[8,8192]{1,0:T(8,128)(2,1)} %get-tuple-element.30), channel_id=1, source_target_pairs={{0,7},{1,0},{2,1},{3,2},{4,3},{5,4},{6,5},{7,6},{8,15},{9,8},{10,9... | collective-permute-start | bytes 393224 | tf_op jit(solution)/shard_map/ppermute | solution.py:414
  30.9 19.5 %collective-permute-start.3 = (bf16[8,8192]{1,0:T(8,128)(2,1)}, bf16[8,8192]{1,0:T(8,128)(2,1)S(1)}, u32[]{:S(2)}, u32[]{:S(2)}) collective-permute-start(bf16[8,8192]{1,0:T(8,128)(2,1)} %get-tuple-element.31), channel_id=1, source_target_pairs={{0,2},{1,3},{2,4},{3,5},{4,6},{5,7},{6,0},{7,1},{8,10},{9,11},{10,... | collective-permute-start | bytes 393224 | tf_op jit(solution)/shard_map/ppermute | solution.py:414
  37.9 12.5 %collective-permute-start.4 = (bf16[8,8192]{1,0:T(8,128)(2,1)}, bf16[8,8192]{1,0:T(8,128)(2,1)S(1)}, u32[]{:S(2)}, u32[]{:S(2)}) collective-permute-start(bf16[8,8192]{1,0:T(8,128)(2,1)} %get-tuple-element.32), channel_id=1, source_target_pairs={{0,6},{1,7},{2,0},{3,1},{4,2},{5,3},{6,4},{7,5},{8,14},{9,15},{10,... | collective-permute-start | bytes 393224 | tf_op jit(solution)/shard_map/ppermute | solution.py:414
  41.9 11.0 %collective-permute-start.5 = (bf16[8,8192]{1,0:T(8,128)(2,1)}, bf16[8,8192]{1,0:T(8,128)(2,1)S(1)}, u32[]{:S(2)}, u32[]{:S(2)}) collective-permute-start(bf16[8,8192]{1,0:T(8,128)(2,1)} %get-tuple-element.33), channel_id=1, source_target_pairs={{0,3},{1,4},{2,5},{3,6},{4,7},{5,0},{6,1},{7,2},{8,11},{9,12},{10,... | collective-permute-start | bytes 393224 | tf_op jit(solution)/shard_map/ppermute | solution.py:414
  47.7 19.4 %copy-start.2 = (bf16[8,8192]{1,0:T(8,128)(2,1)}, bf16[8,8192]{1,0:T(8,128)(2,1)S(1)}, u32[]{:S(2)}) copy-start(bf16[8,8192]{1,0:T(8,128)(2,1)S(1)} %collective-permute-done.1.refs_0_.refs_1_) | copy-start | bytes 393220
  47.7 39.7 %copy-start.1 = (bf16[512,128]{1,0:T(8,128)(2,1)S(1)}, bf16[512,128]{1,0:T(8,128)(2,1)}, u32[]{:S(2)}) copy-start(bf16[512,128]{1,0:T(8,128)(2,1)} %get-tuple-element.47.refs_1_) | copy-start | bytes 393220
  47.7 11.4 %collective-permute-start.6 = (bf16[8,8192]{1,0:T(8,128)(2,1)}, bf16[8,8192]{1,0:T(8,128)(2,1)S(1)}, u32[]{:S(2)}, u32[]{:S(2)}) collective-permute-start(bf16[8,8192]{1,0:T(8,128)(2,1)} %get-tuple-element.34), channel_id=1, source_target_pairs={{0,5},{1,6},{2,7},{3,0},{4,1},{5,2},{6,3},{7,4},{8,13},{9,14},{10,... | collective-permute-start | bytes 393224 | tf_op jit(solution)/shard_map/ppermute | solution.py:414
  50.4 16.7 %copy-start.3 = (bf16[8,8192]{1,0:T(8,128)(2,1)}, bf16[8,8192]{1,0:T(8,128)(2,1)S(1)}, u32[]{:S(2)}) copy-start(bf16[8,8192]{1,0:T(8,128)(2,1)S(1)} %collective-permute-done.2.refs_1_.refs_7_) | copy-start | bytes 393220
  50.4 16.7 %copy-start.4 = (bf16[8,8192]{1,0:T(8,128)(2,1)}, bf16[8,8192]{1,0:T(8,128)(2,1)S(1)}, u32[]{:S(2)}) copy-start(bf16[8,8192]{1,0:T(8,128)(2,1)S(1)} %collective-permute-done.3.refs_2_) | copy-start | bytes 393220
  50.4 16.7 %copy-start.5 = (bf16[8,8192]{1,0:T(8,128)(2,1)}, bf16[8,8192]{1,0:T(8,128)(2,1)S(1)}, u32[]{:S(2)}) copy-start(bf16[8,8192]{1,0:T(8,128)(2,1)S(1)} %collective-permute-done.4.refs_3_.refs_6_) | copy-start | bytes 393220
  52.9 14.2 %copy-start.6 = (bf16[8,8192]{1,0:T(8,128)(2,1)}, bf16[8,8192]{1,0:T(8,128)(2,1)S(1)}, u32[]{:S(2)}) copy-start(bf16[8,8192]{1,0:T(8,128)(2,1)S(1)} %collective-permute-done.5.refs_4_.refs_3_) | copy-start | bytes 393220
  59.1 0.7 copy-start.7
  59.7 0.9 copy-start.8
  61.7 28.3 %copy-start = (bf16[512,128]{1,0:T(8,128)(2,1)S(1)}, bf16[512,128]{1,0:T(8,128)(2,1)}, u32[]{:S(2)}) copy-start(bf16[512,128]{1,0:T(8,128)(2,1)} %get-tuple-element.28.refs_4_.refs_1_) | copy-start | bytes 393220
  61.7 28.3 %copy-start.10 = (f32[512,128]{1,0:T(8,128)S(1)}, f32[512,128]{1,0:T(8,128)}, u32[]{:S(2)}) copy-start(f32[512,128]{1,0:T(8,128)} %get-tuple-element.36.refs_2_) | copy-start | bytes 786436
  61.7 34.5 %collective-permute-start.7 = (bf16[64,32,128]{2,1,0:T(8,128)(2,1)S(1)}, bf16[64,32,128]{2,1,0:T(8,128)(2,1)S(1)}, u32[]{:S(2)}, u32[]{:S(2)}) collective-permute-start(bf16[64,32,128]{2,1,0:T(8,128)(2,1)S(1)} %get-tuple-element.39.refs_5_.refs_2_), channel_id=1, source_target_pairs={{0,16},{8,24},{16,32},{24,40},{32,48},{40,56},{48,0},{56,8},{64,80... | collective-permute-start | bytes 1572872 | tf_op jit(solution)/shard_map/ppermute | solution.py:343
  64.9 31.3 %collective-permute-start.8 = (bf16[64,32,128]{2,1,0:T(8,128)(2,1)S(1)}, bf16[64,32,128]{2,1,0:T(8,128)(2,1)S(1)}, u32[]{:S(2)}, u32[]{:S(2)}) collective-permute-start(bf16[64,32,128]{2,1,0:T(8,128)(2,1)S(1)} %get-tuple-element.39.refs_5_.refs_2_), channel_id=1, source_target_pairs={{0,48},{8,56},{16,0},{24,8},{32,16},{40,24},{48,32},{56,40},{64,11... | collective-permute-start | bytes 1572872 | tf_op jit(solution)/shard_map/ppermute | solution.py:344
  67.2 42.8 %all-to-all-start.1 = ((bf16[64,32,128]{2,1,0:T(8,128)(2,1)}), bf16[64,32,128]{2,1,0:T(8,128)(2,1)}, u32[]{:S(2)}, u32[]{:S(2)}) async-start(bf16[64,32,128]{2,1,0:T(8,128)(2,1)} %get-tuple-element.35), calls=%async_computation.1 | async-start | bytes 1048576 | tf_op jit(solution)/shard_map/all_to_all | solution.py:346
  83.2 13.0 %collective-permute-start.9 = (bf16[8,8192]{1,0:T(8,128)(2,1)}, bf16[8,8192]{1,0:T(8,128)(2,1)S(1)}, u32[]{:S(2)}, u32[]{:S(2)}) collective-permute-start(bf16[8,8192]{1,0:T(8,128)(2,1)} %get-tuple-element.51), channel_id=1, source_target_pairs={{0,4},{1,5},{2,6},{3,7},{4,0},{5,1},{6,2},{7,3},{8,12},{9,13},{10,... | collective-permute-start | bytes 393224 | tf_op jit(solution)/shard_map/ppermute | solution.py:414
  90.0 1.0 copy-start.11
  91.0 0.9 copy-start.12
  94.5 6.9 %copy-start.15 = (s32[16,2]{0,1:T(2,128)S(1)}, s32[16,2]{0,1:T(2,128)}, u32[]{:S(2)}) copy-start(s32[16,2]{0,1:T(2,128)} %param.17) | copy-start | bytes 388
  94.5 7.6 %copy-start.16 = (f32[16,2]{0,1:T(2,128)S(1)}, f32[16,2]{0,1:T(2,128)}, u32[]{:S(2)}) copy-start(f32[16,2]{0,1:T(2,128)} %param.18) | copy-start | bytes 388
  96.2 6.5 %copy-start.9 = (bf16[8,8192]{1,0:T(8,128)(2,1)}, bf16[8,8192]{1,0:T(8,128)(2,1)S(1)}, u32[]{:S(2)}) copy-start(bf16[8,8192]{1,0:T(8,128)(2,1)S(1)} %collective-permute-done.9.refs_7_.refs_4_) | copy-start | bytes 393220
  98.9 13.9 %collective-permute-start.10 = (f32[512,256]{1,0:T(8,128)S(1)}, f32[512,256]{1,0:T(8,128)S(1)}, u32[]{:S(2)}, u32[]{:S(2)}) collective-permute-start(f32[512,256]{1,0:T(8,128)S(1)} %shard_map.130), channel_id=1, source_target_pairs={{0,8},{8,0},{16,24},{24,16},{32,40},{40,32},{48,56},{56,48},{64,72... | collective-permute-start | bytes 1572872 | tf_op jit(solution)/shard_map/ppermute | solution.py:329
  109.2 0.7 copy-start.13
  109.9 2.9 %copy-start.14 = (f32[512,128]{1,0:T(8,128)S(1)}, f32[512,128]{1,0:T(8,128)}, u32[]{:S(2)}) copy-start(f32[512,128]{1,0:T(8,128)} %copy-done.13) | copy-start | bytes 786436

commit v6 on v5

v6 whole, which is shorter than its diff:
```python
import math

import jax
import jax.numpy as jnp
from jax import lax
from jax.experimental import pallas as pl
from jax.experimental.pallas import tpu as pltpu
from jax.sharding import PartitionSpec as P

HD = 128
L = 128
MH = 16
NCTX = 64
QH = 4
CAP = 4
LOG2E = 1.4426950408889634
F32 = jnp.float32
BF16 = jnp.bfloat16
VM = pl.BlockSpec(memory_space=pltpu.VMEM)
SM = pl.BlockSpec(memory_space=pltpu.SMEM)
TILE = pl.BlockSpec((8, 128), lambda i: (0, 0))


GRANT = 62


def params(mib=GRANT):
    return pltpu.CompilerParams(vmem_limit_bytes=mib * 2**20)


def full(shape):
    return pl.BlockSpec(shape, lambda i: (0,) * len(shape))


def cost(flops, nbytes):
    return pl.CostEstimate(flops=flops, bytes_accessed=nbytes, transcendentals=0)


def tri(lower):
    r = lax.broadcasted_iota(jnp.int32, (L, L), 0)
    c = lax.broadcasted_iota(jnp.int32, (L, L), 1)
    return (c <= r) if lower else (r <= c)


def row_cumulative(decay):
    return jnp.dot(
        decay, tri(False).astype(F32), precision=lax.Precision.HIGHEST, preferred_element_type=F32
    )


def col_cumulative(decay):
    return lax.dot_general(
        tri(True).astype(F32),
        decay,
        (((1,), (1,)), ((), ())),
        precision=lax.Precision.HIGHEST,
        preferred_element_type=F32,
    )


PIECE = 16
KV = 2 * PIECE
SL = 32
CHUNK = 2 * KV + SL + 8


def send_kernel(x_ref, b_ref, d_ref, k_ref, v_ref, o_ref):
    cum = row_cumulative(d_ref[...])
    tail = jnp.exp(cum[:, L - 1 :] - cum)
    block_decay = jnp.exp(cum[:, L - 1 :])
    bt = b_ref[...].astype(F32).T
    row = lax.broadcasted_iota(jnp.int32, (8, L), 0)
    pieces = L // PIECE
    for h in range(MH):
        wb = (tail[h : h + 1, :] * bt).astype(BF16)
        s = jnp.dot(wb, x_ref[:, h * HD : (h + 1) * HD], preferred_element_type=F32)
        d = jnp.broadcast_to(block_decay[h : h + 1, :], (8, L))
        hi = d.astype(BF16).astype(F32)
        mid = (d - hi).astype(BF16).astype(F32)
        lo = d - hi - mid
        terms = jnp.where(row == 0, hi, jnp.where(row == 1, mid, jnp.where(row == 2, lo, 0.0)))
        for q in range(4):
            j = h * 4 + q
            for turn in range(2):
                at = (j + turn * pieces // 2) % pieces * PIECE
                o_ref[j, turn * KV : turn * KV + PIECE, :] = k_ref[at : at + PIECE, :]
                o_ref[j, turn * KV + PIECE : (turn + 1) * KV, :] = v_ref[at : at + PIECE, :]
            o_ref[j, 2 * KV : CHUNK, :] = jnp.concatenate(
                [s[q * SL : (q + 1) * SL], terms], axis=0
            ).astype(BF16)


def chunks_to_send(x_in, b_in, decay_log, k_in, v_in):
    return pl.pallas_call(
        send_kernel,
        out_shape=jax.ShapeDtypeStruct((NCTX, CHUNK, HD), BF16),
        in_specs=[VM] * 5,
        out_specs=VM,
        compiler_params=params(),
        cost_estimate=cost(1 << 26, 1 << 21),
    )(x_in, b_in, decay_log, k_in, v_in)


def take_kernel(s_ref, *refs):
    own_ref, opposite_ref = refs[-2:]
    own_ref[...] = s_ref[:, :KV, :]
    opposite_ref[...] = s_ref[:, KV : 2 * KV, :]


def take_received(received, after):
    piece = (NCTX, KV, HD)
    return pl.pallas_call(
        take_kernel,
        grid=(1,),
        out_shape=[jax.ShapeDtypeStruct(piece, BF16)] * 2,
        in_specs=[pl.BlockSpec((NCTX, 2 * KV, HD), lambda i: (0, 0, 0))] + [TILE] * len(after),
        out_specs=[full(piece)] * 2,
        compiler_params=params(),
        cost_estimate=cost(1 << 20, 1 << 21),
    )(received, *after)


def scan_kernel(s_ref, *refs):
    o_ref = refs[-1]

    def step(k, e):
        o_ref[k] = e.astype(BF16)
        block = s_ref[k, 2 * KV : CHUNK, :].astype(F32)
        d = block[SL : SL + 1] + block[SL + 1 : SL + 2] + block[SL + 2 : SL + 3]
        return d * e + block[:SL]

    lax.fori_loop(0, NCTX, step, jnp.zeros((SL, HD), F32), unroll=8)


def scan_states(received, after):
    return pl.pallas_call(
        scan_kernel,
        grid=(1,),
        out_shape=jax.ShapeDtypeStruct((NCTX, SL, HD), BF16),
        in_specs=[full(received.shape)] + [TILE] * len(after),
        out_specs=full((NCTX, SL, HD)),
        compiler_params=params(),
        cost_estimate=cost(1 << 20, 1 << 21),
    )(received, *after)


def local_kernel(x_ref, b_ref, c_ref, d_ref, o_ref, token_ref):
    token_ref[...] = jnp.zeros((8, HD), F32)
    cum = row_cumulative(d_ref[...])
    cum_col = col_cumulative(d_ref[...])
    cross = lax.dot_general(
        c_ref[...], b_ref[...], (((1,), (1,)), ((), ())), preferred_element_type=F32
    )
    mask = tri(True)
    for h in range(MH):
        gap = jnp.where(mask, cum_col[:, h : h + 1] - cum[h : h + 1, :], -1e30)
        w = (jnp.exp(gap) * cross).astype(BF16)
        o_ref[:, h * HD : (h + 1) * HD] = jnp.dot(
            w, x_ref[:, h * HD : (h + 1) * HD], preferred_element_type=F32
        )


TOKEN = jax.ShapeDtypeStruct((8, HD), F32)


def local_part(x_in, b_in, c_in, decay_log):
    return pl.pallas_call(
        local_kernel,
        out_shape=[jax.ShapeDtypeStruct((L, MH * HD), F32), TOKEN],
        in_specs=[VM] * 4,
        out_specs=[VM] * 2,
        compiler_params=params(),
        cost_estimate=cost(1 << 28, 1 << 21),
    )(x_in, b_in, c_in, decay_log)


JOIN_COST = 1 << 26


JOIN_HEADS = 4


def join_kernel(l_ref, e_ref, c_ref, d_ref, o_ref):
    cum = col_cumulative(d_ref[...])
    head = lax.broadcasted_iota(jnp.int32, cum.shape, 1)
    c = c_ref[...]
    for i in range(JOIN_HEADS):
        h = pl.program_id(0) * JOIN_HEADS + i
        grow = jnp.exp(jnp.sum(jnp.where(head == h, cum, 0.0), axis=1, keepdims=True))
        cols = slice(i * HD, (i + 1) * HD)
        readout = jnp.dot(c, e_ref[cols, :], preferred_element_type=F32)
        o_ref[:, cols] = (l_ref[:, cols] + grow * readout).astype(BF16)


def join_mamba(local, entering, c_in, decay_log):
    wide = JOIN_HEADS * HD
    return pl.pallas_call(
        join_kernel,
        grid=(MH // JOIN_HEADS,),
        out_shape=jax.ShapeDtypeStruct((L, MH * HD), BF16),
        in_specs=[
            pl.BlockSpec((L, wide), lambda i: (0, i)),
            pl.BlockSpec((wide, HD), lambda i: (i, 0)),
            full(c_in.shape),
            full(decay_log.shape),
        ],
        out_specs=pl.BlockSpec((L, wide), lambda i: (0, i)),
        compiler_params=params(),
        cost_estimate=cost(JOIN_COST, 1 << 21),
    )(local, entering, c_in, decay_log)


ROWS = QH * L
SCALE2 = LOG2E / math.sqrt(HD)


def stacked_queries(q_ref):
    return jnp.concatenate([q_ref[:, g * HD : (g + 1) * HD] for g in range(QH)], axis=0)


def accumulate(state, s, v):
    m_old, total, acc = state
    m = jnp.maximum(m_old, jnp.max(s, axis=1, keepdims=True))
    factor = jnp.exp2((m_old - m) * SCALE2)
    p = jnp.exp2((s - m) * SCALE2)
    part = p[:, :L]
    for j in range(1, p.shape[1] // L):
        part = part + p[:, j * L : (j + 1) * L]
    added = jnp.dot(p.astype(BF16), v, preferred_element_type=F32)
    return m, total * factor + part, acc * factor + added


def scores(q, k):
    return lax.dot_general(q, k, (((1,), (1,)), ((), ())), preferred_element_type=F32)


def packed(m, total):
    lane = lax.broadcasted_iota(jnp.int32, (ROWS, L), 1)
    return jnp.where(lane < L // 2, m, jnp.sum(total, axis=1, keepdims=True))


def unpacked(ref, at=0):
    lane = lax.broadcasted_iota(jnp.int32, (ROWS, L), 1)
    return ref[:, at : at + 1], jnp.where(lane == 0, ref[:, at + L - 1 : at + L], 0.0)


def open_kernel(q_ref, q2_ref, k_ref, v_ref, _, s_ref, s2_ref, ml_ref, a_ref, token_ref):
    token_ref[...] = jnp.zeros((8, HD), F32)
    q = stacked_queries(q_ref)
    s_ref[...] = q
    s2_ref[...] = stacked_queries(q2_ref)
    s = scores(q, k_ref[...])
    t = lax.broadcasted_iota(jnp.int32, s.shape, 0) % L
    u = lax.broadcasted_iota(jnp.int32, s.shape, 1)
    s = jnp.where(u <= t, s, -1e30)
    m = jnp.max(s, axis=1, keepdims=True)
    p = jnp.exp2((s - m) * SCALE2)
    ml_ref[...] = packed(m, p)
    a_ref[...] = jnp.dot(p.astype(BF16), v_ref[...], preferred_element_type=F32)


PART = jax.ShapeDtypeStruct((ROWS, L), F32)


def open_attention(q_in, q_other, k_in, v_in, after):
    return pl.pallas_call(
        open_kernel,
        out_shape=[jax.ShapeDtypeStruct((ROWS, HD), BF16)] * 2 + [PART] * 2 + [TOKEN],
        in_specs=[VM] * 5,
        out_specs=[VM] * 5,
        compiler_params=params(),
        cost_estimate=cost(1 << 27, 1 << 20),
    )(q_in, q_other, k_in, v_in, after)


def go_on(me, q, state, sets):
    keys = NCTX * PIECE
    shard = lax.broadcasted_iota(jnp.int32, (1, keys), 1) // PIECE
    bias = jnp.where(shard < me, 0.0, -1e30)
    for ref in sets:
        k = ref[:, 0:PIECE, :].reshape(keys, HD)
        v = ref[:, PIECE:KV, :].reshape(keys, HD)
        state = accumulate(state, scores(q, k) + bias, v)
    return state


def early_kernel(me_ref, q_ref, q2_ref, ml_ref, a_ref, *refs):
    sets, (ml1_ref, a1_ref, ml2_ref, a2_ref) = refs[:2], refs[2:]
    me = me_ref[0]
    m, total, acc = go_on(me, q_ref[...], (*unpacked(ml_ref), a_ref[...]), sets)
    ml1_ref[...] = packed(m, total)
    a1_ref[...] = acc
    none = jnp.full((ROWS, 1), -1e30, F32), jnp.zeros((ROWS, L), F32), jnp.zeros((ROWS, HD), F32)
    m, total, acc = go_on(me ^ 1, q2_ref[...], none, sets)
    ml2_ref[...] = packed(m, total)
    a2_ref[...] = acc


def early_attention(me, q_own, q_other, ml, acc, sets):
    return pl.pallas_call(
        early_kernel,
        out_shape=[PART] * 4,
        in_specs=[SM] + [VM] * 6,
        out_specs=[VM] * 4,
        compiler_params=params(),
        cost_estimate=cost(1 << 29, 1 << 22),
    )(me, q_own, q_other, ml, acc, *sets)


def other_kernel(me_ref, q_ref, ml_ref, a_ref, r_ref, l_ref, o_ref):
    state = (*unpacked(ml_ref), a_ref[...])
    m, total, acc = go_on(me_ref[0] ^ 1, q_ref[...], state, (r_ref, l_ref))
    o_ref[:, :HD] = acc
    o_ref[:, HD:] = packed(m, total)


def own_kernel(me_ref, q_ref, ml_ref, a_ref, r_ref, l_ref, mlo_ref, ao_ref):
    state = (*unpacked(ml_ref), a_ref[...])
    m, total, acc = go_on(me_ref[0], q_ref[...], state, (r_ref, l_ref))
    mlo_ref[...] = packed(m, total)
    ao_ref[...] = acc


def late_attention(kernel, outs, me, queries, ml, acc, sets):
    return pl.pallas_call(
        kernel,
        out_shape=outs,
        in_specs=[SM] + [VM] * 5,
        out_specs=[VM] * len(outs),
        compiler_params=params(),
        cost_estimate=cost(1 << 28, 1 << 21),
    )(me, queries, ml, acc, *sets)


def merge_kernel(ml_ref, a_ref, p_ref, o_ref):
    m1, m2 = ml_ref[:, :1], p_ref[:, HD : HD + 1]
    m = jnp.maximum(m1, m2)
    f1, f2 = jnp.exp2((m1 - m) * SCALE2), jnp.exp2((m2 - m) * SCALE2)
    total = ml_ref[:, L - 1 :] * f1 + p_ref[:, HD + L - 1 :] * f2
    out = (a_ref[...] * f1 + p_ref[:, :HD] * f2) / total
    for g in range(QH):
        o_ref[:, g * HD : (g + 1) * HD] = out[g * L : (g + 1) * L].astype(BF16)


def merge_attention(ml, acc, part):
    return pl.pallas_call(
        merge_kernel,
        out_shape=jax.ShapeDtypeStruct((L, QH * HD), BF16),
        in_specs=[VM] * 3,
        out_specs=VM,
        compiler_params=params(),
        cost_estimate=cost(1 << 20, 1 << 20),
    )(ml, acc, part)


CHIPS_X = 4


def along_x(step):
    pairs = []
    for i in range(NCTX):
        y, x, c = i // (2 * CHIPS_X), i // 2 % CHIPS_X, i % 2
        pairs.append((i, (y * CHIPS_X + (x + step) % CHIPS_X) * 2 + c))
    return pairs


def other_core(value):
    return lax.ppermute(value, "ctx", [(i, i ^ 1) for i in range(NCTX)])


def context_parts(x_in, b_in, c_in, decay_log, q_in, k_in, v_in, expert_out):
    me = lax.axis_index("ctx").astype(jnp.int32).reshape(1)
    chunks = chunks_to_send(x_in, b_in, decay_log, k_in, v_in)
    received = lax.all_to_all(chunks, "ctx", split_axis=0, concat_axis=0, tiled=True)
    q_other = other_core(q_in)
    local, token = local_part(x_in, b_in, c_in, decay_log)
    q_own, q_other, ml, acc, token = open_attention(q_in, q_other, k_in, v_in, token)
    blocks = expert_blocks(expert_out, [chunks.reshape(NCTX * CHUNK, HD)])
    own, opposite = take_received(received, [token, *blocks[1:]])
    right = lax.ppermute(own, "ctx", along_x(1))
    left = lax.ppermute(own, "ctx", along_x(-1))

    ml, acc, ml2, acc2 = early_attention(me, q_own, q_other, ml, acc, [own, opposite])
    entering = scan_states(received, [ml2])
    entering = lax.all_to_all(entering, "ctx", split_axis=0, concat_axis=0, tiled=True)
    mamba_out = join_mamba(local, entering.reshape(MH * L, HD), c_in, decay_log)

    sets = [right, left]
    both = jax.ShapeDtypeStruct((ROWS, HD + L), F32)
    [part] = late_attention(other_kernel, [both], me, q_other, ml2, acc2, sets)
    part = other_core(part)
    ml, acc = late_attention(own_kernel, [PART] * 2, me, q_own, ml, acc, sets)
    return mamba_out, merge_attention(ml, acc, part), blocks


def blocks_kernel(n_ties, me_ref, e_ref, *refs):
    outs = refs[n_ties:]
    for d, o_ref in enumerate(outs):
        to = lax.rem(me_ref[0] + d, len(outs))
        o_ref[...] = jnp.concatenate(
            [e_ref[0, i, to].astype(F32) for i in range(e_ref.shape[1])], axis=0
        ).astype(BF16)


def combine_kernel(me_ref, idst_ref, gatest_ref, *refs):
    rows_refs, o_ref = refs[:-1], refs[-1]
    peers = len(rows_refs)
    rows = jnp.concatenate([r[...].astype(F32) for r in rows_refs], axis=0).astype(BF16)
    owned = rows.shape[0] // (peers * CAP)
    count = idst_ref.shape[1]
    idst, gatest = idst_ref[...], gatest_ref[...]
    t = lax.broadcasted_iota(jnp.int32, (count, count), 0)
    u = lax.broadcasted_iota(jnp.int32, (count, count), 1)
    place = lax.broadcasted_iota(jnp.int32, (count, rows.shape[0]), 1)

    def column(row):
        return jnp.sum(jnp.where(t == u, row, jnp.zeros_like(row)), axis=1, keepdims=True)

    out = None
    for k in range(2):
        mine = column(idst[k : k + 1, :])
        slot = jnp.zeros((count, 1), jnp.int32)
        for j in range(2):
            before = (u < t) if j >= k else (u <= t)
            same = jnp.logical_and(before, idst[j : j + 1, :] == mine)
            slot = slot + jnp.sum(same.astype(jnp.int32), axis=1, keepdims=True)
        distance = (me_ref[0] - mine // owned + peers) % peers
        number = (distance * owned + mine % owned) * CAP + slot
        pick = (place == number).astype(F32).astype(BF16)
        row = jnp.dot(pick, rows, preferred_element_type=F32)
        term = column(gatest[k : k + 1, :]) * row
        out = term if out is None else out + term
    o_ref[...] = out.astype(BF16)


def expert_blocks(expert_out, after):
    owned, peers, cap, width = expert_out.shape[1:]
    me = lax.axis_index("grp").astype(jnp.int32).reshape(1)
    def kernel(*refs):
        blocks_kernel(len(after), *refs)

    held = pl.pallas_call(
        kernel,
        out_shape=[jax.ShapeDtypeStruct((owned * cap, width), BF16)] * peers,
        grid=(1,),
        in_specs=[SM, full(expert_out.shape)] + [TILE] * len(after),
        out_specs=[full((owned * cap, width))] * peers,
        compiler_params=params(),
        cost_estimate=cost(1 << 20, 1 << 21),
    )(me, expert_out, *after)
    blocks = list(held)
    for d in sorted(range(1, peers), key=lambda d: (1, 7, 2, 6, 4, 3, 5).index(d)):
        pairs = [(i, (i + d) % peers) for i in range(peers)]
        blocks[d] = lax.ppermute(held[d], "grp", pairs)
    return blocks


def expert_part(expert_ids, gates, blocks):
    me = lax.axis_index("grp").astype(jnp.int32).reshape(1)
    peers = len(blocks)
    rows, width = blocks[0].shape
    count = expert_ids.shape[0]
    return pl.pallas_call(
        combine_kernel,
        grid=(1,),
        out_shape=jax.ShapeDtypeStruct((count, width), BF16),
        in_specs=[SM, full((2, count)), full((2, count))] + [full((rows, width))] * peers,
        out_specs=full((count, width)),
        compiler_params=params(),
        cost_estimate=cost(1 << 24, 1 << 20),
    )(me, expert_ids.T, gates.T, *blocks)


def shards(x_in, b_in, c_in, decay_log, q_in, k_in, v_in, expert_ids, gates, expert_out):
    mamba_out, attn_out, blocks = context_parts(
        x_in, b_in, c_in, decay_log, q_in, k_in, v_in, expert_out
    )
    moe_out = expert_part(expert_ids, gates, blocks)
    return (mamba_out, attn_out, moe_out)


def solution(mesh):
    return jax.shard_map(
        shards,
        mesh=mesh,
        in_specs=(
            P("ctx", "grp"),
            P("ctx", None),
            P("ctx", None),
            P("grp", "ctx"),
            P("ctx", "grp"),
            P("ctx", "grp"),
            P("ctx", "grp"),
            P(("ctx", "grp"), None),
            P(("ctx", "grp"), None),
            P("ctx", "grp", None, None, None),
        ),
        out_specs=(P("ctx", "grp"), P("ctx", "grp"), P(("ctx", "grp"), None)),
        check_vma=False,
    )
```

time: 115 us -> 121 us (1.052)
  the two profiles are of different devices: /device:TPU:67 before, /device:TPU:1 now
where the time goes in v6:
time: 121 us; the launch traced here: 120 us
  starting transfers between devices  65.9 us (54%)
  Pallas kernels  39.9 us (33%)
  waiting for transfers between devices  10 us (8%)
  local copies, waits for them, and re-layouts  3.76 us (3%)
    ppermute x7, starting transfers between devices, expert_blocks(): blocks[d] = lax.ppermute(held[d], 'grp', pairs)  31.6 us
    all_to_all x1, starting transfers between devices, context_parts(): lax.all_to_all(chunks, 'ctx', split_axis=0, concat_axis=0, tiled=True)  11.6 us
    all_to_all x1, starting transfers between devices, context_parts(): lax.all_to_all(entering, 'ctx', split_axis=0, concat_axis=0, tiled=True)  11.5 us
    pallas_call x2, Pallas kernels, late_attention(): pl.pallas_call(kernel, out_shape=outs, in_specs=[SM] + [VM] * 5, out_spec...  9.46 us
    ppermute x7, waiting for transfers between devices, expert_blocks(): blocks[d] = lax.ppermute(held[d], 'grp', pairs)  7.85 us
    pallas_call x1, Pallas kernels, early_attention(): pl.pallas_call(early_kernel, out_shape=[PART] * 4, in_specs=[SM] + [VM] *...  6.54 us
    ppermute x2, starting transfers between devices, other_core(): return lax.ppermute(value, 'ctx', [(i, i ^ 1) for i in range(NCTX)])  4.9 us
    ppermute x1, starting transfers between devices, context_parts(): left = lax.ppermute(own, 'ctx', along_x(-1))  4.4 us
  transfers between devices with their start and end apart: 13, of which 3 were waited for; matrix products, arithmetic and copies ran while one was open for 0% of the time, Pallas kernels for 27%

profile of v6, /device:TPU:1, one launch (start us, length us, event | category | flops | bytes accessed | tf_op | source)
XLA Modules:
  0.0 120.4 jit_solution(11003633820509442358)
XLA Ops:
  0.6 3.0 %shard_map.122 = bf16[64,104,128]{2,1,0:T(8,128)(2,1)} custom-call(bf16[128,2048]{1,0:T(8,128)(2,1)} %x_ref.3, bf16[128,128]{1,0:T(8,128)(2,1)} %b_ref.3, f32[16,128]{1,0:T(8,128)} %d_ref.5, bf16[128,128]{1,0:T(8,128)(2,1)} %k_ref.3, bf16[128,128]{1,0:T(8,128)(2,1)} %v_ref.3), custom_call_target="tpu_custom_call" | custom-call | flops 67108864 | bytes 2097152 | tf_op jit(solution)/shard_map/pallas_call | solution.py:94
  3.6 11.6 %all-to-all-start = ((bf16[64,104,128]{2,1,0:T(8,128)(2,1)}), bf16[64,104,128]{2,1,0:T(8,128)(2,1)S(1)}, u32[]{:S(2)}, u32[]{:S(2)}) async-start(bf16[64,104,128]{2,1,0:T(8,128)(2,1)} %shard_map.122), calls=%async_computation | async-start | bytes 3407872 | tf_op jit(solution)/shard_map/all_to_all | solution.py:374
  15.3 2.4 %collective-permute-start = (bf16[128,512]{1,0:T(8,128)(2,1)}, bf16[128,512]{1,0:T(8,128)(2,1)}, u32[]{:S(2)}, u32[]{:S(2)}) collective-permute-start(bf16[128,512]{1,0:T(8,128)(2,1)} %q_ref.1), channel_id=1, source_target_pairs={{0,8},{8,0},{16,24},{24,16},{32,40},{40,32},{48,56},{56,48},{64,72... | collective-permute-start | bytes 393224 | tf_op jit(solution)/shard_map/ppermute | solution.py:368
  17.6 2.2 %shard_map.124 = (bf16[8,8192]{1,0:T(8,128)(2,1)}, bf16[8,8192]{1,0:T(8,128)(2,1)}, bf16[8,8192]{1,0:T(8,128)(2,1)}, bf16[8,8192]{1,0:T(8,128)(2,1)}, bf16[8,819...) custom-call(s32[1]{0:T(128)} %bitcast.1.refs_0_.me_ref, ...), custom_call_target="tpu_custom_call" | custom-call | flops 1048576 | bytes 2097152 | tf_op jit(solution)/shard_map/pallas_call | solution.py:442
  19.9 4.0 %collective-permute-start.1 = (bf16[8,8192]{1,0:T(8,128)(2,1)}, bf16[8,8192]{1,0:T(8,128)(2,1)S(1)}, u32[]{:S(2)}, u32[]{:S(2)}) collective-permute-start(bf16[8,8192]{1,0:T(8,128)(2,1)} %get-tuple-element.33), channel_id=1, source_target_pairs={{0,1},{1,2},{2,3},{3,4},{4,5},{5,6},{6,7},{7,0},{8,9},{9,10},{10,1... | collective-permute-start | bytes 393224 | tf_op jit(solution)/shard_map/ppermute | solution.py:454
  23.9 5.8 %collective-permute-start.2 = (bf16[8,8192]{1,0:T(8,128)(2,1)}, bf16[8,8192]{1,0:T(8,128)(2,1)S(1)}, u32[]{:S(2)}, u32[]{:S(2)}) collective-permute-start(bf16[8,8192]{1,0:T(8,128)(2,1)} %get-tuple-element.34), channel_id=1, source_target_pairs={{0,2},{1,3},{2,4},{3,5},{4,6},{5,7},{6,0},{7,1},{8,10},{9,11},{10,... | collective-permute-start | bytes 393224 | tf_op jit(solution)/shard_map/ppermute | solution.py:454
  29.7 7.0 %collective-permute-start.3 = (bf16[8,8192]{1,0:T(8,128)(2,1)}, bf16[8,8192]{1,0:T(8,128)(2,1)}, u32[]{:S(2)}, u32[]{:S(2)}) collective-permute-start(bf16[8,8192]{1,0:T(8,128)(2,1)} %get-tuple-element.35), channel_id=1, source_target_pairs={{0,3},{1,4},{2,5},{3,6},{4,7},{5,0},{6,1},{7,2},{8,11},{9,12},{10,... | collective-permute-start | bytes 393224 | tf_op jit(solution)/shard_map/ppermute | solution.py:454
  36.7 2.8 %collective-permute-start.4 = (bf16[8,8192]{1,0:T(8,128)(2,1)}, bf16[8,8192]{1,0:T(8,128)(2,1)}, u32[]{:S(2)}, u32[]{:S(2)}) collective-permute-start(bf16[8,8192]{1,0:T(8,128)(2,1)} %get-tuple-element.36), channel_id=1, source_target_pairs={{0,4},{1,5},{2,6},{3,7},{4,0},{5,1},{6,2},{7,3},{8,12},{9,13},{10,... | collective-permute-start | bytes 393224 | tf_op jit(solution)/shard_map/ppermute | solution.py:454
  39.6 0.0 collective-permute-done.q2_ref
  39.6 6.4 %collective-permute-start.5 = (bf16[8,8192]{1,0:T(8,128)(2,1)}, bf16[8,8192]{1,0:T(8,128)(2,1)}, u32[]{:S(2)}, u32[]{:S(2)}) collective-permute-start(bf16[8,8192]{1,0:T(8,128)(2,1)} %get-tuple-element.37), channel_id=1, source_target_pairs={{0,5},{1,6},{2,7},{3,0},{4,1},{5,2},{6,3},{7,4},{8,13},{9,14},{10,... | collective-permute-start | bytes 393224 | tf_op jit(solution)/shard_map/ppermute | solution.py:454
  45.9 0.0 collective-permute-done.1.refs_1_
  46.0 0.0 copy-start.4
  46.0 3.4 %collective-permute-start.6 = (bf16[8,8192]{1,0:T(8,128)(2,1)}, bf16[8,8192]{1,0:T(8,128)(2,1)}, u32[]{:S(2)}, u32[]{:S(2)}) collective-permute-start(bf16[8,8192]{1,0:T(8,128)(2,1)} %get-tuple-element.38), channel_id=1, source_target_pairs={{0,6},{1,7},{2,0},{3,1},{4,2},{5,3},{6,4},{7,5},{8,14},{9,15},{10,... | collective-permute-start | bytes 393224 | tf_op jit(solution)/shard_map/ppermute | solution.py:454
  49.4 0.0 collective-permute-done.2.refs_2_
  49.4 0.0 copy-start.5
  49.4 2.2 %collective-permute-start.7 = (bf16[8,8192]{1,0:T(8,128)(2,1)}, bf16[8,8192]{1,0:T(8,128)(2,1)}, u32[]{:S(2)}, u32[]{:S(2)}) collective-permute-start(bf16[8,8192]{1,0:T(8,128)(2,1)} %get-tuple-element.39), channel_id=1, source_target_pairs={{0,7},{1,0},{2,1},{3,2},{4,3},{5,4},{6,5},{7,6},{8,15},{9,8},{10,9... | collective-permute-start | bytes 393224 | tf_op jit(solution)/shard_map/ppermute | solution.py:454
  51.6 2.9 %shard_map.121 = (f32[128,2048]{1,0:T(8,128)}, f32[8,128]{1,0:T(8,128)}) custom-call(bf16[128,2048]{1,0:T(8,128)(2,1)} %x_ref.3, bf16[128,128]{1,0:T(8,128)(2,1)} %b_ref.3, bf16[128,128]{1,0:T(8,128)(2,1)} %c_ref.3, f32[16,128]{1,0:T(8,128)} %d_ref.5), custom_call_target="tpu_custom_call" | custom-call | flops 268435456 | bytes 2097152 | tf_op jit(solution)/shard_map/pallas_call | solution.py:167
  54.4 2.2 %shard_map.123 = (bf16[512,128]{1,0:T(8,128)(2,1)}, bf16[512,128]{1,0:T(8,128)(2,1)}, f32[512,128]{1,0:T(8,128)}, f32[512,128]{1,0:T(8,128)}, f32[8,128]{1,0:T(8,128)}) custom-call(bf16[128,512]{1,0:T(8,128)(2,1)} %q_ref.1, bf16[128,512]{1,0:T(8,128)(2,1)} %collective-permute-done.q2_ref, bf16[128,128]{1,0:T(8,128)(2,1)} %k_ref.3, bf16[128,128]{1,0:T(8,128)(2,1)} %v_ref.3, ...), custom_call_target="tpu_custom_call" | custom-call | flops 134217728 | bytes 1048576 | tf_op jit(solution)/shard_map/pallas_call | solution.py:266
  56.6 0.0 collective-permute-done.3.refs_3_
  56.6 0.0 collective-permute-done.4.refs_4_
  56.6 0.0 collective-permute-done.5.refs_5_
  56.6 7.6 %collective-permute-done.6.refs_6_ = bf16[8,8192]{1,0:T(8,128)(2,1)} collective-permute-done((bf16[8,8192]{1,0:T(8,128)(2,1)}, bf16[8,8192]{1,0:T(8,128)(2,1)}, u32[]{:S(2)}, u32[]{:S(2)}) %collective-permute-start.6) | collective-permute-done | bytes 131104 | tf_op jit(solution)/shard_map/ppermute | solution.py:454
  64.2 0.3 collective-permute-done.7.refs_7_
  64.5 0.0 all-to-all-done.s_ref
  64.5 0.0 copy-done.4
  64.5 0.0 copy-done.5
  64.5 1.2 copy-done
  65.7 2.2 %shard_map.125 = (bf16[64,32,128]{2,1,0:T(8,128)(2,1)}, bf16[64,32,128]{2,1,0:T(8,128)(2,1)}) custom-call(bf16[64,104,128]{2,1,0:T(8,128)(2,1)} %copy-done, f32[8,128]{1,0:T(8,128)} %get-tuple-element.32.refs_0_, bf16[8,8192]{1,0:T(8,128)(2,1)} %copy-done.4, bf16[8,8192]{1,0:T(8,128)(2,1)} %copy-done.5, bf16[8,8192]{1,0:T(8,128)(2,1)} %collective-permute-done.3.refs_3_, ...), custom_call_target="tpu_custom_call" | custom-call | flops 1048576 | bytes 2097152 | tf_op jit(solution)/shard_map/pallas_call | solution.py:112
  67.9 4.4 %collective-permute-start.9 = (bf16[64,32,128]{2,1,0:T(8,128)(2,1)}, bf16[64,32,128]{2,1,0:T(8,128)(2,1)S(1)}, u32[]{:S(2)}, u32[]{:S(2)}) collective-permute-start(bf16[64,32,128]{2,1,0:T(8,128)(2,1)} %get-tuple-element.40.refs_0_), channel_id=1, source_target_pairs={{0,48},{8,56},{16,0},{24,8},{32,16},{40,24},{48,32},{56,40},{64,11... | collective-permute-start | bytes 1572872 | tf_op jit(solution)/shard_map/ppermute | solution.py:381
  72.3 1.9 %collective-permute-start.8 = (bf16[64,32,128]{2,1,0:T(8,128)(2,1)}, bf16[64,32,128]{2,1,0:T(8,128)(2,1)S(1)}, u32[]{:S(2)}, u32[]{:S(2)}) collective-permute-start(bf16[64,32,128]{2,1,0:T(8,128)(2,1)} %get-tuple-element.40.refs_0_), channel_id=1, source_target_pairs={{0,16},{8,24},{16,32},{24,40},{32,48},{40,56},{48,0},{56,8},{64,80... | collective-permute-start | bytes 1572872 | tf_op jit(solution)/shard_map/ppermute | solution.py:380
  74.3 6.5 %shard_map.126 = (f32[512,128]{1,0:T(8,128)}, f32[512,128]{1,0:T(8,128)}, f32[512,128]{1,0:T(8,128)}, f32[512,128]{1,0:T(8,128)}) custom-call(s32[1]{0:T(128)} %bitcast.me_ref, bf16[512,128]{1,0:T(8,128)(2,1)} %get-tuple-element.28.q_ref, bf16[512,128]{1,0:T(8,128)(2,1)} %get-tuple-element.29.q2_ref.q_ref, f32[512,128]{1,0:T(8,128)} %get-tuple-element.30.ml_ref, ...), custom_call_target="tpu_custom_call" | custom-call | flops 536870912 | bytes 4194304 | tf_op jit(solution)/shard_map/pallas_call | solution.py:300
  80.8 2.4 %shard_map.127 = bf16[64,32,128]{2,1,0:T(8,128)(2,1)} custom-call(bf16[64,104,128]{2,1,0:T(8,128)(2,1)} %copy-done, f32[512,128]{1,0:T(8,128)} %get-tuple-element.42.refs_0_.ml_ref), custom_call_target="tpu_custom_call" | custom-call | flops 1048576 | bytes 2097152 | tf_op jit(solution)/shard_map/pallas_call | solution.py:136
  83.2 11.5 %all-to-all-start.1 = ((bf16[64,32,128]{2,1,0:T(8,128)(2,1)}), bf16[64,32,128]{2,1,0:T(8,128)(2,1)S(1)}, u32[]{:S(2)}, u32[]{:S(2)}) async-start(bf16[64,32,128]{2,1,0:T(8,128)(2,1)} %shard_map.127), calls=%async_computation.1 | async-start | bytes 1048576 | tf_op jit(solution)/shard_map/all_to_all | solution.py:385
  94.8 0.0 collective-permute-done.9.l_ref
  94.8 0.0 collective-permute-done.8.r_ref
  94.8 0.0 copy-start.2
  94.8 0.8 copy-done.1
  95.6 0.2 copy-done.2
  95.7 4.7 %shard_map.130 = f32[512,256]{1,0:T(8,128)} custom-call(s32[1]{0:T(128)} %bitcast.me_ref, bf16[512,128]{1,0:T(8,128)(2,1)} %get-tuple-element.29.q2_ref.q_ref, f32[512,128]{1,0:T(8,128)} %get-tuple-element.42.refs_0_.ml_ref, f32[512,128]{1,0:T(8,128)} %get-tuple-element.47.a_ref, bf16[64,32,128]{2,1,0:T(8,128)(2,1)} %copy-done.2, bf16[64,32,128]{2,1,0:T(8,128)(2,1)} %copy-done.1), custom_call_target="tpu_custom_call" | custom-call | flops 268435456 | bytes 2097152 | tf_op jit(solution)/shard_map/pallas_call | solution.py:325
  100.5 2.5 %collective-permute-start.10 = (f32[512,256]{1,0:T(8,128)}, f32[512,256]{1,0:T(8,128)S(1)}, u32[]{:S(2)}, u32[]{:S(2)}) collective-permute-start(f32[512,256]{1,0:T(8,128)} %shard_map.130), channel_id=1, source_target_pairs={{0,8},{8,0},{16,24},{24,16},{32,40},{40,32},{48,56},{56,48},{64,72... | collective-permute-start | bytes 1572872 | tf_op jit(solution)/shard_map/ppermute | solution.py:368
  103.0 2.6 %shard_map.132 = bf16[16,8192]{1,0:T(8,128)(2,1)} custom-call(s32[1]{0:T(128)} %bitcast.1.refs_0_.me_ref, s32[2,16]{1,0:T(2,128)} %bitcast.8, f32[2,16]{1,0:T(2,128)} %bitcast.9, bf16[8,8192]{1,0:T(8,128)(2,1)} %get-tuple-element.48.refs_0_, bf16[8,8192]{1,0:T(8,128)(2,1)} %copy-done.4, bf16[8,8192]{1,0:T(8,128)(2,1)} %copy-done.5, ...), custom_call_target="tpu_custom_call" | custom-call | flops 16777216 | bytes 1048576 | tf_op jit(solution)/shard_map/pallas_call | solution.py:463
  105.6 4.7 %shard_map.129 = (f32[512,128]{1,0:T(8,128)}, f32[512,128]{1,0:T(8,128)}) custom-call(s32[1]{0:T(128)} %bitcast.me_ref, bf16[512,128]{1,0:T(8,128)(2,1)} %get-tuple-element.28.q_ref, f32[512,128]{1,0:T(8,128)} %get-tuple-element.43.ml_ref, f32[512,128]{1,0:T(8,128)} %get-tuple-element.44.a_ref, bf16[64,32,128]{2,1,0:T(8,128)(2,1)} %copy-done.2, ...), custom_call_target="tpu_custom_call" | custom-call | flops 268435456 | bytes 2097152 | tf_op jit(solution)/shard_map/pallas_call | solution.py:325
  110.3 2.1 %all-to-all-done.1 = bf16[64,32,128]{2,1,0:T(8,128)(2,1)S(1)} async-done(((bf16[64,32,128]{2,1,0:T(8,128)(2,1)}), bf16[64,32,128]{2,1,0:T(8,128)(2,1)S(1)}, u32[]{:S(2)}, u32[]{:S(2)}) %all-to-all-start.1) | async-done | bytes 524320 | tf_op jit(solution)/shard_map/all_to_all | solution.py:385
  112.5 0.8 copy-done.3
  113.3 4.1 %shard_map.128 = bf16[128,2048]{1,0:T(8,128)(2,1)} custom-call(f32[128,2048]{1,0:T(8,128)} %get-tuple-element.26.l_ref, bf16[2048,128]{1,0:T(8,128)(2,1)} %bitcast.7, bf16[128,128]{1,0:T(8,128)(2,1)} %c_ref.3, f32[16,128]{1,0:T(8,128)} %d_ref.5), custom_call_target="tpu_custom_call" | custom-call | flops 67108864 | bytes 2097152 | tf_op jit(solution)/shard_map/pallas_call | solution.py:197
  117.3 0.0 collective-permute-done.10.p_ref
  117.4 0.8 copy-done.6
  118.2 2.3 %shard_map.131 = bf16[128,512]{1,0:T(8,128)(2,1)} custom-call(f32[512,128]{1,0:T(8,128)} %get-tuple-element.45.ml_ref, f32[512,128]{1,0:T(8,128)} %get-tuple-element.46.a_ref, f32[512,256]{1,0:T(8,128)} %copy-done.6), custom_call_target="tpu_custom_call" | custom-call | flops 1048576 | bytes 1048576 | tf_op jit(solution)/shard_map/pallas_call | solution.py:346
  (4 shorter events, 0.0 us)
Async XLA Ops:
  3.6 60.8 %all-to-all-start = ((bf16[64,104,128]{2,1,0:T(8,128)(2,1)}), bf16[64,104,128]{2,1,0:T(8,128)(2,1)S(1)}, u32[]{:S(2)}, u32[]{:S(2)}) async-start(bf16[64,104,128]{2,1,0:T(8,128)(2,1)} %shard_map.122), calls=%async_computation | async-start | bytes 3407872 | tf_op jit(solution)/shard_map/all_to_all | solution.py:374
  15.3 24.3 %collective-permute-start = (bf16[128,512]{1,0:T(8,128)(2,1)}, bf16[128,512]{1,0:T(8,128)(2,1)}, u32[]{:S(2)}, u32[]{:S(2)}) collective-permute-start(bf16[128,512]{1,0:T(8,128)(2,1)} %q_ref.1), channel_id=1, source_target_pairs={{0,8},{8,0},{16,24},{24,16},{32,40},{40,32},{48,56},{56,48},{64,72... | collective-permute-start | bytes 393224 | tf_op jit(solution)/shard_map/ppermute | solution.py:368
  19.9 26.1 %collective-permute-start.1 = (bf16[8,8192]{1,0:T(8,128)(2,1)}, bf16[8,8192]{1,0:T(8,128)(2,1)S(1)}, u32[]{:S(2)}, u32[]{:S(2)}) collective-permute-start(bf16[8,8192]{1,0:T(8,128)(2,1)} %get-tuple-element.33), channel_id=1, source_target_pairs={{0,1},{1,2},{2,3},{3,4},{4,5},{5,6},{6,7},{7,0},{8,9},{9,10},{10,1... | collective-permute-start | bytes 393224 | tf_op jit(solution)/shard_map/ppermute | solution.py:454
  23.9 25.5 %collective-permute-start.2 = (bf16[8,8192]{1,0:T(8,128)(2,1)}, bf16[8,8192]{1,0:T(8,128)(2,1)S(1)}, u32[]{:S(2)}, u32[]{:S(2)}) collective-permute-start(bf16[8,8192]{1,0:T(8,128)(2,1)} %get-tuple-element.34), channel_id=1, source_target_pairs={{0,2},{1,3},{2,4},{3,5},{4,6},{5,7},{6,0},{7,1},{8,10},{9,11},{10,... | collective-permute-start | bytes 393224 | tf_op jit(solution)/shard_map/ppermute | solution.py:454
  29.7 26.9 %collective-permute-start.3 = (bf16[8,8192]{1,0:T(8,128)(2,1)}, bf16[8,8192]{1,0:T(8,128)(2,1)}, u32[]{:S(2)}, u32[]{:S(2)}) collective-permute-start(bf16[8,8192]{1,0:T(8,128)(2,1)} %get-tuple-element.35), channel_id=1, source_target_pairs={{0,3},{1,4},{2,5},{3,6},{4,7},{5,0},{6,1},{7,2},{8,11},{9,12},{10,... | collective-permute-start | bytes 393224 | tf_op jit(solution)/shard_map/ppermute | solution.py:454
  36.7 19.9 %collective-permute-start.4 = (bf16[8,8192]{1,0:T(8,128)(2,1)}, bf16[8,8192]{1,0:T(8,128)(2,1)}, u32[]{:S(2)}, u32[]{:S(2)}) collective-permute-start(bf16[8,8192]{1,0:T(8,128)(2,1)} %get-tuple-element.36), channel_id=1, source_target_pairs={{0,4},{1,5},{2,6},{3,7},{4,0},{5,1},{6,2},{7,3},{8,12},{9,13},{10,... | collective-permute-start | bytes 393224 | tf_op jit(solution)/shard_map/ppermute | solution.py:454
  39.6 17.1 %collective-permute-start.5 = (bf16[8,8192]{1,0:T(8,128)(2,1)}, bf16[8,8192]{1,0:T(8,128)(2,1)}, u32[]{:S(2)}, u32[]{:S(2)}) collective-permute-start(bf16[8,8192]{1,0:T(8,128)(2,1)} %get-tuple-element.37), channel_id=1, source_target_pairs={{0,5},{1,6},{2,7},{3,0},{4,1},{5,2},{6,3},{7,4},{8,13},{9,14},{10,... | collective-permute-start | bytes 393224 | tf_op jit(solution)/shard_map/ppermute | solution.py:454
  46.0 18.5 %copy-start.4 = (bf16[8,8192]{1,0:T(8,128)(2,1)}, bf16[8,8192]{1,0:T(8,128)(2,1)S(1)}, u32[]{:S(2)}) copy-start(bf16[8,8192]{1,0:T(8,128)(2,1)S(1)} %collective-permute-done.1.refs_1_) | copy-start | bytes 393220
  46.0 18.2 %collective-permute-start.6 = (bf16[8,8192]{1,0:T(8,128)(2,1)}, bf16[8,8192]{1,0:T(8,128)(2,1)}, u32[]{:S(2)}, u32[]{:S(2)}) collective-permute-start(bf16[8,8192]{1,0:T(8,128)(2,1)} %get-tuple-element.38), channel_id=1, source_target_pairs={{0,6},{1,7},{2,0},{3,1},{4,2},{5,3},{6,4},{7,5},{8,14},{9,15},{10,... | collective-permute-start | bytes 393224 | tf_op jit(solution)/shard_map/ppermute | solution.py:454
  49.4 15.1 %copy-start.5 = (bf16[8,8192]{1,0:T(8,128)(2,1)}, bf16[8,8192]{1,0:T(8,128)(2,1)S(1)}, u32[]{:S(2)}) copy-start(bf16[8,8192]{1,0:T(8,128)(2,1)S(1)} %collective-permute-done.2.refs_2_) | copy-start | bytes 393220
  49.4 15.1 %collective-permute-start.7 = (bf16[8,8192]{1,0:T(8,128)(2,1)}, bf16[8,8192]{1,0:T(8,128)(2,1)}, u32[]{:S(2)}, u32[]{:S(2)}) collective-permute-start(bf16[8,8192]{1,0:T(8,128)(2,1)} %get-tuple-element.39), channel_id=1, source_target_pairs={{0,7},{1,0},{2,1},{3,2},{4,3},{5,4},{6,5},{7,6},{8,15},{9,8},{10,9... | collective-permute-start | bytes 393224 | tf_op jit(solution)/shard_map/ppermute | solution.py:454
  64.5 1.2 %copy-start = (bf16[64,104,128]{2,1,0:T(8,128)(2,1)}, bf16[64,104,128]{2,1,0:T(8,128)(2,1)S(1)}, u32[]{:S(2)}) copy-start(bf16[64,104,128]{2,1,0:T(8,128)(2,1)S(1)} %all-to-all-done.s_ref) | copy-start | bytes 5111812
  67.9 26.8 %collective-permute-start.9 = (bf16[64,32,128]{2,1,0:T(8,128)(2,1)}, bf16[64,32,128]{2,1,0:T(8,128)(2,1)S(1)}, u32[]{:S(2)}, u32[]{:S(2)}) collective-permute-start(bf16[64,32,128]{2,1,0:T(8,128)(2,1)} %get-tuple-element.40.refs_0_), channel_id=1, source_target_pairs={{0,48},{8,56},{16,0},{24,8},{32,16},{40,24},{48,32},{56,40},{64,11... | collective-permute-start | bytes 1572872 | tf_op jit(solution)/shard_map/ppermute | solution.py:381
  72.3 22.4 %collective-permute-start.8 = (bf16[64,32,128]{2,1,0:T(8,128)(2,1)}, bf16[64,32,128]{2,1,0:T(8,128)(2,1)S(1)}, u32[]{:S(2)}, u32[]{:S(2)}) collective-permute-start(bf16[64,32,128]{2,1,0:T(8,128)(2,1)} %get-tuple-element.40.refs_0_), channel_id=1, source_target_pairs={{0,16},{8,24},{16,32},{24,40},{32,48},{40,56},{48,0},{56,8},{64,80... | collective-permute-start | bytes 1572872 | tf_op jit(solution)/shard_map/ppermute | solution.py:380
  83.2 29.2 %all-to-all-start.1 = ((bf16[64,32,128]{2,1,0:T(8,128)(2,1)}), bf16[64,32,128]{2,1,0:T(8,128)(2,1)S(1)}, u32[]{:S(2)}, u32[]{:S(2)}) async-start(bf16[64,32,128]{2,1,0:T(8,128)(2,1)} %shard_map.127), calls=%async_computation.1 | async-start | bytes 1048576 | tf_op jit(solution)/shard_map/all_to_all | solution.py:385
  94.8 0.8 copy-start.1
  94.8 0.9 copy-start.2
  100.5 16.9 %collective-permute-start.10 = (f32[512,256]{1,0:T(8,128)}, f32[512,256]{1,0:T(8,128)S(1)}, u32[]{:S(2)}, u32[]{:S(2)}) collective-permute-start(f32[512,256]{1,0:T(8,128)} %shard_map.130), channel_id=1, source_target_pairs={{0,8},{8,0},{16,24},{24,16},{32,40},{40,32},{48,56},{56,48},{64,72... | collective-permute-start | bytes 1572872 | tf_op jit(solution)/shard_map/ppermute | solution.py:368
  112.5 0.8 copy-start.3
  117.4 0.8 copy-start.6

commit v7 on v6

--- a/solution.py
+++ b/solution.py
@@ -21,10 +21,10 @@
 TILE = pl.BlockSpec((8, 128), lambda i: (0, 0))
 
 
-GRANT = 62
-
-
-def params(mib=GRANT):
+LARGE, SMALL = 60, 24
+
+
+def params(mib=SMALL):
     return pltpu.CompilerParams(vmem_limit_bytes=mib * 2**20)
 
 
@@ -96,32 +96,15 @@
         out_shape=jax.ShapeDtypeStruct((NCTX, CHUNK, HD), BF16),
         in_specs=[VM] * 5,
         out_specs=VM,
-        compiler_params=params(),
+        compiler_params=params(LARGE),
         cost_estimate=cost(1 << 26, 1 << 21),
     )(x_in, b_in, decay_log, k_in, v_in)
 
 
 def take_kernel(s_ref, *refs):
-    own_ref, opposite_ref = refs[-2:]
+    own_ref, opposite_ref, o_ref = refs[-3:]
     own_ref[...] = s_ref[:, :KV, :]
     opposite_ref[...] = s_ref[:, KV : 2 * KV, :]
-
-
-def take_received(received, after):
-    piece = (NCTX, KV, HD)
-    return pl.pallas_call(
-        take_kernel,
-        grid=(1,),
-        out_shape=[jax.ShapeDtypeStruct(piece, BF16)] * 2,
-        in_specs=[pl.BlockSpec((NCTX, 2 * KV, HD), lambda i: (0, 0, 0))] + [TILE] * len(after),
-        out_specs=[full(piece)] * 2,
-        compiler_params=params(),
-        cost_estimate=cost(1 << 20, 1 << 21),
-    )(received, *after)
-
-
-def scan_kernel(s_ref, *refs):
-    o_ref = refs[-1]
 
     def step(k, e):
         o_ref[k] = e.astype(BF16)
@@ -132,13 +115,17 @@
     lax.fori_loop(0, NCTX, step, jnp.zeros((SL, HD), F32), unroll=8)
 
 
-def scan_states(received, after):
-    return pl.pallas_call(
-        scan_kernel,
+def take_received(received, after):
+    return pl.pallas_call(
+        take_kernel,
+        out_shape=[
+            jax.ShapeDtypeStruct((NCTX, KV, HD), BF16),
+            jax.ShapeDtypeStruct((NCTX, KV, HD), BF16),
+            jax.ShapeDtypeStruct((NCTX, SL, HD), BF16),
+        ],
         grid=(1,),
-        out_shape=jax.ShapeDtypeStruct((NCTX, SL, HD), BF16),
         in_specs=[full(received.shape)] + [TILE] * len(after),
-        out_specs=full((NCTX, SL, HD)),
+        out_specs=[full((NCTX, KV, HD)), full((NCTX, KV, HD)), full((NCTX, SL, HD))],
         compiler_params=params(),
         cost_estimate=cost(1 << 20, 1 << 21),
     )(received, *after)
@@ -169,7 +156,7 @@
         out_shape=[jax.ShapeDtypeStruct((L, MH * HD), F32), TOKEN],
         in_specs=[VM] * 4,
         out_specs=[VM] * 2,
-        compiler_params=params(),
+        compiler_params=params(LARGE),
         cost_estimate=cost(1 << 28, 1 << 21),
     )(x_in, b_in, c_in, decay_log)
 
@@ -177,35 +164,22 @@
 JOIN_COST = 1 << 26
 
 
-JOIN_HEADS = 4
-
-
 def join_kernel(l_ref, e_ref, c_ref, d_ref, o_ref):
-    cum = col_cumulative(d_ref[...])
-    head = lax.broadcasted_iota(jnp.int32, cum.shape, 1)
+    grow = jnp.exp(col_cumulative(d_ref[...]))
     c = c_ref[...]
-    for i in range(JOIN_HEADS):
-        h = pl.program_id(0) * JOIN_HEADS + i
-        grow = jnp.exp(jnp.sum(jnp.where(head == h, cum, 0.0), axis=1, keepdims=True))
-        cols = slice(i * HD, (i + 1) * HD)
+    for h in range(MH):
+        cols = slice(h * HD, (h + 1) * HD)
         readout = jnp.dot(c, e_ref[cols, :], preferred_element_type=F32)
-        o_ref[:, cols] = (l_ref[:, cols] + grow * readout).astype(BF16)
+        o_ref[:, cols] = (l_ref[:, cols] + grow[:, h : h + 1] * readout).astype(BF16)
 
 
 def join_mamba(local, entering, c_in, decay_log):
-    wide = JOIN_HEADS * HD
     return pl.pallas_call(
         join_kernel,
-        grid=(MH // JOIN_HEADS,),
         out_shape=jax.ShapeDtypeStruct((L, MH * HD), BF16),
-        in_specs=[
-            pl.BlockSpec((L, wide), lambda i: (0, i)),
-            pl.BlockSpec((wide, HD), lambda i: (i, 0)),
-            full(c_in.shape),
-            full(decay_log.shape),
-        ],
-        out_specs=pl.BlockSpec((L, wide), lambda i: (0, i)),
-        compiler_params=params(),
+        in_specs=[VM] * 4,
+        out_specs=VM,
+        compiler_params=params(LARGE),
         cost_estimate=cost(JOIN_COST, 1 << 21),
     )(local, entering, c_in, decay_log)
 
@@ -268,7 +242,7 @@
         out_shape=[jax.ShapeDtypeStruct((ROWS, HD), BF16)] * 2 + [PART] * 2 + [TOKEN],
         in_specs=[VM] * 5,
         out_specs=[VM] * 5,
-        compiler_params=params(),
+        compiler_params=params(LARGE),
         cost_estimate=cost(1 << 27, 1 << 20),
     )(q_in, q_other, k_in, v_in, after)
 
@@ -375,13 +349,13 @@
     q_other = other_core(q_in)
     local, token = local_part(x_in, b_in, c_in, decay_log)
     q_own, q_other, ml, acc, token = open_attention(q_in, q_other, k_in, v_in, token)
-    blocks = expert_blocks(expert_out, [chunks.reshape(NCTX * CHUNK, HD)])
-    own, opposite = take_received(received, [token, *blocks[1:]])
+    blocks = expert_blocks(expert_out, [chunks.reshape(NCTX * CHUNK, HD), token])
+    arrived = sum(b[:8, :HD] for b in blocks[1:]) if len(blocks) > 1 else blocks[0][:8, :HD]
+    own, opposite, entering = take_received(received, [arrived])
     right = lax.ppermute(own, "ctx", along_x(1))
     left = lax.ppermute(own, "ctx", along_x(-1))
 
     ml, acc, ml2, acc2 = early_attention(me, q_own, q_other, ml, acc, [own, opposite])
-    entering = scan_states(received, [ml2])
     entering = lax.all_to_all(entering, "ctx", split_axis=0, concat_axis=0, tiled=True)
     mamba_out = join_mamba(local, entering.reshape(MH * L, HD), c_in, decay_log)
 
@@ -445,7 +419,7 @@
         grid=(1,),
         in_specs=[SM, full(expert_out.shape)] + [TILE] * len(after),
         out_specs=[full((owned * cap, width))] * peers,
-        compiler_params=params(),
+        compiler_params=params(LARGE),
         cost_estimate=cost(1 << 20, 1 << 21),
     )(me, expert_out, *after)
     blocks = list(held)
@@ -466,7 +440,7 @@
         out_shape=jax.ShapeDtypeStruct((count, width), BF16),
         in_specs=[SM, full((2, count)), full((2, count))] + [full((rows, width))] * peers,
         out_specs=full((count, width)),
-        compiler_params=params(),
+        compiler_params=params(LARGE),
         cost_estimate=cost(1 << 24, 1 << 20),
     )(me, expert_ids.T, gates.T, *blocks)
 

time: 121 us -> 112 us (0.926)
  Pallas kernels: 39.9 us -> 27.1 us
  waiting for transfers between devices: 10 us -> 14.9 us
  local copies, waits for them, and re-layouts: 3.76 us -> 2.25 us
    ppermute x7, waiting for transfers between devices: 7.85 us -> 12.8 us  [expert_blocks(): blocks[d] = lax.ppermute(held[d], 'grp', pairs)]
    pallas_call x3 -> x2, Pallas kernels: 8.74 us -> 3.89 us  [the longest x1 2.84 us: join_mamba(): pl.pallas_call(join_kernel, out_shape=jax.ShapeDtypeStruct((L, MH * HD),...]
    pallas_call x2, Pallas kernels: 9.46 us -> 5.06 us  [late_attention(): pl.pallas_call(kernel, out_shape=outs, in_specs=[SM] + [VM] * 5, out_spec...]
    pallas_call x1, Pallas kernels: 6.54 us -> 4.24 us  [early_attention(): pl.pallas_call(early_kernel, out_shape=[PART] * 4, in_specs=[SM] + [VM] *...]
    unnamed x14 -> x26, local copies, waits for them, and re-layouts: 3.76 us -> 2.25 us
    ppermute x1, starting transfers between devices: 1.92 us -> 3.2 us  [context_parts(): right = lax.ppermute(own, 'ctx', along_x(1))]
  transfers between devices with their start and end apart: 13 -> 13, of which waited for: 3 -> 5; matrix products, arithmetic and copies ran while one was open for 0% -> 0% of each run, Pallas kernels for 27% -> 20%
where the time goes in v7:
time: 112 us; the launch traced here: 111 us
  starting transfers between devices  65.5 us (58%)
  Pallas kernels  27.1 us (24%)
  waiting for transfers between devices  14.9 us (13%)
  local copies, waits for them, and re-layouts  2.25 us (2%)
    ppermute x7, starting transfers between devices, expert_blocks(): blocks[d] = lax.ppermute(held[d], 'grp', pairs)  31.7 us
    ppermute x7, waiting for transfers between devices, expert_blocks(): blocks[d] = lax.ppermute(held[d], 'grp', pairs)  12.8 us
    all_to_all x1, starting transfers between devices, context_parts(): lax.all_to_all(chunks, 'ctx', split_axis=0, concat_axis=0, tiled=True)  11.7 us
    all_to_all x1, starting transfers between devices, context_parts(): lax.all_to_all(entering, 'ctx', split_axis=0, concat_axis=0, tiled=True)  10.6 us
    pallas_call x2, Pallas kernels, late_attention(): pl.pallas_call(kernel, out_shape=outs, in_specs=[SM] + [VM] * 5, out_spec...  5.06 us
    ppermute x2, starting transfers between devices, other_core(): return lax.ppermute(value, 'ctx', [(i, i ^ 1) for i in range(NCTX)])  4.98 us
    pallas_call x1, Pallas kernels, early_attention(): pl.pallas_call(early_kernel, out_shape=[PART] * 4, in_specs=[SM] + [VM] *...  4.24 us
    ppermute x1, starting transfers between devices, context_parts(): left = lax.ppermute(own, 'ctx', along_x(-1))  3.28 us
  transfers between devices with their start and end apart: 13, of which 5 were waited for; matrix products, arithmetic and copies ran while one was open for 0% of the time, Pallas kernels for 20%

profile of v7, /device:TPU:1, one launch (start us, length us, event | category | flops | bytes accessed | tf_op | source)
XLA Modules:
  0.0 110.8 jit_solution(7345270202000462749)
XLA Ops:
  0.6 3.0 %shard_map.122 = bf16[64,104,128]{2,1,0:T(8,128)(2,1)} custom-call(bf16[128,2048]{1,0:T(8,128)(2,1)} %x_ref.3, bf16[128,128]{1,0:T(8,128)(2,1)} %b_ref.3, f32[16,128]{1,0:T(8,128)} %d_ref.5, bf16[128,128]{1,0:T(8,128)(2,1)} %k_ref.3, bf16[128,128]{1,0:T(8,128)(2,1)} %v_ref.3), custom_call_target="tpu_custom_call" | custom-call | flops 67108864 | bytes 2097152 | tf_op jit(solution)/shard_map/pallas_call | solution.py:94
  3.7 11.7 %all-to-all-start = ((bf16[64,104,128]{2,1,0:T(8,128)(2,1)}), bf16[64,104,128]{2,1,0:T(8,128)(2,1)S(1)}, u32[]{:S(2)}, u32[]{:S(2)}) async-start(bf16[64,104,128]{2,1,0:T(8,128)(2,1)} %shard_map.122), calls=%async_computation | async-start | bytes 3407872 | tf_op jit(solution)/shard_map/all_to_all | solution.py:348
  15.4 0.0 copy-done.11
  15.4 2.4 %collective-permute-start = (bf16[128,512]{1,0:T(8,128)(2,1)S(1)}, bf16[128,512]{1,0:T(8,128)(2,1)S(1)}, u32[]{:S(2)}, u32[]{:S(2)}) collective-permute-start(bf16[128,512]{1,0:T(8,128)(2,1)S(1)} %copy-done.11), channel_id=1, source_target_pairs={{0,8},{8,0},{16,24},{24,16},{32,40},{40,32},{48,56},{56,48},{64,72... | collective-permute-start | bytes 393224 | tf_op jit(solution)/shard_map/ppermute | solution.py:342
  17.8 2.8 %shard_map.121 = (f32[128,2048]{1,0:T(8,128)}, f32[8,128]{1,0:T(8,128)}) custom-call(bf16[128,2048]{1,0:T(8,128)(2,1)} %x_ref.3, bf16[128,128]{1,0:T(8,128)(2,1)} %b_ref.3, bf16[128,128]{1,0:T(8,128)(2,1)} %c_ref.3, f32[16,128]{1,0:T(8,128)} %d_ref.5), custom_call_target="tpu_custom_call" | custom-call | flops 268435456 | bytes 2097152 | tf_op jit(solution)/shard_map/pallas_call | solution.py:154
  20.6 0.0 collective-permute-done.q2_ref
  20.7 0.7 copy-done.12
  21.3 2.2 %shard_map.123 = (bf16[512,128]{1,0:T(8,128)(2,1)}, bf16[512,128]{1,0:T(8,128)(2,1)}, f32[512,128]{1,0:T(8,128)}, f32[512,128]{1,0:T(8,128)}, f32[8,128]{1,0:T(8,128)}) custom-call(bf16[128,512]{1,0:T(8,128)(2,1)} %q_ref.1, bf16[128,512]{1,0:T(8,128)(2,1)} %copy-done.12, bf16[128,128]{1,0:T(8,128)(2,1)} %k_ref.3, bf16[128,128]{1,0:T(8,128)(2,1)} %v_ref.3, ...), custom_call_target="tpu_custom_call" | custom-call | flops 134217728 | bytes 1048576 | tf_op jit(solution)/shard_map/pallas_call | solution.py:240
  23.5 2.2 %shard_map.124 = (bf16[8,8192]{1,0:T(8,128)(2,1)}, bf16[8,8192]{1,0:T(8,128)(2,1)}, bf16[8,8192]{1,0:T(8,128)(2,1)}, bf16[8,8192]{1,0:T(8,128)(2,1)}, bf16[8,819...) custom-call(s32[1]{0:T(128)} %bitcast.refs_0_.me_ref, ...), custom_call_target="tpu_custom_call" | custom-call | flops 1048576 | bytes 2097152 | tf_op jit(solution)/shard_map/pallas_call | solution.py:416
  25.7 4.1 %collective-permute-start.1 = (bf16[8,8192]{1,0:T(8,128)(2,1)}, bf16[8,8192]{1,0:T(8,128)(2,1)S(1)}, u32[]{:S(2)}, u32[]{:S(2)}) collective-permute-start(bf16[8,8192]{1,0:T(8,128)(2,1)} %get-tuple-element.30), channel_id=1, source_target_pairs={{0,1},{1,2},{2,3},{3,4},{4,5},{5,6},{6,7},{7,0},{8,9},{9,10},{10,1... | collective-permute-start | bytes 393224 | tf_op jit(solution)/shard_map/ppermute | solution.py:428
  29.9 5.8 %collective-permute-start.2 = (bf16[8,8192]{1,0:T(8,128)(2,1)}, bf16[8,8192]{1,0:T(8,128)(2,1)S(1)}, u32[]{:S(2)}, u32[]{:S(2)}) collective-permute-start(bf16[8,8192]{1,0:T(8,128)(2,1)} %get-tuple-element.31), channel_id=1, source_target_pairs={{0,2},{1,3},{2,4},{3,5},{4,6},{5,7},{6,0},{7,1},{8,10},{9,11},{10,... | collective-permute-start | bytes 393224 | tf_op jit(solution)/shard_map/ppermute | solution.py:428
  35.7 7.0 %collective-permute-start.3 = (bf16[8,8192]{1,0:T(8,128)(2,1)}, bf16[8,8192]{1,0:T(8,128)(2,1)S(1)}, u32[]{:S(2)}, u32[]{:S(2)}) collective-permute-start(bf16[8,8192]{1,0:T(8,128)(2,1)} %get-tuple-element.32), channel_id=1, source_target_pairs={{0,3},{1,4},{2,5},{3,6},{4,7},{5,0},{6,1},{7,2},{8,11},{9,12},{10,... | collective-permute-start | bytes 393224 | tf_op jit(solution)/shard_map/ppermute | solution.py:428
  42.7 2.8 %collective-permute-start.4 = (bf16[8,8192]{1,0:T(8,128)(2,1)}, bf16[8,8192]{1,0:T(8,128)(2,1)S(1)}, u32[]{:S(2)}, u32[]{:S(2)}) collective-permute-start(bf16[8,8192]{1,0:T(8,128)(2,1)} %get-tuple-element.33), channel_id=1, source_target_pairs={{0,4},{1,5},{2,6},{3,7},{4,0},{5,1},{6,2},{7,3},{8,12},{9,13},{10,... | collective-permute-start | bytes 393224 | tf_op jit(solution)/shard_map/ppermute | solution.py:428
  45.6 6.4 %collective-permute-start.5 = (bf16[8,8192]{1,0:T(8,128)(2,1)}, bf16[8,8192]{1,0:T(8,128)(2,1)S(1)}, u32[]{:S(2)}, u32[]{:S(2)}) collective-permute-start(bf16[8,8192]{1,0:T(8,128)(2,1)} %get-tuple-element.34), channel_id=1, source_target_pairs={{0,5},{1,6},{2,7},{3,0},{4,1},{5,2},{6,3},{7,4},{8,13},{9,14},{10,... | collective-permute-start | bytes 393224 | tf_op jit(solution)/shard_map/ppermute | solution.py:428
  51.9 0.0 collective-permute-done.1.refs_1_
  52.0 0.0 copy-start.4
  52.0 3.4 %collective-permute-start.6 = (bf16[8,8192]{1,0:T(8,128)(2,1)}, bf16[8,8192]{1,0:T(8,128)(2,1)S(1)}, u32[]{:S(2)}, u32[]{:S(2)}) collective-permute-start(bf16[8,8192]{1,0:T(8,128)(2,1)} %get-tuple-element.35), channel_id=1, source_target_pairs={{0,6},{1,7},{2,0},{3,1},{4,2},{5,3},{6,4},{7,5},{8,14},{9,15},{10,... | collective-permute-start | bytes 393224 | tf_op jit(solution)/shard_map/ppermute | solution.py:428
  55.3 0.0 collective-permute-done.2.refs_2_
  55.4 0.0 copy-start.5
  55.4 2.2 %collective-permute-start.7 = (bf16[8,8192]{1,0:T(8,128)(2,1)}, bf16[8,8192]{1,0:T(8,128)(2,1)S(1)}, u32[]{:S(2)}, u32[]{:S(2)}) collective-permute-start(bf16[8,8192]{1,0:T(8,128)(2,1)} %get-tuple-element.36), channel_id=1, source_target_pairs={{0,7},{1,0},{2,1},{3,2},{4,3},{5,4},{6,5},{7,6},{8,15},{9,8},{10,9... | collective-permute-start | bytes 393224 | tf_op jit(solution)/shard_map/ppermute | solution.py:428
  57.6 0.0 collective-permute-done.3.refs_3_
  57.6 0.0 copy-start.6
  57.6 1.0 collective-permute-done.4.refs_4_
  58.6 0.3 collective-permute-done.5.refs_5_
  58.9 11.2 %collective-permute-done.6.refs_6_ = bf16[8,8192]{1,0:T(8,128)(2,1)S(1)} collective-permute-done((bf16[8,8192]{1,0:T(8,128)(2,1)}, bf16[8,8192]{1,0:T(8,128)(2,1)S(1)}, u32[]{:S(2)}, u32[]{:S(2)}) %collective-permute-start.6) | collective-permute-done | bytes 131104 | tf_op jit(solution)/shard_map/ppermute | solution.py:428
  70.1 0.3 collective-permute-done.7.refs_7_
  70.4 0.0 copy-done.6
  70.4 0.0 copy-done.7
  70.4 0.0 copy-done.8
  70.4 0.3 copy-done.9
  70.8 0.3 copy-done.10
  71.0 0.0 all-to-all-done.s_ref
  71.0 1.1 shard_map.125
  72.1 3.2 %collective-permute-start.8 = (bf16[64,32,128]{2,1,0:T(8,128)(2,1)S(1)}, bf16[64,32,128]{2,1,0:T(8,128)(2,1)S(1)}, u32[]{:S(2)}, u32[]{:S(2)}) collective-permute-start(bf16[64,32,128]{2,1,0:T(8,128)(2,1)S(1)} %get-tuple-element.42.refs_0_), channel_id=1, source_target_pairs={{0,16},{8,24},{16,32},{24,40},{32,48},{40,56},{48,0},{56,8},{64,80... | collective-permute-start | bytes 1572872 | tf_op jit(solution)/shard_map/ppermute | solution.py:355
  75.3 3.3 %collective-permute-start.9 = (bf16[64,32,128]{2,1,0:T(8,128)(2,1)S(1)}, bf16[64,32,128]{2,1,0:T(8,128)(2,1)S(1)}, u32[]{:S(2)}, u32[]{:S(2)}) collective-permute-start(bf16[64,32,128]{2,1,0:T(8,128)(2,1)S(1)} %get-tuple-element.42.refs_0_), channel_id=1, source_target_pairs={{0,48},{8,56},{16,0},{24,8},{32,16},{40,24},{48,32},{56,40},{64,11... | collective-permute-start | bytes 1572872 | tf_op jit(solution)/shard_map/ppermute | solution.py:356
  78.6 10.6 %all-to-all-start.1 = ((bf16[64,32,128]{2,1,0:T(8,128)(2,1)}), bf16[64,32,128]{2,1,0:T(8,128)(2,1)}, u32[]{:S(2)}, u32[]{:S(2)}) async-start(bf16[64,32,128]{2,1,0:T(8,128)(2,1)} %get-tuple-element.37), calls=%async_computation.1 | async-start | bytes 1048576 | tf_op jit(solution)/shard_map/all_to_all | solution.py:359
  89.2 0.9 copy-done.3
  90.2 4.2 %shard_map.127 = (f32[512,128]{1,0:T(8,128)S(1)}, f32[512,128]{1,0:T(8,128)S(1)}, f32[512,128]{1,0:T(8,128)S(1)}, f32[512,128]{1,0:T(8,128)S(1)}) custom-call(s32[1]{0:T(128)} %bitcast.3.me_ref, bf16[512,128]{1,0:T(8,128)(2,1)S(1)} %copy-done, bf16[512,128]{1,0:T(8,128)(2,1)S(1)} %copy-done.1, f32[512,128]{1,0:T(8,128)S(1)} %copy-done.2, ...), custom_call_target="tpu_custom_call" | custom-call | flops 536870912 | bytes 4194304 | tf_op jit(solution)/shard_map/pallas_call | solution.py:274
  94.4 0.0 collective-permute-done.8.r_ref
  94.5 0.0 collective-permute-done.9.l_ref
  94.5 2.5 %shard_map.129 = f32[512,256]{1,0:T(8,128)S(1)} custom-call(s32[1]{0:T(128)} %bitcast.3.me_ref, bf16[512,128]{1,0:T(8,128)(2,1)S(1)} %copy-done.1, f32[512,128]{1,0:T(8,128)S(1)} %get-tuple-element.48.ml_ref, f32[512,128]{1,0:T(8,128)S(1)} %get-tuple-element.49.a_ref, bf16[64,32,128]{2,1,0:T(8,128)(2,1)S(1)} %collective-permute-done.8.r_ref, ...), custom_call_target="tpu_custom_call" | custom-call | flops 268435456 | bytes 2097152 | tf_op jit(solution)/shard_map/pallas_call | solution.py:299
  97.0 2.6 %collective-permute-start.10 = (f32[512,256]{1,0:T(8,128)S(1)}, f32[512,256]{1,0:T(8,128)S(1)}, u32[]{:S(2)}, u32[]{:S(2)}) collective-permute-start(f32[512,256]{1,0:T(8,128)S(1)} %shard_map.129), channel_id=1, source_target_pairs={{0,8},{8,0},{16,24},{24,16},{32,40},{40,32},{48,56},{56,48},{64,72... | collective-permute-start | bytes 1572872 | tf_op jit(solution)/shard_map/ppermute | solution.py:342
  99.6 2.6 %shard_map.131 = bf16[16,8192]{1,0:T(8,128)(2,1)} custom-call(s32[1]{0:T(128)} %bitcast.refs_0_.me_ref, s32[2,16]{1,0:T(2,128)} %bitcast.7, f32[2,16]{1,0:T(2,128)} %bitcast.8, bf16[8,8192]{1,0:T(8,128)(2,1)} %get-tuple-element.50.refs_0_, bf16[8,8192]{1,0:T(8,128)(2,1)} %copy-done.4, bf16[8,8192]{1,0:T(8,128)(2,1)} %copy-done.5, bf16[8,8192]{1,0:T(8,128)(2,1)} %copy-done.6, ...), custom_call_target="tpu_custom_call" | custom-call | flops 16777216 | bytes 1048576 | tf_op jit(solution)/shard_map/pallas_call | solution.py:437
  102.2 2.5 %shard_map.128 = (f32[512,128]{1,0:T(8,128)S(1)}, f32[512,128]{1,0:T(8,128)S(1)}) custom-call(s32[1]{0:T(128)} %bitcast.3.me_ref, bf16[512,128]{1,0:T(8,128)(2,1)S(1)} %copy-done, f32[512,128]{1,0:T(8,128)S(1)} %get-tuple-element.44.ml_ref, f32[512,128]{1,0:T(8,128)S(1)} %get-tuple-element.45.a_ref, bf16[64,32,128]{2,1,0:T(8,128)(2,1)S(1)} %collective-permute-done.8.r_ref, ...), custom_call_target="tpu_custom_call" | custom-call | flops 268435456 | bytes 2097152 | tf_op jit(solution)/shard_map/pallas_call | solution.py:299
  104.8 2.1 %all-to-all-done.1 = bf16[64,32,128]{2,1,0:T(8,128)(2,1)} async-done(((bf16[64,32,128]{2,1,0:T(8,128)(2,1)}), bf16[64,32,128]{2,1,0:T(8,128)(2,1)}, u32[]{:S(2)}, u32[]{:S(2)}) %all-to-all-start.1) | async-done | bytes 524320 | tf_op jit(solution)/shard_map/all_to_all | solution.py:359
  106.8 2.8 %shard_map.126 = bf16[128,2048]{1,0:T(8,128)(2,1)} custom-call(f32[128,2048]{1,0:T(8,128)} %get-tuple-element.27.l_ref, bf16[2048,128]{1,0:T(8,128)(2,1)} %bitcast.2.e_ref, bf16[128,128]{1,0:T(8,128)(2,1)} %c_ref.3, f32[16,128]{1,0:T(8,128)} %d_ref.5), custom_call_target="tpu_custom_call" | custom-call | flops 67108864 | bytes 2097152 | tf_op jit(solution)/shard_map/pallas_call | solution.py:177
  109.7 0.0 collective-permute-done.10.p_ref
  109.7 1.1 shard_map.130
  (16 shorter events, 0.0 us)
Async XLA Ops:
  3.7 11.8 %copy-start.11 = (bf16[128,512]{1,0:T(8,128)(2,1)S(1)}, bf16[128,512]{1,0:T(8,128)(2,1)}, u32[]{:S(2)}) copy-start(bf16[128,512]{1,0:T(8,128)(2,1)} %q_ref.1) | copy-start | bytes 393220
  3.7 67.4 %all-to-all-start = ((bf16[64,104,128]{2,1,0:T(8,128)(2,1)}), bf16[64,104,128]{2,1,0:T(8,128)(2,1)S(1)}, u32[]{:S(2)}, u32[]{:S(2)}) async-start(bf16[64,104,128]{2,1,0:T(8,128)(2,1)} %shard_map.122), calls=%async_computation | async-start | bytes 3407872 | tf_op jit(solution)/shard_map/all_to_all | solution.py:348
  15.4 5.2 %collective-permute-start = (bf16[128,512]{1,0:T(8,128)(2,1)S(1)}, bf16[128,512]{1,0:T(8,128)(2,1)S(1)}, u32[]{:S(2)}, u32[]{:S(2)}) collective-permute-start(bf16[128,512]{1,0:T(8,128)(2,1)S(1)} %copy-done.11), channel_id=1, source_target_pairs={{0,8},{8,0},{16,24},{24,16},{32,40},{40,32},{48,56},{56,48},{64,72... | collective-permute-start | bytes 393224 | tf_op jit(solution)/shard_map/ppermute | solution.py:342
  20.6 0.7 copy-start.12
  25.7 63.5 %copy-start = (bf16[512,128]{1,0:T(8,128)(2,1)S(1)}, bf16[512,128]{1,0:T(8,128)(2,1)}, u32[]{:S(2)}) copy-start(bf16[512,128]{1,0:T(8,128)(2,1)} %get-tuple-element.38.q_ref) | copy-start | bytes 393220
  25.7 63.5 %copy-start.1 = (bf16[512,128]{1,0:T(8,128)(2,1)S(1)}, bf16[512,128]{1,0:T(8,128)(2,1)}, u32[]{:S(2)}) copy-start(bf16[512,128]{1,0:T(8,128)(2,1)} %get-tuple-element.39.q2_ref.q_ref) | copy-start | bytes 393220
  25.7 63.5 %copy-start.2 = (f32[512,128]{1,0:T(8,128)S(1)}, f32[512,128]{1,0:T(8,128)}, u32[]{:S(2)}) copy-start(f32[512,128]{1,0:T(8,128)} %get-tuple-element.40.ml_ref) | copy-start | bytes 786436
  25.7 26.2 %collective-permute-start.1 = (bf16[8,8192]{1,0:T(8,128)(2,1)}, bf16[8,8192]{1,0:T(8,128)(2,1)S(1)}, u32[]{:S(2)}, u32[]{:S(2)}) collective-permute-start(bf16[8,8192]{1,0:T(8,128)(2,1)} %get-tuple-element.30), channel_id=1, source_target_pairs={{0,1},{1,2},{2,3},{3,4},{4,5},{5,6},{6,7},{7,0},{8,9},{9,10},{10,1... | collective-permute-start | bytes 393224 | tf_op jit(solution)/shard_map/ppermute | solution.py:428
  29.9 25.5 %collective-permute-start.2 = (bf16[8,8192]{1,0:T(8,128)(2,1)}, bf16[8,8192]{1,0:T(8,128)(2,1)S(1)}, u32[]{:S(2)}, u32[]{:S(2)}) collective-permute-start(bf16[8,8192]{1,0:T(8,128)(2,1)} %get-tuple-element.31), channel_id=1, source_target_pairs={{0,2},{1,3},{2,4},{3,5},{4,6},{5,7},{6,0},{7,1},{8,10},{9,11},{10,... | collective-permute-start | bytes 393224 | tf_op jit(solution)/shard_map/ppermute | solution.py:428
  35.7 21.9 %collective-permute-start.3 = (bf16[8,8192]{1,0:T(8,128)(2,1)}, bf16[8,8192]{1,0:T(8,128)(2,1)S(1)}, u32[]{:S(2)}, u32[]{:S(2)}) collective-permute-start(bf16[8,8192]{1,0:T(8,128)(2,1)} %get-tuple-element.32), channel_id=1, source_target_pairs={{0,3},{1,4},{2,5},{3,6},{4,7},{5,0},{6,1},{7,2},{8,11},{9,12},{10,... | collective-permute-start | bytes 393224 | tf_op jit(solution)/shard_map/ppermute | solution.py:428
  42.7 15.9 %collective-permute-start.4 = (bf16[8,8192]{1,0:T(8,128)(2,1)}, bf16[8,8192]{1,0:T(8,128)(2,1)S(1)}, u32[]{:S(2)}, u32[]{:S(2)}) collective-permute-start(bf16[8,8192]{1,0:T(8,128)(2,1)} %get-tuple-element.33), channel_id=1, source_target_pairs={{0,4},{1,5},{2,6},{3,7},{4,0},{5,1},{6,2},{7,3},{8,12},{9,13},{10,... | collective-permute-start | bytes 393224 | tf_op jit(solution)/shard_map/ppermute | solution.py:428
  45.6 13.3 %collective-permute-start.5 = (bf16[8,8192]{1,0:T(8,128)(2,1)}, bf16[8,8192]{1,0:T(8,128)(2,1)S(1)}, u32[]{:S(2)}, u32[]{:S(2)}) collective-permute-start(bf16[8,8192]{1,0:T(8,128)(2,1)} %get-tuple-element.34), channel_id=1, source_target_pairs={{0,5},{1,6},{2,7},{3,0},{4,1},{5,2},{6,3},{7,4},{8,13},{9,14},{10,... | collective-permute-start | bytes 393224 | tf_op jit(solution)/shard_map/ppermute | solution.py:428
  52.0 42.5 %copy-start.4 = (bf16[8,8192]{1,0:T(8,128)(2,1)}, bf16[8,8192]{1,0:T(8,128)(2,1)S(1)}, u32[]{:S(2)}) copy-start(bf16[8,8192]{1,0:T(8,128)(2,1)S(1)} %collective-permute-done.1.refs_1_) | copy-start | bytes 393220
  52.0 18.1 %collective-permute-start.6 = (bf16[8,8192]{1,0:T(8,128)(2,1)}, bf16[8,8192]{1,0:T(8,128)(2,1)S(1)}, u32[]{:S(2)}, u32[]{:S(2)}) collective-permute-start(bf16[8,8192]{1,0:T(8,128)(2,1)} %get-tuple-element.35), channel_id=1, source_target_pairs={{0,6},{1,7},{2,0},{3,1},{4,2},{5,3},{6,4},{7,5},{8,14},{9,15},{10,... | collective-permute-start | bytes 393224 | tf_op jit(solution)/shard_map/ppermute | solution.py:428
  55.4 39.1 %copy-start.5 = (bf16[8,8192]{1,0:T(8,128)(2,1)}, bf16[8,8192]{1,0:T(8,128)(2,1)S(1)}, u32[]{:S(2)}) copy-start(bf16[8,8192]{1,0:T(8,128)(2,1)S(1)} %collective-permute-done.2.refs_2_) | copy-start | bytes 393220
  55.4 15.0 %collective-permute-start.7 = (bf16[8,8192]{1,0:T(8,128)(2,1)}, bf16[8,8192]{1,0:T(8,128)(2,1)S(1)}, u32[]{:S(2)}, u32[]{:S(2)}) collective-permute-start(bf16[8,8192]{1,0:T(8,128)(2,1)} %get-tuple-element.36), channel_id=1, source_target_pairs={{0,7},{1,0},{2,1},{3,2},{4,3},{5,4},{6,5},{7,6},{8,15},{9,8},{10,9... | collective-permute-start | bytes 393224 | tf_op jit(solution)/shard_map/ppermute | solution.py:428
  57.6 12.8 %copy-start.6 = (bf16[8,8192]{1,0:T(8,128)(2,1)}, bf16[8,8192]{1,0:T(8,128)(2,1)S(1)}, u32[]{:S(2)}) copy-start(bf16[8,8192]{1,0:T(8,128)(2,1)S(1)} %collective-permute-done.3.refs_3_) | copy-start | bytes 393220
  58.6 11.8 %copy-start.7 = (bf16[8,8192]{1,0:T(8,128)(2,1)}, bf16[8,8192]{1,0:T(8,128)(2,1)S(1)}, u32[]{:S(2)}) copy-start(bf16[8,8192]{1,0:T(8,128)(2,1)S(1)} %collective-permute-done.4.refs_4_) | copy-start | bytes 393220
  58.9 11.5 %copy-start.8 = (bf16[8,8192]{1,0:T(8,128)(2,1)}, bf16[8,8192]{1,0:T(8,128)(2,1)S(1)}, u32[]{:S(2)}) copy-start(bf16[8,8192]{1,0:T(8,128)(2,1)S(1)} %collective-permute-done.5.refs_5_) | copy-start | bytes 393220
  70.1 0.6 copy-start.9
  70.4 0.7 copy-start.10
  72.1 22.3 %collective-permute-start.8 = (bf16[64,32,128]{2,1,0:T(8,128)(2,1)S(1)}, bf16[64,32,128]{2,1,0:T(8,128)(2,1)S(1)}, u32[]{:S(2)}, u32[]{:S(2)}) collective-permute-start(bf16[64,32,128]{2,1,0:T(8,128)(2,1)S(1)} %get-tuple-element.42.refs_0_), channel_id=1, source_target_pairs={{0,16},{8,24},{16,32},{24,40},{32,48},{40,56},{48,0},{56,8},{64,80... | collective-permute-start | bytes 1572872 | tf_op jit(solution)/shard_map/ppermute | solution.py:355
  75.3 19.1 %collective-permute-start.9 = (bf16[64,32,128]{2,1,0:T(8,128)(2,1)S(1)}, bf16[64,32,128]{2,1,0:T(8,128)(2,1)S(1)}, u32[]{:S(2)}, u32[]{:S(2)}) collective-permute-start(bf16[64,32,128]{2,1,0:T(8,128)(2,1)S(1)} %get-tuple-element.42.refs_0_), channel_id=1, source_target_pairs={{0,48},{8,56},{16,0},{24,8},{32,16},{40,24},{48,32},{56,40},{64,11... | collective-permute-start | bytes 1572872 | tf_op jit(solution)/shard_map/ppermute | solution.py:356
  78.6 28.2 %all-to-all-start.1 = ((bf16[64,32,128]{2,1,0:T(8,128)(2,1)}), bf16[64,32,128]{2,1,0:T(8,128)(2,1)}, u32[]{:S(2)}, u32[]{:S(2)}) async-start(bf16[64,32,128]{2,1,0:T(8,128)(2,1)} %get-tuple-element.37), calls=%async_computation.1 | async-start | bytes 1048576 | tf_op jit(solution)/shard_map/all_to_all | solution.py:359
  89.2 1.0 copy-start.3
  97.0 12.7 %collective-permute-start.10 = (f32[512,256]{1,0:T(8,128)S(1)}, f32[512,256]{1,0:T(8,128)S(1)}, u32[]{:S(2)}, u32[]{:S(2)}) collective-permute-start(f32[512,256]{1,0:T(8,128)S(1)} %shard_map.129), channel_id=1, source_target_pairs={{0,8},{8,0},{16,24},{24,16},{32,40},{40,32},{48,56},{56,48},{64,72... | collective-permute-start | bytes 1572872 | tf_op jit(solution)/shard_map/ppermute | solution.py:342

commit v8 on v7

--- a/solution.py
+++ b/solution.py
@@ -164,7 +164,7 @@
 JOIN_COST = 1 << 26
 
 
-def join_kernel(l_ref, e_ref, c_ref, d_ref, o_ref):
+def join_kernel(l_ref, e_ref, c_ref, d_ref, _, o_ref):
     grow = jnp.exp(col_cumulative(d_ref[...]))
     c = c_ref[...]
     for h in range(MH):
@@ -173,15 +173,16 @@
         o_ref[:, cols] = (l_ref[:, cols] + grow[:, h : h + 1] * readout).astype(BF16)
 
 
-def join_mamba(local, entering, c_in, decay_log):
+def join_mamba(local, entering, c_in, decay_log, after):
     return pl.pallas_call(
         join_kernel,
+        grid=(1,),
         out_shape=jax.ShapeDtypeStruct((L, MH * HD), BF16),
-        in_specs=[VM] * 4,
-        out_specs=VM,
+        in_specs=[full(a.shape) for a in (local, entering, c_in, decay_log)] + [TILE],
+        out_specs=full((L, MH * HD)),
         compiler_params=params(LARGE),
         cost_estimate=cost(JOIN_COST, 1 << 21),
-    )(local, entering, c_in, decay_log)
+    )(local, entering, c_in, decay_log, after)
 
 
 ROWS = QH * L
@@ -349,22 +350,23 @@
     q_other = other_core(q_in)
     local, token = local_part(x_in, b_in, c_in, decay_log)
     q_own, q_other, ml, acc, token = open_attention(q_in, q_other, k_in, v_in, token)
-    blocks = expert_blocks(expert_out, [chunks.reshape(NCTX * CHUNK, HD), token])
-    arrived = sum(b[:8, :HD] for b in blocks[1:]) if len(blocks) > 1 else blocks[0][:8, :HD]
+    blocks = expert_blocks(expert_out, [chunks.reshape(NCTX * CHUNK, HD)])
+    arrived = sum((b[:8, :HD] for b in blocks[1:]), token.astype(BF16))
     own, opposite, entering = take_received(received, [arrived])
     right = lax.ppermute(own, "ctx", along_x(1))
     left = lax.ppermute(own, "ctx", along_x(-1))
 
     ml, acc, ml2, acc2 = early_attention(me, q_own, q_other, ml, acc, [own, opposite])
     entering = lax.all_to_all(entering, "ctx", split_axis=0, concat_axis=0, tiled=True)
-    mamba_out = join_mamba(local, entering.reshape(MH * L, HD), c_in, decay_log)
 
     sets = [right, left]
     both = jax.ShapeDtypeStruct((ROWS, HD + L), F32)
     [part] = late_attention(other_kernel, [both], me, q_other, ml2, acc2, sets)
     part = other_core(part)
     ml, acc = late_attention(own_kernel, [PART] * 2, me, q_own, ml, acc, sets)
-    return mamba_out, merge_attention(ml, acc, part), blocks
+    attn_out = merge_attention(ml, acc, part)
+    mamba_out = join_mamba(local, entering.reshape(MH * L, HD), c_in, decay_log, attn_out)
+    return mamba_out, attn_out, blocks
 
 
 def blocks_kernel(n_ties, me_ref, e_ref, *refs):

time: 112 us -> 106 us (0.946)
  waiting for transfers between devices: 14.9 us -> 7.92 us
    ppermute x7, waiting for transfers between devices: 12.8 us -> 7.68 us  [expert_blocks(): blocks[d] = lax.ppermute(held[d], 'grp', pairs)]
    all_to_all x1, waiting for transfers between devices: 2.08 us -> 0.22 us  [context_parts(): lax.all_to_all(entering, 'ctx', split_axis=0, concat_axis=0, tiled=True)]
    unnamed x26 -> x28, local copies, waits for them, and re-layouts: 2.25 us -> 2.74 us
  transfers between devices with their start and end apart: 13 -> 13, of which waited for: 5 -> 3; matrix products, arithmetic and copies ran while one was open for 0% -> 1% of each run, Pallas kernels for 20% -> 19%
where the time goes in v8:
time: 106 us; the launch traced here: 105 us
  starting transfers between devices  65.3 us (62%)
  Pallas kernels  27.2 us (26%)
  waiting for transfers between devices  7.92 us (7%)
  local copies, waits for them, and re-layouts  2.74 us (3%)
    ppermute x7, starting transfers between devices, expert_blocks(): blocks[d] = lax.ppermute(held[d], 'grp', pairs)  31.6 us
    all_to_all x1, starting transfers between devices, context_parts(): lax.all_to_all(chunks, 'ctx', split_axis=0, concat_axis=0, tiled=True)  11.6 us
    all_to_all x1, starting transfers between devices, context_parts(): lax.all_to_all(entering, 'ctx', split_axis=0, concat_axis=0, tiled=True)  10.1 us
    ppermute x7, waiting for transfers between devices, expert_blocks(): blocks[d] = lax.ppermute(held[d], 'grp', pairs)  7.68 us
    ppermute x2, starting transfers between devices, other_core(): return lax.ppermute(value, 'ctx', [(i, i ^ 1) for i in range(NCTX)])  5.47 us
    pallas_call x2, Pallas kernels, late_attention(): pl.pallas_call(kernel, out_shape=outs, in_specs=[SM] + [VM] * 5, out_spec...  5.06 us
    pallas_call x1, Pallas kernels, early_attention(): pl.pallas_call(early_kernel, out_shape=[PART] * 4, in_specs=[SM] + [VM] *...  4.24 us
    ppermute x1, starting transfers between devices, context_parts(): left = lax.ppermute(own, 'ctx', along_x(-1))  3.29 us
  transfers between devices with their start and end apart: 13, of which 3 were waited for; matrix products, arithmetic and copies ran while one was open for 1% of the time, Pallas kernels for 19%

profile of v8, /device:TPU:1, one launch (start us, length us, event | category | flops | bytes accessed | tf_op | source)
XLA Modules:
  0.0 104.8 jit_solution(13736742016178195676)
XLA Ops:
  0.6 3.0 %shard_map.122 = bf16[64,104,128]{2,1,0:T(8,128)(2,1)} custom-call(bf16[128,2048]{1,0:T(8,128)(2,1)} %x_ref.3, bf16[128,128]{1,0:T(8,128)(2,1)} %b_ref.3, f32[16,128]{1,0:T(8,128)} %d_ref.5, bf16[128,128]{1,0:T(8,128)(2,1)} %k_ref.3, bf16[128,128]{1,0:T(8,128)(2,1)} %v_ref.3), custom_call_target="tpu_custom_call" | custom-call | flops 67108864 | bytes 2097152 | tf_op jit(solution)/shard_map/pallas_call | solution.py:94
  3.6 11.6 %all-to-all-start = ((bf16[64,104,128]{2,1,0:T(8,128)(2,1)}), bf16[64,104,128]{2,1,0:T(8,128)(2,1)S(1)}, u32[]{:S(2)}, u32[]{:S(2)}) async-start(bf16[64,104,128]{2,1,0:T(8,128)(2,1)} %shard_map.122), calls=%async_computation | async-start | bytes 3407872 | tf_op jit(solution)/shard_map/all_to_all | solution.py:349
  15.3 0.0 copy-start.12
  15.3 2.3 %shard_map.124 = (bf16[8,8192]{1,0:T(8,128)(2,1)}, bf16[8,8192]{1,0:T(8,128)(2,1)}, bf16[8,8192]{1,0:T(8,128)(2,1)}, bf16[8,8192]{1,0:T(8,128)(2,1)}, bf16[8,819...) custom-call(s32[1]{0:T(128)} %bitcast.refs_0_.me_ref, ...), custom_call_target="tpu_custom_call" | custom-call | flops 1048576 | bytes 2097152 | tf_op jit(solution)/shard_map/pallas_call | solution.py:418
  17.5 4.0 %collective-permute-start.1 = (bf16[8,8192]{1,0:T(8,128)(2,1)}, bf16[8,8192]{1,0:T(8,128)(2,1)S(1)}, u32[]{:S(2)}, u32[]{:S(2)}) collective-permute-start(bf16[8,8192]{1,0:T(8,128)(2,1)} %get-tuple-element.30), channel_id=1, source_target_pairs={{0,1},{1,2},{2,3},{3,4},{4,5},{5,6},{6,7},{7,0},{8,9},{9,10},{10,1... | collective-permute-start | bytes 393224 | tf_op jit(solution)/shard_map/ppermute | solution.py:430
  21.5 5.8 %collective-permute-start.2 = (bf16[8,8192]{1,0:T(8,128)(2,1)}, bf16[8,8192]{1,0:T(8,128)(2,1)S(1)}, u32[]{:S(2)}, u32[]{:S(2)}) collective-permute-start(bf16[8,8192]{1,0:T(8,128)(2,1)} %get-tuple-element.31), channel_id=1, source_target_pairs={{0,2},{1,3},{2,4},{3,5},{4,6},{5,7},{6,0},{7,1},{8,10},{9,11},{10,... | collective-permute-start | bytes 393224 | tf_op jit(solution)/shard_map/ppermute | solution.py:430
  27.4 0.0 copy-done.12
  27.4 2.9 %collective-permute-start = (bf16[128,512]{1,0:T(8,128)(2,1)S(1)}, bf16[128,512]{1,0:T(8,128)(2,1)S(1)}, u32[]{:S(2)}, u32[]{:S(2)}) collective-permute-start(bf16[128,512]{1,0:T(8,128)(2,1)S(1)} %copy-done.12), channel_id=1, source_target_pairs={{0,8},{8,0},{16,24},{24,16},{32,40},{40,32},{48,56},{56,48},{64,72... | collective-permute-start | bytes 393224 | tf_op jit(solution)/shard_map/ppermute | solution.py:343
  30.3 7.0 %collective-permute-start.3 = (bf16[8,8192]{1,0:T(8,128)(2,1)}, bf16[8,8192]{1,0:T(8,128)(2,1)S(1)}, u32[]{:S(2)}, u32[]{:S(2)}) collective-permute-start(bf16[8,8192]{1,0:T(8,128)(2,1)} %get-tuple-element.32), channel_id=1, source_target_pairs={{0,3},{1,4},{2,5},{3,6},{4,7},{5,0},{6,1},{7,2},{8,11},{9,12},{10,... | collective-permute-start | bytes 393224 | tf_op jit(solution)/shard_map/ppermute | solution.py:430
  37.3 2.8 %collective-permute-start.4 = (bf16[8,8192]{1,0:T(8,128)(2,1)}, bf16[8,8192]{1,0:T(8,128)(2,1)S(1)}, u32[]{:S(2)}, u32[]{:S(2)}) collective-permute-start(bf16[8,8192]{1,0:T(8,128)(2,1)} %get-tuple-element.33), channel_id=1, source_target_pairs={{0,4},{1,5},{2,6},{3,7},{4,0},{5,1},{6,2},{7,3},{8,12},{9,13},{10,... | collective-permute-start | bytes 393224 | tf_op jit(solution)/shard_map/ppermute | solution.py:430
  40.2 0.0 collective-permute-done.1.refs_1_
  40.2 0.0 copy-start.5
  40.2 6.4 %collective-permute-start.5 = (bf16[8,8192]{1,0:T(8,128)(2,1)}, bf16[8,8192]{1,0:T(8,128)(2,1)S(1)}, u32[]{:S(2)}, u32[]{:S(2)}) collective-permute-start(bf16[8,8192]{1,0:T(8,128)(2,1)} %get-tuple-element.34), channel_id=1, source_target_pairs={{0,5},{1,6},{2,7},{3,0},{4,1},{5,2},{6,3},{7,4},{8,13},{9,14},{10,... | collective-permute-start | bytes 393224 | tf_op jit(solution)/shard_map/ppermute | solution.py:430
  46.6 0.0 collective-permute-done.2.refs_2_
  46.6 3.4 %collective-permute-start.6 = (bf16[8,8192]{1,0:T(8,128)(2,1)}, bf16[8,8192]{1,0:T(8,128)(2,1)S(1)}, u32[]{:S(2)}, u32[]{:S(2)}) collective-permute-start(bf16[8,8192]{1,0:T(8,128)(2,1)} %get-tuple-element.35), channel_id=1, source_target_pairs={{0,6},{1,7},{2,0},{3,1},{4,2},{5,3},{6,4},{7,5},{8,14},{9,15},{10,... | collective-permute-start | bytes 393224 | tf_op jit(solution)/shard_map/ppermute | solution.py:430
  50.0 0.0 collective-permute-done.q2_ref
  50.0 0.0 copy-start.13
  50.0 2.2 %collective-permute-start.7 = (bf16[8,8192]{1,0:T(8,128)(2,1)}, bf16[8,8192]{1,0:T(8,128)(2,1)S(1)}, u32[]{:S(2)}, u32[]{:S(2)}) collective-permute-start(bf16[8,8192]{1,0:T(8,128)(2,1)} %get-tuple-element.36), channel_id=1, source_target_pairs={{0,7},{1,0},{2,1},{3,2},{4,3},{5,4},{6,5},{7,6},{8,15},{9,8},{10,9... | collective-permute-start | bytes 393224 | tf_op jit(solution)/shard_map/ppermute | solution.py:430
  52.2 2.9 %shard_map.121 = (f32[128,2048]{1,0:T(8,128)}, f32[8,128]{1,0:T(8,128)}) custom-call(bf16[128,2048]{1,0:T(8,128)(2,1)} %x_ref.3, bf16[128,128]{1,0:T(8,128)(2,1)} %b_ref.3, bf16[128,128]{1,0:T(8,128)(2,1)} %c_ref.3, f32[16,128]{1,0:T(8,128)} %d_ref.5), custom_call_target="tpu_custom_call" | custom-call | flops 268435456 | bytes 2097152 | tf_op jit(solution)/shard_map/pallas_call | solution.py:154
  55.1 2.2 %shard_map.123 = (bf16[512,128]{1,0:T(8,128)(2,1)}, bf16[512,128]{1,0:T(8,128)(2,1)}, f32[512,128]{1,0:T(8,128)}, f32[512,128]{1,0:T(8,128)}, f32[8,128]{1,0:T(8,128)}) custom-call(bf16[128,512]{1,0:T(8,128)(2,1)} %q_ref.1, bf16[128,512]{1,0:T(8,128)(2,1)} %copy-done.13, bf16[128,128]{1,0:T(8,128)(2,1)} %k_ref.3, bf16[128,128]{1,0:T(8,128)(2,1)} %v_ref.3, ...), custom_call_target="tpu_custom_call" | custom-call | flops 134217728 | bytes 1048576 | tf_op jit(solution)/shard_map/pallas_call | solution.py:241
  57.2 0.0 collective-permute-done.3.refs_3_
  57.3 0.0 collective-permute-done.4.refs_4_
  57.3 0.0 collective-permute-done.5.refs_5_
  57.3 0.0 copy-start.9
  57.3 7.5 %collective-permute-done.6.refs_6_ = bf16[8,8192]{1,0:T(8,128)(2,1)S(1)} collective-permute-done((bf16[8,8192]{1,0:T(8,128)(2,1)}, bf16[8,8192]{1,0:T(8,128)(2,1)S(1)}, u32[]{:S(2)}, u32[]{:S(2)}) %collective-permute-start.6) | collective-permute-done | bytes 131104 | tf_op jit(solution)/shard_map/ppermute | solution.py:430
  64.8 0.2 collective-permute-done.7.refs_7_
  65.0 0.7 slice_add_fusion.refs_0_
  65.7 0.0 copy-done.11
  65.7 0.0 all-to-all-done.s_ref
  65.7 1.1 %shard_map.125 = (bf16[64,32,128]{2,1,0:T(8,128)(2,1)S(1)}, bf16[64,32,128]{2,1,0:T(8,128)(2,1)S(1)}, bf16[64,32,128]{2,1,0:T(8,128)(2,1)}) custom-call(bf16[64,104,128]{2,1,0:T(8,128)(2,1)S(1)} %all-to-all-done.s_ref, bf16[8,128]{1,0:T(8,128)(2,1)S(1)} %slice_add_fusion.refs_0_), custom_call_target="tpu_custom_call" | custom-call | flops 1048576 | bytes 2097152 | tf_op jit(solution)/shard_map/pallas_call | solution.py:119
  66.8 3.2 %collective-permute-start.8 = (bf16[64,32,128]{2,1,0:T(8,128)(2,1)S(1)}, bf16[64,32,128]{2,1,0:T(8,128)(2,1)S(1)}, u32[]{:S(2)}, u32[]{:S(2)}) collective-permute-start(bf16[64,32,128]{2,1,0:T(8,128)(2,1)S(1)} %get-tuple-element.42.refs_0_), channel_id=1, source_target_pairs={{0,16},{8,24},{16,32},{24,40},{32,48},{40,56},{48,0},{56,8},{64,80... | collective-permute-start | bytes 1572872 | tf_op jit(solution)/shard_map/ppermute | solution.py:356
  70.0 3.3 %collective-permute-start.9 = (bf16[64,32,128]{2,1,0:T(8,128)(2,1)S(1)}, bf16[64,32,128]{2,1,0:T(8,128)(2,1)S(1)}, u32[]{:S(2)}, u32[]{:S(2)}) collective-permute-start(bf16[64,32,128]{2,1,0:T(8,128)(2,1)S(1)} %get-tuple-element.42.refs_0_), channel_id=1, source_target_pairs={{0,48},{8,56},{16,0},{24,8},{32,16},{40,24},{48,32},{56,40},{64,11... | collective-permute-start | bytes 1572872 | tf_op jit(solution)/shard_map/ppermute | solution.py:357
  73.3 10.1 %all-to-all-start.1 = ((bf16[64,32,128]{2,1,0:T(8,128)(2,1)}), bf16[64,32,128]{2,1,0:T(8,128)(2,1)S(1)}, u32[]{:S(2)}, u32[]{:S(2)}) async-start(bf16[64,32,128]{2,1,0:T(8,128)(2,1)} %get-tuple-element.37), calls=%async_computation.1 | async-start | bytes 1048576 | tf_op jit(solution)/shard_map/all_to_all | solution.py:360
  83.5 0.0 copy-start.2
  83.5 0.9 copy-done.2
  84.4 0.9 copy-done.3
  85.4 4.2 %shard_map.126 = (f32[512,128]{1,0:T(8,128)S(1)}, f32[512,128]{1,0:T(8,128)S(1)}, f32[512,128]{1,0:T(8,128)S(1)}, f32[512,128]{1,0:T(8,128)S(1)}) custom-call(s32[1]{0:T(128)} %bitcast.3.me_ref, bf16[512,128]{1,0:T(8,128)(2,1)S(1)} %copy-done, bf16[512,128]{1,0:T(8,128)(2,1)S(1)} %copy-done.1, f32[512,128]{1,0:T(8,128)S(1)} %copy-done.2, ...), custom_call_target="tpu_custom_call" | custom-call | flops 536870912 | bytes 4194304 | tf_op jit(solution)/shard_map/pallas_call | solution.py:275
  89.6 0.0 collective-permute-done.8.r_ref
  89.6 0.0 collective-permute-done.9.l_ref
  89.6 2.5 %shard_map.128 = f32[512,256]{1,0:T(8,128)S(1)} custom-call(s32[1]{0:T(128)} %bitcast.3.me_ref, bf16[512,128]{1,0:T(8,128)(2,1)S(1)} %copy-done.1, f32[512,128]{1,0:T(8,128)S(1)} %get-tuple-element.48.ml_ref, f32[512,128]{1,0:T(8,128)S(1)} %get-tuple-element.49.a_ref, bf16[64,32,128]{2,1,0:T(8,128)(2,1)S(1)} %collective-permute-done.8.r_ref, ...), custom_call_target="tpu_custom_call" | custom-call | flops 268435456 | bytes 2097152 | tf_op jit(solution)/shard_map/pallas_call | solution.py:300
  92.2 2.5 %collective-permute-start.10 = (f32[512,256]{1,0:T(8,128)S(1)}, f32[512,256]{1,0:T(8,128)S(1)}, u32[]{:S(2)}, u32[]{:S(2)}) collective-permute-start(f32[512,256]{1,0:T(8,128)S(1)} %shard_map.128), channel_id=1, source_target_pairs={{0,8},{8,0},{16,24},{24,16},{32,40},{40,32},{48,56},{56,48},{64,72... | collective-permute-start | bytes 1572872 | tf_op jit(solution)/shard_map/ppermute | solution.py:343
  94.7 2.6 %shard_map.131 = bf16[16,8192]{1,0:T(8,128)(2,1)} custom-call(s32[1]{0:T(128)} %bitcast.refs_0_.me_ref, s32[2,16]{1,0:T(2,128)} %bitcast.8, f32[2,16]{1,0:T(2,128)} %bitcast.9, bf16[8,8192]{1,0:T(8,128)(2,1)} %get-tuple-element.50.refs_0_, bf16[8,8192]{1,0:T(8,128)(2,1)} %copy-done.5, bf16[8,8192]{1,0:T(8,128)(2,1)} %copy-done.6, bf16[8,8192]{1,0:T(8,128)(2,1)} %copy-done.7, ...), custom_call_target="tpu_custom_call" | custom-call | flops 16777216 | bytes 1048576 | tf_op jit(solution)/shard_map/pallas_call | solution.py:439
  97.3 2.5 %shard_map.127 = (f32[512,128]{1,0:T(8,128)S(1)}, f32[512,128]{1,0:T(8,128)S(1)}) custom-call(s32[1]{0:T(128)} %bitcast.3.me_ref, bf16[512,128]{1,0:T(8,128)(2,1)S(1)} %copy-done, f32[512,128]{1,0:T(8,128)S(1)} %get-tuple-element.44.ml_ref, f32[512,128]{1,0:T(8,128)S(1)} %get-tuple-element.45.a_ref, bf16[64,32,128]{2,1,0:T(8,128)(2,1)S(1)} %collective-permute-done.8.r_ref, ...), custom_call_target="tpu_custom_call" | custom-call | flops 268435456 | bytes 2097152 | tf_op jit(solution)/shard_map/pallas_call | solution.py:300
  99.9 0.0 collective-permute-done.10.p_ref
  99.9 1.1 %shard_map.129._ = bf16[128,512]{1,0:T(8,128)(2,1)} custom-call(f32[512,128]{1,0:T(8,128)S(1)} %get-tuple-element.46.ml_ref, f32[512,128]{1,0:T(8,128)S(1)} %get-tuple-element.47.a_ref, f32[512,256]{1,0:T(8,128)S(1)} %collective-permute-done.10.p_ref), custom_call_target="tpu_custom_call" | custom-call | flops 1048576 | bytes 1048576 | tf_op jit(solution)/shard_map/pallas_call | solution.py:321
  100.9 0.2 all-to-all-done.1
  101.2 0.8 copy-done.4
  102.0 2.8 %shard_map.130 = bf16[128,2048]{1,0:T(8,128)(2,1)} custom-call(f32[128,2048]{1,0:T(8,128)} %get-tuple-element.27.l_ref, bf16[2048,128]{1,0:T(8,128)(2,1)} %bitcast.7, bf16[128,128]{1,0:T(8,128)(2,1)} %c_ref.3, f32[16,128]{1,0:T(8,128)} %d_ref.5, bf16[128,512]{1,0:T(8,128)(2,1)} %shard_map.129._), custom_call_target="tpu_custom_call" | custom-call | flops 67108864 | bytes 2097152 | tf_op jit(solution)/shard_map/pallas_call | solution.py:177
  (18 shorter events, 0.0 us)
Async XLA Ops:
  3.6 62.1 %all-to-all-start = ((bf16[64,104,128]{2,1,0:T(8,128)(2,1)}), bf16[64,104,128]{2,1,0:T(8,128)(2,1)S(1)}, u32[]{:S(2)}, u32[]{:S(2)}) async-start(bf16[64,104,128]{2,1,0:T(8,128)(2,1)} %shard_map.122), calls=%async_computation | async-start | bytes 3407872 | tf_op jit(solution)/shard_map/all_to_all | solution.py:349
  15.3 12.1 %copy-start.12 = (bf16[128,512]{1,0:T(8,128)(2,1)S(1)}, bf16[128,512]{1,0:T(8,128)(2,1)}, u32[]{:S(2)}) copy-start(bf16[128,512]{1,0:T(8,128)(2,1)} %q_ref.1) | copy-start | bytes 393220
  17.5 22.6 %collective-permute-start.1 = (bf16[8,8192]{1,0:T(8,128)(2,1)}, bf16[8,8192]{1,0:T(8,128)(2,1)S(1)}, u32[]{:S(2)}, u32[]{:S(2)}) collective-permute-start(bf16[8,8192]{1,0:T(8,128)(2,1)} %get-tuple-element.30), channel_id=1, source_target_pairs={{0,1},{1,2},{2,3},{3,4},{4,5},{5,6},{6,7},{7,0},{8,9},{9,10},{10,1... | collective-permute-start | bytes 393224 | tf_op jit(solution)/shard_map/ppermute | solution.py:430
  21.5 25.0 %collective-permute-start.2 = (bf16[8,8192]{1,0:T(8,128)(2,1)}, bf16[8,8192]{1,0:T(8,128)(2,1)S(1)}, u32[]{:S(2)}, u32[]{:S(2)}) collective-permute-start(bf16[8,8192]{1,0:T(8,128)(2,1)} %get-tuple-element.31), channel_id=1, source_target_pairs={{0,2},{1,3},{2,4},{3,5},{4,6},{5,7},{6,0},{7,1},{8,10},{9,11},{10,... | collective-permute-start | bytes 393224 | tf_op jit(solution)/shard_map/ppermute | solution.py:430
  27.4 22.6 %collective-permute-start = (bf16[128,512]{1,0:T(8,128)(2,1)S(1)}, bf16[128,512]{1,0:T(8,128)(2,1)S(1)}, u32[]{:S(2)}, u32[]{:S(2)}) collective-permute-start(bf16[128,512]{1,0:T(8,128)(2,1)S(1)} %copy-done.12), channel_id=1, source_target_pairs={{0,8},{8,0},{16,24},{24,16},{32,40},{40,32},{48,56},{56,48},{64,72... | collective-permute-start | bytes 393224 | tf_op jit(solution)/shard_map/ppermute | solution.py:343
  30.3 26.9 %collective-permute-start.3 = (bf16[8,8192]{1,0:T(8,128)(2,1)}, bf16[8,8192]{1,0:T(8,128)(2,1)S(1)}, u32[]{:S(2)}, u32[]{:S(2)}) collective-permute-start(bf16[8,8192]{1,0:T(8,128)(2,1)} %get-tuple-element.32), channel_id=1, source_target_pairs={{0,3},{1,4},{2,5},{3,6},{4,7},{5,0},{6,1},{7,2},{8,11},{9,12},{10,... | collective-permute-start | bytes 393224 | tf_op jit(solution)/shard_map/ppermute | solution.py:430
  37.3 19.9 %collective-permute-start.4 = (bf16[8,8192]{1,0:T(8,128)(2,1)}, bf16[8,8192]{1,0:T(8,128)(2,1)S(1)}, u32[]{:S(2)}, u32[]{:S(2)}) collective-permute-start(bf16[8,8192]{1,0:T(8,128)(2,1)} %get-tuple-element.33), channel_id=1, source_target_pairs={{0,4},{1,5},{2,6},{3,7},{4,0},{5,1},{6,2},{7,3},{8,12},{9,13},{10,... | collective-permute-start | bytes 393224 | tf_op jit(solution)/shard_map/ppermute | solution.py:430
  40.2 24.8 %copy-start.5 = (bf16[8,8192]{1,0:T(8,128)(2,1)}, bf16[8,8192]{1,0:T(8,128)(2,1)S(1)}, u32[]{:S(2)}) copy-start(bf16[8,8192]{1,0:T(8,128)(2,1)S(1)} %collective-permute-done.1.refs_1_) | copy-start | bytes 393220
  40.2 17.1 %collective-permute-start.5 = (bf16[8,8192]{1,0:T(8,128)(2,1)}, bf16[8,8192]{1,0:T(8,128)(2,1)S(1)}, u32[]{:S(2)}, u32[]{:S(2)}) collective-permute-start(bf16[8,8192]{1,0:T(8,128)(2,1)} %get-tuple-element.34), channel_id=1, source_target_pairs={{0,5},{1,6},{2,7},{3,0},{4,1},{5,2},{6,3},{7,4},{8,13},{9,14},{10,... | collective-permute-start | bytes 393224 | tf_op jit(solution)/shard_map/ppermute | solution.py:430
  46.6 18.4 %copy-start.6 = (bf16[8,8192]{1,0:T(8,128)(2,1)}, bf16[8,8192]{1,0:T(8,128)(2,1)S(1)}, u32[]{:S(2)}) copy-start(bf16[8,8192]{1,0:T(8,128)(2,1)S(1)} %collective-permute-done.2.refs_2_) | copy-start | bytes 393220
  46.6 18.2 %collective-permute-start.6 = (bf16[8,8192]{1,0:T(8,128)(2,1)}, bf16[8,8192]{1,0:T(8,128)(2,1)S(1)}, u32[]{:S(2)}, u32[]{:S(2)}) collective-permute-start(bf16[8,8192]{1,0:T(8,128)(2,1)} %get-tuple-element.35), channel_id=1, source_target_pairs={{0,6},{1,7},{2,0},{3,1},{4,2},{5,3},{6,4},{7,5},{8,14},{9,15},{10,... | collective-permute-start | bytes 393224 | tf_op jit(solution)/shard_map/ppermute | solution.py:430
  50.0 5.1 %copy-start.13 = (bf16[128,512]{1,0:T(8,128)(2,1)}, bf16[128,512]{1,0:T(8,128)(2,1)S(1)}, u32[]{:S(2)}) copy-start(bf16[128,512]{1,0:T(8,128)(2,1)S(1)} %collective-permute-done.q2_ref) | copy-start | bytes 393220
  50.0 15.0 %collective-permute-start.7 = (bf16[8,8192]{1,0:T(8,128)(2,1)}, bf16[8,8192]{1,0:T(8,128)(2,1)S(1)}, u32[]{:S(2)}, u32[]{:S(2)}) collective-permute-start(bf16[8,8192]{1,0:T(8,128)(2,1)} %get-tuple-element.36), channel_id=1, source_target_pairs={{0,7},{1,0},{2,1},{3,2},{4,3},{5,4},{6,5},{7,6},{8,15},{9,8},{10,9... | collective-permute-start | bytes 393224 | tf_op jit(solution)/shard_map/ppermute | solution.py:430
  57.2 26.2 %copy-start = (bf16[512,128]{1,0:T(8,128)(2,1)S(1)}, bf16[512,128]{1,0:T(8,128)(2,1)}, u32[]{:S(2)}) copy-start(bf16[512,128]{1,0:T(8,128)(2,1)} %get-tuple-element.38.q_ref) | copy-start | bytes 393220
  57.2 26.2 %copy-start.1 = (bf16[512,128]{1,0:T(8,128)(2,1)S(1)}, bf16[512,128]{1,0:T(8,128)(2,1)}, u32[]{:S(2)}) copy-start(bf16[512,128]{1,0:T(8,128)(2,1)} %get-tuple-element.39.q2_ref.q_ref) | copy-start | bytes 393220
  57.2 7.7 %copy-start.7 = (bf16[8,8192]{1,0:T(8,128)(2,1)}, bf16[8,8192]{1,0:T(8,128)(2,1)S(1)}, u32[]{:S(2)}) copy-start(bf16[8,8192]{1,0:T(8,128)(2,1)S(1)} %collective-permute-done.3.refs_3_) | copy-start | bytes 393220
  57.3 7.7 %copy-start.8 = (bf16[8,8192]{1,0:T(8,128)(2,1)}, bf16[8,8192]{1,0:T(8,128)(2,1)S(1)}, u32[]{:S(2)}) copy-start(bf16[8,8192]{1,0:T(8,128)(2,1)S(1)} %collective-permute-done.4.refs_4_) | copy-start | bytes 393220
  57.3 8.4 %copy-start.9 = (bf16[8,8192]{1,0:T(8,128)(2,1)}, bf16[8,8192]{1,0:T(8,128)(2,1)S(1)}, u32[]{:S(2)}) copy-start(bf16[8,8192]{1,0:T(8,128)(2,1)S(1)} %collective-permute-done.5.refs_5_) | copy-start | bytes 393220
  64.8 1.0 copy-start.10
  65.0 0.7 copy-start.11
  66.8 22.8 %collective-permute-start.8 = (bf16[64,32,128]{2,1,0:T(8,128)(2,1)S(1)}, bf16[64,32,128]{2,1,0:T(8,128)(2,1)S(1)}, u32[]{:S(2)}, u32[]{:S(2)}) collective-permute-start(bf16[64,32,128]{2,1,0:T(8,128)(2,1)S(1)} %get-tuple-element.42.refs_0_), channel_id=1, source_target_pairs={{0,16},{8,24},{16,32},{24,40},{32,48},{40,56},{48,0},{56,8},{64,80... | collective-permute-start | bytes 1572872 | tf_op jit(solution)/shard_map/ppermute | solution.py:356
  70.0 19.6 %collective-permute-start.9 = (bf16[64,32,128]{2,1,0:T(8,128)(2,1)S(1)}, bf16[64,32,128]{2,1,0:T(8,128)(2,1)S(1)}, u32[]{:S(2)}, u32[]{:S(2)}) collective-permute-start(bf16[64,32,128]{2,1,0:T(8,128)(2,1)S(1)} %get-tuple-element.42.refs_0_), channel_id=1, source_target_pairs={{0,48},{8,56},{16,0},{24,8},{32,16},{40,24},{48,32},{56,40},{64,11... | collective-permute-start | bytes 1572872 | tf_op jit(solution)/shard_map/ppermute | solution.py:357
  73.3 27.9 %all-to-all-start.1 = ((bf16[64,32,128]{2,1,0:T(8,128)(2,1)}), bf16[64,32,128]{2,1,0:T(8,128)(2,1)S(1)}, u32[]{:S(2)}, u32[]{:S(2)}) async-start(bf16[64,32,128]{2,1,0:T(8,128)(2,1)} %get-tuple-element.37), calls=%async_computation.1 | async-start | bytes 1048576 | tf_op jit(solution)/shard_map/all_to_all | solution.py:360
  83.5 1.0 copy-start.2
  84.4 0.9 copy-start.3
  92.2 7.7 %collective-permute-start.10 = (f32[512,256]{1,0:T(8,128)S(1)}, f32[512,256]{1,0:T(8,128)S(1)}, u32[]{:S(2)}, u32[]{:S(2)}) collective-permute-start(f32[512,256]{1,0:T(8,128)S(1)} %shard_map.128), channel_id=1, source_target_pairs={{0,8},{8,0},{16,24},{24,16},{32,40},{40,32},{48,56},{56,48},{64,72... | collective-permute-start | bytes 1572872 | tf_op jit(solution)/shard_map/ppermute | solution.py:343
  101.2 0.8 copy-start.4

commit v9 on v8

--- a/solution.py
+++ b/solution.py
@@ -131,10 +131,11 @@
     )(received, *after)
 
 
-def local_kernel(x_ref, b_ref, c_ref, d_ref, o_ref, token_ref):
+def local_kernel(x_ref, b_ref, c_ref, d_ref, o_ref, grow_ref, token_ref):
     token_ref[...] = jnp.zeros((8, HD), F32)
     cum = row_cumulative(d_ref[...])
     cum_col = col_cumulative(d_ref[...])
+    grow_ref[...] = jnp.exp(cum_col)
     cross = lax.dot_general(
         c_ref[...], b_ref[...], (((1,), (1,)), ((), ())), preferred_element_type=F32
     )
@@ -153,9 +154,13 @@
 def local_part(x_in, b_in, c_in, decay_log):
     return pl.pallas_call(
         local_kernel,
-        out_shape=[jax.ShapeDtypeStruct((L, MH * HD), F32), TOKEN],
+        out_shape=[
+            jax.ShapeDtypeStruct((L, MH * HD), F32),
+            jax.ShapeDtypeStruct((L, MH), F32),
+            TOKEN,
+        ],
         in_specs=[VM] * 4,
-        out_specs=[VM] * 2,
+        out_specs=[VM] * 3,
         compiler_params=params(LARGE),
         cost_estimate=cost(1 << 28, 1 << 21),
     )(x_in, b_in, c_in, decay_log)
@@ -164,8 +169,8 @@
 JOIN_COST = 1 << 26
 
 
-def join_kernel(l_ref, e_ref, c_ref, d_ref, _, o_ref):
-    grow = jnp.exp(col_cumulative(d_ref[...]))
+def join_kernel(l_ref, e_ref, c_ref, g_ref, _, o_ref):
+    grow = g_ref[...]
     c = c_ref[...]
     for h in range(MH):
         cols = slice(h * HD, (h + 1) * HD)
@@ -173,16 +178,16 @@
         o_ref[:, cols] = (l_ref[:, cols] + grow[:, h : h + 1] * readout).astype(BF16)
 
 
-def join_mamba(local, entering, c_in, decay_log, after):
+def join_mamba(local, entering, c_in, grow, after):
     return pl.pallas_call(
         join_kernel,
         grid=(1,),
         out_shape=jax.ShapeDtypeStruct((L, MH * HD), BF16),
-        in_specs=[full(a.shape) for a in (local, entering, c_in, decay_log)] + [TILE],
+        in_specs=[full(a.shape) for a in (local, entering, c_in, grow)] + [TILE],
         out_specs=full((L, MH * HD)),
         compiler_params=params(LARGE),
         cost_estimate=cost(JOIN_COST, 1 << 21),
-    )(local, entering, c_in, decay_log, after)
+    )(local, entering, c_in, grow, after)
 
 
 ROWS = QH * L
@@ -219,33 +224,24 @@
     return ref[:, at : at + 1], jnp.where(lane == 0, ref[:, at + L - 1 : at + L], 0.0)
 
 
-def open_kernel(q_ref, q2_ref, k_ref, v_ref, _, s_ref, s2_ref, ml_ref, a_ref, token_ref):
+def stack_kernel(q_ref, q2_ref, _, s_ref, s2_ref, token_ref):
     token_ref[...] = jnp.zeros((8, HD), F32)
-    q = stacked_queries(q_ref)
-    s_ref[...] = q
+    s_ref[...] = stacked_queries(q_ref)
     s2_ref[...] = stacked_queries(q2_ref)
-    s = scores(q, k_ref[...])
-    t = lax.broadcasted_iota(jnp.int32, s.shape, 0) % L
-    u = lax.broadcasted_iota(jnp.int32, s.shape, 1)
-    s = jnp.where(u <= t, s, -1e30)
-    m = jnp.max(s, axis=1, keepdims=True)
-    p = jnp.exp2((s - m) * SCALE2)
-    ml_ref[...] = packed(m, p)
-    a_ref[...] = jnp.dot(p.astype(BF16), v_ref[...], preferred_element_type=F32)
 
 
 PART = jax.ShapeDtypeStruct((ROWS, L), F32)
 
 
-def open_attention(q_in, q_other, k_in, v_in, after):
-    return pl.pallas_call(
-        open_kernel,
-        out_shape=[jax.ShapeDtypeStruct((ROWS, HD), BF16)] * 2 + [PART] * 2 + [TOKEN],
-        in_specs=[VM] * 5,
-        out_specs=[VM] * 5,
-        compiler_params=params(LARGE),
-        cost_estimate=cost(1 << 27, 1 << 20),
-    )(q_in, q_other, k_in, v_in, after)
+def stack_both(q_in, q_other, after):
+    return pl.pallas_call(
+        stack_kernel,
+        out_shape=[jax.ShapeDtypeStruct((ROWS, HD), BF16)] * 2 + [TOKEN],
+        in_specs=[VM] * 3,
+        out_specs=[VM] * 3,
+        compiler_params=params(LARGE),
+        cost_estimate=cost(1 << 20, 1 << 19),
+    )(q_in, q_other, after)
 
 
 def go_on(me, q, state, sets):
@@ -259,10 +255,18 @@
     return state
 
 
-def early_kernel(me_ref, q_ref, q2_ref, ml_ref, a_ref, *refs):
+def early_kernel(me_ref, q_ref, q2_ref, k_ref, v_ref, *refs):
     sets, (ml1_ref, a1_ref, ml2_ref, a2_ref) = refs[:2], refs[2:]
     me = me_ref[0]
-    m, total, acc = go_on(me, q_ref[...], (*unpacked(ml_ref), a_ref[...]), sets)
+    q = q_ref[...]
+    s = scores(q, k_ref[...])
+    t = lax.broadcasted_iota(jnp.int32, s.shape, 0) % L
+    u = lax.broadcasted_iota(jnp.int32, s.shape, 1)
+    s = jnp.where(u <= t, s, -1e30)
+    m = jnp.max(s, axis=1, keepdims=True)
+    p = jnp.exp2((s - m) * SCALE2)
+    acc = jnp.dot(p.astype(BF16), v_ref[...], preferred_element_type=F32)
+    m, total, acc = go_on(me, q, (m, p, acc), sets)
     ml1_ref[...] = packed(m, total)
     a1_ref[...] = acc
     none = jnp.full((ROWS, 1), -1e30, F32), jnp.zeros((ROWS, L), F32), jnp.zeros((ROWS, HD), F32)
@@ -271,7 +275,7 @@
     a2_ref[...] = acc
 
 
-def early_attention(me, q_own, q_other, ml, acc, sets):
+def early_attention(me, q_own, q_other, k_in, v_in, sets):
     return pl.pallas_call(
         early_kernel,
         out_shape=[PART] * 4,
@@ -279,7 +283,7 @@
         out_specs=[VM] * 4,
         compiler_params=params(),
         cost_estimate=cost(1 << 29, 1 << 22),
-    )(me, q_own, q_other, ml, acc, *sets)
+    )(me, q_own, q_other, k_in, v_in, *sets)
 
 
 def other_kernel(me_ref, q_ref, ml_ref, a_ref, r_ref, l_ref, o_ref):
@@ -348,15 +352,15 @@
     chunks = chunks_to_send(x_in, b_in, decay_log, k_in, v_in)
     received = lax.all_to_all(chunks, "ctx", split_axis=0, concat_axis=0, tiled=True)
     q_other = other_core(q_in)
-    local, token = local_part(x_in, b_in, c_in, decay_log)
-    q_own, q_other, ml, acc, token = open_attention(q_in, q_other, k_in, v_in, token)
+    local, grow, token = local_part(x_in, b_in, c_in, decay_log)
+    q_own, q_other, token = stack_both(q_in, q_other, token)
     blocks = expert_blocks(expert_out, [chunks.reshape(NCTX * CHUNK, HD)])
     arrived = sum((b[:8, :HD] for b in blocks[1:]), token.astype(BF16))
     own, opposite, entering = take_received(received, [arrived])
     right = lax.ppermute(own, "ctx", along_x(1))
     left = lax.ppermute(own, "ctx", along_x(-1))
 
-    ml, acc, ml2, acc2 = early_attention(me, q_own, q_other, ml, acc, [own, opposite])
+    ml, acc, ml2, acc2 = early_attention(me, q_own, q_other, k_in, v_in, [own, opposite])
     entering = lax.all_to_all(entering, "ctx", split_axis=0, concat_axis=0, tiled=True)
 
     sets = [right, left]
@@ -365,7 +369,7 @@
     part = other_core(part)
     ml, acc = late_attention(own_kernel, [PART] * 2, me, q_own, ml, acc, sets)
     attn_out = merge_attention(ml, acc, part)
-    mamba_out = join_mamba(local, entering.reshape(MH * L, HD), c_in, decay_log, attn_out)
+    mamba_out = join_mamba(local, entering.reshape(MH * L, HD), c_in, grow, attn_out)
     return mamba_out, attn_out, blocks
 
 

time: 106 us -> 105 us (level)
  waiting for transfers between devices: 7.92 us -> 10.7 us
  local copies, waits for them, and re-layouts: 2.74 us -> 0.69 us
  Pallas kernels: 27.2 us -> 25.8 us
    all_to_all x1, waiting for transfers between devices: 0.22 us -> 2.6 us  [context_parts(): lax.all_to_all(entering, 'ctx', split_axis=0, concat_axis=0, tiled=True)]
    unnamed x28 -> x26, local copies, waits for them, and re-layouts: 2.74 us -> 0.69 us
  transfers between devices with their start and end apart: 13 -> 13, of which waited for: 3 -> 3; matrix products, arithmetic and copies ran while one was open for 1% -> 1% of each run, Pallas kernels for 19% -> 18%
where the time goes in v9:
time: 105 us; the launch traced here: 104 us
  starting transfers between devices  65.6 us (62%)
  Pallas kernels  25.8 us (25%)
  waiting for transfers between devices  10.7 us (10%)
    ppermute x7, starting transfers between devices, expert_blocks(): blocks[d] = lax.ppermute(held[d], 'grp', pairs)  31.6 us
    all_to_all x1, starting transfers between devices, context_parts(): lax.all_to_all(chunks, 'ctx', split_axis=0, concat_axis=0, tiled=True)  11.6 us
    all_to_all x1, starting transfers between devices, context_parts(): lax.all_to_all(entering, 'ctx', split_axis=0, concat_axis=0, tiled=True)  10.3 us
    ppermute x7, waiting for transfers between devices, expert_blocks(): blocks[d] = lax.ppermute(held[d], 'grp', pairs)  8.13 us
    ppermute x2, starting transfers between devices, other_core(): return lax.ppermute(value, 'ctx', [(i, i ^ 1) for i in range(NCTX)])  5.54 us
    pallas_call x2, Pallas kernels, late_attention(): pl.pallas_call(kernel, out_shape=outs, in_specs=[SM] + [VM] * 5, out_spec...  5.06 us
    pallas_call x1, Pallas kernels, early_attention(): pl.pallas_call(early_kernel, out_shape=[PART] * 4, in_specs=[SM] + [VM] *...  3.57 us
    ppermute x1, starting transfers between devices, context_parts(): left = lax.ppermute(own, 'ctx', along_x(-1))  3.29 us
  transfers between devices with their start and end apart: 13, of which 3 were waited for; matrix products, arithmetic and copies ran while one was open for 1% of the time, Pallas kernels for 18%

profile of v9, /device:TPU:1, one launch (start us, length us, event | category | flops | bytes accessed | tf_op | source)
XLA Modules:
  0.0 104.5 jit_solution(4880236114282619558)
XLA Ops:
  0.6 3.0 %shard_map.122 = bf16[64,104,128]{2,1,0:T(8,128)(2,1)} custom-call(bf16[128,2048]{1,0:T(8,128)(2,1)} %x_ref.3, bf16[128,128]{1,0:T(8,128)(2,1)} %b_ref.3, f32[16,128]{1,0:T(8,128)} %d_ref.3, bf16[128,128]{1,0:T(8,128)(2,1)} %k_ref.3, bf16[128,128]{1,0:T(8,128)(2,1)} %v_ref.3), custom_call_target="tpu_custom_call" | custom-call | flops 67108864 | bytes 2097152 | tf_op jit(solution)/shard_map/pallas_call | solution.py:94
  3.7 11.6 %all-to-all-start = ((bf16[64,104,128]{2,1,0:T(8,128)(2,1)}), bf16[64,104,128]{2,1,0:T(8,128)(2,1)S(1)}, u32[]{:S(2)}, u32[]{:S(2)}) async-start(bf16[64,104,128]{2,1,0:T(8,128)(2,1)} %shard_map.122), calls=%async_computation | async-start | bytes 3407872 | tf_op jit(solution)/shard_map/all_to_all | solution.py:353
  15.3 0.0 copy-start.11
  15.3 2.2 %shard_map.124 = (bf16[8,8192]{1,0:T(8,128)(2,1)}, bf16[8,8192]{1,0:T(8,128)(2,1)}, bf16[8,8192]{1,0:T(8,128)(2,1)}, bf16[8,8192]{1,0:T(8,128)(2,1)}, bf16[8,819...) custom-call(s32[1]{0:T(128)} %bitcast.refs_0_.me_ref, ...), custom_call_target="tpu_custom_call" | custom-call | flops 1048576 | bytes 2097152 | tf_op jit(solution)/shard_map/pallas_call | solution.py:422
  17.5 4.0 %collective-permute-start.1 = (bf16[8,8192]{1,0:T(8,128)(2,1)}, bf16[8,8192]{1,0:T(8,128)(2,1)S(1)}, u32[]{:S(2)}, u32[]{:S(2)}) collective-permute-start(bf16[8,8192]{1,0:T(8,128)(2,1)} %get-tuple-element.29), channel_id=1, source_target_pairs={{0,1},{1,2},{2,3},{3,4},{4,5},{5,6},{6,7},{7,0},{8,9},{9,10},{10,1... | collective-permute-start | bytes 393224 | tf_op jit(solution)/shard_map/ppermute | solution.py:434
  21.5 5.8 %collective-permute-start.2 = (bf16[8,8192]{1,0:T(8,128)(2,1)}, bf16[8,8192]{1,0:T(8,128)(2,1)S(1)}, u32[]{:S(2)}, u32[]{:S(2)}) collective-permute-start(bf16[8,8192]{1,0:T(8,128)(2,1)} %get-tuple-element.30), channel_id=1, source_target_pairs={{0,2},{1,3},{2,4},{3,5},{4,6},{5,7},{6,0},{7,1},{8,10},{9,11},{10,... | collective-permute-start | bytes 393224 | tf_op jit(solution)/shard_map/ppermute | solution.py:434
  27.4 2.9 %collective-permute-start = (bf16[128,512]{1,0:T(8,128)(2,1)S(1)}, bf16[128,512]{1,0:T(8,128)(2,1)S(1)}, u32[]{:S(2)}, u32[]{:S(2)}) collective-permute-start(bf16[128,512]{1,0:T(8,128)(2,1)S(1)} %copy-done.11), channel_id=1, source_target_pairs={{0,8},{8,0},{16,24},{24,16},{32,40},{40,32},{48,56},{56,48},{64,72... | collective-permute-start | bytes 393224 | tf_op jit(solution)/shard_map/ppermute | solution.py:347
  30.3 7.0 %collective-permute-start.3 = (bf16[8,8192]{1,0:T(8,128)(2,1)}, bf16[8,8192]{1,0:T(8,128)(2,1)S(1)}, u32[]{:S(2)}, u32[]{:S(2)}) collective-permute-start(bf16[8,8192]{1,0:T(8,128)(2,1)} %get-tuple-element.31), channel_id=1, source_target_pairs={{0,3},{1,4},{2,5},{3,6},{4,7},{5,0},{6,1},{7,2},{8,11},{9,12},{10,... | collective-permute-start | bytes 393224 | tf_op jit(solution)/shard_map/ppermute | solution.py:434
  37.3 2.8 %collective-permute-start.4 = (bf16[8,8192]{1,0:T(8,128)(2,1)}, bf16[8,8192]{1,0:T(8,128)(2,1)S(1)}, u32[]{:S(2)}, u32[]{:S(2)}) collective-permute-start(bf16[8,8192]{1,0:T(8,128)(2,1)} %get-tuple-element.32), channel_id=1, source_target_pairs={{0,4},{1,5},{2,6},{3,7},{4,0},{5,1},{6,2},{7,3},{8,12},{9,13},{10,... | collective-permute-start | bytes 393224 | tf_op jit(solution)/shard_map/ppermute | solution.py:434
  40.2 0.0 collective-permute-done.1.refs_1_
  40.2 0.0 copy-start.4
  40.2 6.4 %collective-permute-start.5 = (bf16[8,8192]{1,0:T(8,128)(2,1)}, bf16[8,8192]{1,0:T(8,128)(2,1)S(1)}, u32[]{:S(2)}, u32[]{:S(2)}) collective-permute-start(bf16[8,8192]{1,0:T(8,128)(2,1)} %get-tuple-element.33), channel_id=1, source_target_pairs={{0,5},{1,6},{2,7},{3,0},{4,1},{5,2},{6,3},{7,4},{8,13},{9,14},{10,... | collective-permute-start | bytes 393224 | tf_op jit(solution)/shard_map/ppermute | solution.py:434
  46.6 0.0 collective-permute-done.2.refs_2_
  46.6 0.0 copy-start.5
  46.6 3.4 %collective-permute-start.6 = (bf16[8,8192]{1,0:T(8,128)(2,1)}, bf16[8,8192]{1,0:T(8,128)(2,1)S(1)}, u32[]{:S(2)}, u32[]{:S(2)}) collective-permute-start(bf16[8,8192]{1,0:T(8,128)(2,1)} %get-tuple-element.34), channel_id=1, source_target_pairs={{0,6},{1,7},{2,0},{3,1},{4,2},{5,3},{6,4},{7,5},{8,14},{9,15},{10,... | collective-permute-start | bytes 393224 | tf_op jit(solution)/shard_map/ppermute | solution.py:434
  50.0 0.0 collective-permute-done.q2_ref
  50.0 0.0 copy-start.12
  50.0 2.2 %collective-permute-start.7 = (bf16[8,8192]{1,0:T(8,128)(2,1)}, bf16[8,8192]{1,0:T(8,128)(2,1)S(1)}, u32[]{:S(2)}, u32[]{:S(2)}) collective-permute-start(bf16[8,8192]{1,0:T(8,128)(2,1)} %get-tuple-element.35), channel_id=1, source_target_pairs={{0,7},{1,0},{2,1},{3,2},{4,3},{5,4},{6,5},{7,6},{8,15},{9,8},{10,9... | collective-permute-start | bytes 393224 | tf_op jit(solution)/shard_map/ppermute | solution.py:434
  52.2 2.9 %shard_map.121 = (f32[128,2048]{1,0:T(8,128)}, f32[128,16]{1,0:T(8,128)}, f32[8,128]{1,0:T(8,128)}) custom-call(bf16[128,2048]{1,0:T(8,128)(2,1)} %x_ref.3, bf16[128,128]{1,0:T(8,128)(2,1)} %b_ref.3, bf16[128,128]{1,0:T(8,128)(2,1)} %c_ref.3, f32[16,128]{1,0:T(8,128)} %d_ref.3), custom_call_target="tpu_custom_call" | custom-call | flops 268435456 | bytes 2097152 | tf_op jit(solution)/shard_map/pallas_call | solution.py:155
  55.1 1.7 %shard_map.123 = (bf16[512,128]{1,0:T(8,128)(2,1)}, bf16[512,128]{1,0:T(8,128)(2,1)}, f32[8,128]{1,0:T(8,128)}) custom-call(bf16[128,512]{1,0:T(8,128)(2,1)} %q_ref.1, bf16[128,512]{1,0:T(8,128)(2,1)} %copy-done.12, f32[8,128]{1,0:T(8,128)} %get-tuple-element.27._), custom_call_target="tpu_custom_call" | custom-call | flops 1048576 | bytes 524288 | tf_op jit(solution)/shard_map/pallas_call | solution.py:237
  56.8 0.0 collective-permute-done.3.refs_3_
  56.8 0.0 collective-permute-done.4.refs_4_
  56.8 0.0 collective-permute-done.5.refs_5_
  56.8 7.9 %collective-permute-done.6.refs_6_ = bf16[8,8192]{1,0:T(8,128)(2,1)S(1)} collective-permute-done((bf16[8,8192]{1,0:T(8,128)(2,1)}, bf16[8,8192]{1,0:T(8,128)(2,1)S(1)}, u32[]{:S(2)}, u32[]{:S(2)}) %collective-permute-start.6) | collective-permute-done | bytes 131104 | tf_op jit(solution)/shard_map/ppermute | solution.py:434
  64.8 0.2 collective-permute-done.7.refs_7_
  65.0 0.0 copy-done.7
  65.0 0.4 copy-done.9
  65.4 0.2 copy-done.10
  65.6 0.7 slice_add_fusion.refs_0_
  66.3 0.0 all-to-all-done.s_ref
  66.3 1.1 %shard_map.125 = (bf16[64,32,128]{2,1,0:T(8,128)(2,1)S(1)}, bf16[64,32,128]{2,1,0:T(8,128)(2,1)S(1)}, bf16[64,32,128]{2,1,0:T(8,128)(2,1)}) custom-call(bf16[64,104,128]{2,1,0:T(8,128)(2,1)S(1)} %all-to-all-done.s_ref, bf16[8,128]{1,0:T(8,128)(2,1)S(1)} %slice_add_fusion.refs_0_), custom_call_target="tpu_custom_call" | custom-call | flops 1048576 | bytes 2097152 | tf_op jit(solution)/shard_map/pallas_call | solution.py:119
  67.4 3.2 %collective-permute-start.8 = (bf16[64,32,128]{2,1,0:T(8,128)(2,1)S(1)}, bf16[64,32,128]{2,1,0:T(8,128)(2,1)S(1)}, u32[]{:S(2)}, u32[]{:S(2)}) collective-permute-start(bf16[64,32,128]{2,1,0:T(8,128)(2,1)S(1)} %get-tuple-element.40.refs_0_), channel_id=1, source_target_pairs={{0,16},{8,24},{16,32},{24,40},{32,48},{40,56},{48,0},{56,8},{64,80... | collective-permute-start | bytes 1572872 | tf_op jit(solution)/shard_map/ppermute | solution.py:360
  70.6 3.3 %collective-permute-start.9 = (bf16[64,32,128]{2,1,0:T(8,128)(2,1)S(1)}, bf16[64,32,128]{2,1,0:T(8,128)(2,1)S(1)}, u32[]{:S(2)}, u32[]{:S(2)}) collective-permute-start(bf16[64,32,128]{2,1,0:T(8,128)(2,1)S(1)} %get-tuple-element.40.refs_0_), channel_id=1, source_target_pairs={{0,48},{8,56},{16,0},{24,8},{32,16},{40,24},{48,32},{56,40},{64,11... | collective-permute-start | bytes 1572872 | tf_op jit(solution)/shard_map/ppermute | solution.py:361
  73.9 10.3 %all-to-all-start.1 = ((bf16[64,32,128]{2,1,0:T(8,128)(2,1)}), bf16[64,32,128]{2,1,0:T(8,128)(2,1)}, u32[]{:S(2)}, u32[]{:S(2)}) async-start(bf16[64,32,128]{2,1,0:T(8,128)(2,1)} %get-tuple-element.36), calls=%async_computation.1 | async-start | bytes 1048576 | tf_op jit(solution)/shard_map/all_to_all | solution.py:364
  84.2 0.0 copy-done.2
  84.2 0.0 copy-done.3
  84.3 0.0 copy-done
  84.3 3.6 %shard_map.126 = (f32[512,128]{1,0:T(8,128)S(1)}, f32[512,128]{1,0:T(8,128)S(1)}, f32[512,128]{1,0:T(8,128)S(1)}, f32[512,128]{1,0:T(8,128)S(1)}) custom-call(s32[1]{0:T(128)} %bitcast.3.me_ref, bf16[512,128]{1,0:T(8,128)(2,1)S(1)} %copy-done, bf16[512,128]{1,0:T(8,128)(2,1)S(1)} %copy-done.1, bf16[128,128]{1,0:T(8,128)(2,1)S(1)} %copy-done.2, ...), custom_call_target="tpu_custom_call" | custom-call | flops 536870912 | bytes 4194304 | tf_op jit(solution)/shard_map/pallas_call | solution.py:279
  87.9 0.0 collective-permute-done.8.r_ref
  87.9 0.0 collective-permute-done.9.l_ref
  87.9 2.5 %shard_map.128 = f32[512,256]{1,0:T(8,128)S(1)} custom-call(s32[1]{0:T(128)} %bitcast.3.me_ref, bf16[512,128]{1,0:T(8,128)(2,1)S(1)} %copy-done.1, f32[512,128]{1,0:T(8,128)S(1)} %get-tuple-element.46.ml_ref, f32[512,128]{1,0:T(8,128)S(1)} %get-tuple-element.47.a_ref, bf16[64,32,128]{2,1,0:T(8,128)(2,1)S(1)} %collective-permute-done.8.r_ref, ...), custom_call_target="tpu_custom_call" | custom-call | flops 268435456 | bytes 2097152 | tf_op jit(solution)/shard_map/pallas_call | solution.py:304
  90.4 2.6 %collective-permute-start.10 = (f32[512,256]{1,0:T(8,128)S(1)}, f32[512,256]{1,0:T(8,128)S(1)}, u32[]{:S(2)}, u32[]{:S(2)}) collective-permute-start(f32[512,256]{1,0:T(8,128)S(1)} %shard_map.128), channel_id=1, source_target_pairs={{0,8},{8,0},{16,24},{24,16},{32,40},{40,32},{48,56},{56,48},{64,72... | collective-permute-start | bytes 1572872 | tf_op jit(solution)/shard_map/ppermute | solution.py:347
  93.0 2.6 %shard_map.131 = bf16[16,8192]{1,0:T(8,128)(2,1)} custom-call(s32[1]{0:T(128)} %bitcast.refs_0_.me_ref, s32[2,16]{1,0:T(2,128)} %bitcast.7, f32[2,16]{1,0:T(2,128)} %bitcast.8, bf16[8,8192]{1,0:T(8,128)(2,1)} %get-tuple-element.48.refs_0_, bf16[8,8192]{1,0:T(8,128)(2,1)} %copy-done.4, bf16[8,8192]{1,0:T(8,128)(2,1)} %copy-done.5, bf16[8,8192]{1,0:T(8,128)(2,1)} %copy-done.6, ...), custom_call_target="tpu_custom_call" | custom-call | flops 16777216 | bytes 1048576 | tf_op jit(solution)/shard_map/pallas_call | solution.py:443
  95.6 2.5 %shard_map.127 = (f32[512,128]{1,0:T(8,128)S(1)}, f32[512,128]{1,0:T(8,128)S(1)}) custom-call(s32[1]{0:T(128)} %bitcast.3.me_ref, bf16[512,128]{1,0:T(8,128)(2,1)S(1)} %copy-done, f32[512,128]{1,0:T(8,128)S(1)} %get-tuple-element.42.ml_ref, f32[512,128]{1,0:T(8,128)S(1)} %get-tuple-element.43.a_ref, bf16[64,32,128]{2,1,0:T(8,128)(2,1)S(1)} %collective-permute-done.8.r_ref, ...), custom_call_target="tpu_custom_call" | custom-call | flops 268435456 | bytes 2097152 | tf_op jit(solution)/shard_map/pallas_call | solution.py:304
  98.2 0.0 collective-permute-done.10.p_ref
  98.2 1.1 %shard_map.129._ = bf16[128,512]{1,0:T(8,128)(2,1)} custom-call(f32[512,128]{1,0:T(8,128)S(1)} %get-tuple-element.44.ml_ref, f32[512,128]{1,0:T(8,128)S(1)} %get-tuple-element.45.a_ref, f32[512,256]{1,0:T(8,128)S(1)} %collective-permute-done.10.p_ref), custom_call_target="tpu_custom_call" | custom-call | flops 1048576 | bytes 1048576 | tf_op jit(solution)/shard_map/pallas_call | solution.py:325
  99.3 2.6 %all-to-all-done.1 = bf16[64,32,128]{2,1,0:T(8,128)(2,1)} async-done(((bf16[64,32,128]{2,1,0:T(8,128)(2,1)}), bf16[64,32,128]{2,1,0:T(8,128)(2,1)}, u32[]{:S(2)}, u32[]{:S(2)}) %all-to-all-start.1) | async-done | bytes 524320 | tf_op jit(solution)/shard_map/all_to_all | solution.py:364
  101.9 2.6 %shard_map.130 = bf16[128,2048]{1,0:T(8,128)(2,1)} custom-call(f32[128,2048]{1,0:T(8,128)} %get-tuple-element.26.l_ref, bf16[2048,128]{1,0:T(8,128)(2,1)} %bitcast.2.e_ref, bf16[128,128]{1,0:T(8,128)(2,1)} %c_ref.3, f32[128,16]{1,0:T(8,128)} %get-tuple-element.37.g_ref, bf16[128,512]{1,0:T(8,128)(2,1)} %shard_map.129._), custom_call_target="tpu_custom_call" | custom-call | flops 67108864 | bytes 2097152 | tf_op jit(solution)/shard_map/pallas_call | solution.py:182
  (16 shorter events, 0.0 us)
Async XLA Ops:
  3.7 62.7 %all-to-all-start = ((bf16[64,104,128]{2,1,0:T(8,128)(2,1)}), bf16[64,104,128]{2,1,0:T(8,128)(2,1)S(1)}, u32[]{:S(2)}, u32[]{:S(2)}) async-start(bf16[64,104,128]{2,1,0:T(8,128)(2,1)} %shard_map.122), calls=%async_computation | async-start | bytes 3407872 | tf_op jit(solution)/shard_map/all_to_all | solution.py:353
  15.3 12.1 %copy-start.11 = (bf16[128,512]{1,0:T(8,128)(2,1)S(1)}, bf16[128,512]{1,0:T(8,128)(2,1)}, u32[]{:S(2)}) copy-start(bf16[128,512]{1,0:T(8,128)(2,1)} %q_ref.1) | copy-start | bytes 393220
  17.5 22.6 %collective-permute-start.1 = (bf16[8,8192]{1,0:T(8,128)(2,1)}, bf16[8,8192]{1,0:T(8,128)(2,1)S(1)}, u32[]{:S(2)}, u32[]{:S(2)}) collective-permute-start(bf16[8,8192]{1,0:T(8,128)(2,1)} %get-tuple-element.29), channel_id=1, source_target_pairs={{0,1},{1,2},{2,3},{3,4},{4,5},{5,6},{6,7},{7,0},{8,9},{9,10},{10,1... | collective-permute-start | bytes 393224 | tf_op jit(solution)/shard_map/ppermute | solution.py:434
  21.5 25.0 %collective-permute-start.2 = (bf16[8,8192]{1,0:T(8,128)(2,1)}, bf16[8,8192]{1,0:T(8,128)(2,1)S(1)}, u32[]{:S(2)}, u32[]{:S(2)}) collective-permute-start(bf16[8,8192]{1,0:T(8,128)(2,1)} %get-tuple-element.30), channel_id=1, source_target_pairs={{0,2},{1,3},{2,4},{3,5},{4,6},{5,7},{6,0},{7,1},{8,10},{9,11},{10,... | collective-permute-start | bytes 393224 | tf_op jit(solution)/shard_map/ppermute | solution.py:434
  27.4 22.6 %collective-permute-start = (bf16[128,512]{1,0:T(8,128)(2,1)S(1)}, bf16[128,512]{1,0:T(8,128)(2,1)S(1)}, u32[]{:S(2)}, u32[]{:S(2)}) collective-permute-start(bf16[128,512]{1,0:T(8,128)(2,1)S(1)} %copy-done.11), channel_id=1, source_target_pairs={{0,8},{8,0},{16,24},{24,16},{32,40},{40,32},{48,56},{56,48},{64,72... | collective-permute-start | bytes 393224 | tf_op jit(solution)/shard_map/ppermute | solution.py:347
  30.3 26.5 %collective-permute-start.3 = (bf16[8,8192]{1,0:T(8,128)(2,1)}, bf16[8,8192]{1,0:T(8,128)(2,1)S(1)}, u32[]{:S(2)}, u32[]{:S(2)}) collective-permute-start(bf16[8,8192]{1,0:T(8,128)(2,1)} %get-tuple-element.31), channel_id=1, source_target_pairs={{0,3},{1,4},{2,5},{3,6},{4,7},{5,0},{6,1},{7,2},{8,11},{9,12},{10,... | collective-permute-start | bytes 393224 | tf_op jit(solution)/shard_map/ppermute | solution.py:434
  37.3 19.5 %collective-permute-start.4 = (bf16[8,8192]{1,0:T(8,128)(2,1)}, bf16[8,8192]{1,0:T(8,128)(2,1)S(1)}, u32[]{:S(2)}, u32[]{:S(2)}) collective-permute-start(bf16[8,8192]{1,0:T(8,128)(2,1)} %get-tuple-element.32), channel_id=1, source_target_pairs={{0,4},{1,5},{2,6},{3,7},{4,0},{5,1},{6,2},{7,3},{8,12},{9,13},{10,... | collective-permute-start | bytes 393224 | tf_op jit(solution)/shard_map/ppermute | solution.py:434
  40.2 33.7 %copy-start.4 = (bf16[8,8192]{1,0:T(8,128)(2,1)}, bf16[8,8192]{1,0:T(8,128)(2,1)S(1)}, u32[]{:S(2)}) copy-start(bf16[8,8192]{1,0:T(8,128)(2,1)S(1)} %collective-permute-done.1.refs_1_) | copy-start | bytes 393220
  40.2 16.6 %collective-permute-start.5 = (bf16[8,8192]{1,0:T(8,128)(2,1)}, bf16[8,8192]{1,0:T(8,128)(2,1)S(1)}, u32[]{:S(2)}, u32[]{:S(2)}) collective-permute-start(bf16[8,8192]{1,0:T(8,128)(2,1)} %get-tuple-element.33), channel_id=1, source_target_pairs={{0,5},{1,6},{2,7},{3,0},{4,1},{5,2},{6,3},{7,4},{8,13},{9,14},{10,... | collective-permute-start | bytes 393224 | tf_op jit(solution)/shard_map/ppermute | solution.py:434
  46.6 27.3 %copy-start.5 = (bf16[8,8192]{1,0:T(8,128)(2,1)}, bf16[8,8192]{1,0:T(8,128)(2,1)S(1)}, u32[]{:S(2)}) copy-start(bf16[8,8192]{1,0:T(8,128)(2,1)S(1)} %collective-permute-done.2.refs_2_) | copy-start | bytes 393220
  46.6 18.2 %collective-permute-start.6 = (bf16[8,8192]{1,0:T(8,128)(2,1)}, bf16[8,8192]{1,0:T(8,128)(2,1)S(1)}, u32[]{:S(2)}, u32[]{:S(2)}) collective-permute-start(bf16[8,8192]{1,0:T(8,128)(2,1)} %get-tuple-element.34), channel_id=1, source_target_pairs={{0,6},{1,7},{2,0},{3,1},{4,2},{5,3},{6,4},{7,5},{8,14},{9,15},{10,... | collective-permute-start | bytes 393224 | tf_op jit(solution)/shard_map/ppermute | solution.py:434
  50.0 5.1 %copy-start.12 = (bf16[128,512]{1,0:T(8,128)(2,1)}, bf16[128,512]{1,0:T(8,128)(2,1)S(1)}, u32[]{:S(2)}) copy-start(bf16[128,512]{1,0:T(8,128)(2,1)S(1)} %collective-permute-done.q2_ref) | copy-start | bytes 393220
  50.0 15.0 %collective-permute-start.7 = (bf16[8,8192]{1,0:T(8,128)(2,1)}, bf16[8,8192]{1,0:T(8,128)(2,1)S(1)}, u32[]{:S(2)}, u32[]{:S(2)}) collective-permute-start(bf16[8,8192]{1,0:T(8,128)(2,1)} %get-tuple-element.35), channel_id=1, source_target_pairs={{0,7},{1,0},{2,1},{3,2},{4,3},{5,4},{6,5},{7,6},{8,15},{9,8},{10,9... | collective-permute-start | bytes 393224 | tf_op jit(solution)/shard_map/ppermute | solution.py:434
  55.0 29.2 %copy-start.2 = (bf16[128,128]{1,0:T(8,128)(2,1)S(1)}, bf16[128,128]{1,0:T(8,128)(2,1)}, u32[]{:S(2)}) copy-start(bf16[128,128]{1,0:T(8,128)(2,1)} %k_ref.3) | copy-start | bytes 98308
  55.0 29.2 %copy-start.3 = (bf16[128,128]{1,0:T(8,128)(2,1)S(1)}, bf16[128,128]{1,0:T(8,128)(2,1)}, u32[]{:S(2)}) copy-start(bf16[128,128]{1,0:T(8,128)(2,1)} %v_ref.3) | copy-start | bytes 98308
  56.8 27.5 %copy-start = (bf16[512,128]{1,0:T(8,128)(2,1)S(1)}, bf16[512,128]{1,0:T(8,128)(2,1)}, u32[]{:S(2)}) copy-start(bf16[512,128]{1,0:T(8,128)(2,1)} %get-tuple-element.38.q_ref) | copy-start | bytes 393220
  56.8 27.5 %copy-start.1 = (bf16[512,128]{1,0:T(8,128)(2,1)S(1)}, bf16[512,128]{1,0:T(8,128)(2,1)}, u32[]{:S(2)}) copy-start(bf16[512,128]{1,0:T(8,128)(2,1)} %get-tuple-element.39.q2_ref.q_ref) | copy-start | bytes 393220
  56.8 31.1 %copy-start.6 = (bf16[8,8192]{1,0:T(8,128)(2,1)}, bf16[8,8192]{1,0:T(8,128)(2,1)S(1)}, u32[]{:S(2)}) copy-start(bf16[8,8192]{1,0:T(8,128)(2,1)S(1)} %collective-permute-done.3.refs_3_) | copy-start | bytes 393220
  56.8 8.2 %copy-start.7 = (bf16[8,8192]{1,0:T(8,128)(2,1)}, bf16[8,8192]{1,0:T(8,128)(2,1)S(1)}, u32[]{:S(2)}) copy-start(bf16[8,8192]{1,0:T(8,128)(2,1)S(1)} %collective-permute-done.4.refs_4_) | copy-start | bytes 393220
  56.8 8.1 %copy-start.8 = (bf16[8,8192]{1,0:T(8,128)(2,1)}, bf16[8,8192]{1,0:T(8,128)(2,1)S(1)}, u32[]{:S(2)}) copy-start(bf16[8,8192]{1,0:T(8,128)(2,1)S(1)} %collective-permute-done.5.refs_5_) | copy-start | bytes 393220
  64.8 0.6 copy-start.9
  65.0 0.6 copy-start.10
  67.4 20.5 %collective-permute-start.8 = (bf16[64,32,128]{2,1,0:T(8,128)(2,1)S(1)}, bf16[64,32,128]{2,1,0:T(8,128)(2,1)S(1)}, u32[]{:S(2)}, u32[]{:S(2)}) collective-permute-start(bf16[64,32,128]{2,1,0:T(8,128)(2,1)S(1)} %get-tuple-element.40.refs_0_), channel_id=1, source_target_pairs={{0,16},{8,24},{16,32},{24,40},{32,48},{40,56},{48,0},{56,8},{64,80... | collective-permute-start | bytes 1572872 | tf_op jit(solution)/shard_map/ppermute | solution.py:360
  70.6 17.3 %collective-permute-start.9 = (bf16[64,32,128]{2,1,0:T(8,128)(2,1)S(1)}, bf16[64,32,128]{2,1,0:T(8,128)(2,1)S(1)}, u32[]{:S(2)}, u32[]{:S(2)}) collective-permute-start(bf16[64,32,128]{2,1,0:T(8,128)(2,1)S(1)} %get-tuple-element.40.refs_0_), channel_id=1, source_target_pairs={{0,48},{8,56},{16,0},{24,8},{32,16},{40,24},{48,32},{56,40},{64,11... | collective-permute-start | bytes 1572872 | tf_op jit(solution)/shard_map/ppermute | solution.py:361
  73.9 28.0 %all-to-all-start.1 = ((bf16[64,32,128]{2,1,0:T(8,128)(2,1)}), bf16[64,32,128]{2,1,0:T(8,128)(2,1)}, u32[]{:S(2)}, u32[]{:S(2)}) async-start(bf16[64,32,128]{2,1,0:T(8,128)(2,1)} %get-tuple-element.36), calls=%async_computation.1 | async-start | bytes 1048576 | tf_op jit(solution)/shard_map/all_to_all | solution.py:364
  90.4 7.8 %collective-permute-start.10 = (f32[512,256]{1,0:T(8,128)S(1)}, f32[512,256]{1,0:T(8,128)S(1)}, u32[]{:S(2)}, u32[]{:S(2)}) collective-permute-start(f32[512,256]{1,0:T(8,128)S(1)} %shard_map.128), channel_id=1, source_target_pairs={{0,8},{8,0},{16,24},{24,16},{32,40},{40,32},{48,56},{56,48},{64,72... | collective-permute-start | bytes 1572872 | tf_op jit(solution)/shard_map/ppermute | solution.py:347
